TPU v7x, 128 devices: a whole 4x4x4 slice. The times are simulated.
128 devices in a mesh: dp: 32 (over y, x, z_hi), tensor: 4 (over z_lo, core).
Axes of the slice: x: 4, y: 4, z: 4 (z_hi: 2, z_lo: 2; z = z_hi * 2 + z_lo), core: 2. Of those that a mesh axis runs over, the one named last changes fastest.
Arguments:
- tokens: bfloat16 [16384, 1024], P('dp'), may hold values from -6 to 6
- norm1_gain: float32 [1024], replicated, may hold values from 0.5 to 1.5
- w_query: bfloat16 [1024, 1024], P(None, 'tensor'), may hold values from -0.1875 to 0.1875
- w_key: bfloat16 [1024, 512], P(None, 'tensor'), may hold values from -0.1875 to 0.1875
- w_value: bfloat16 [1024, 512], P(None, 'tensor'), may hold values from -0.1875 to 0.1875
- w_out: bfloat16 [1024, 1024], P('tensor'), may hold values from -0.75 to 0.75
- norm2_gain: float32 [1024], replicated, may hold values from 0.5 to 1.5
- expert_gate: bfloat16 [8, 1024, 512], P(None, None, 'tensor'), may hold values from -0.1875 to 0.1875
- expert_up: bfloat16 [8, 1024, 512], P(None, None, 'tensor'), may hold values from -0.1875 to 0.1875
- expert_down: bfloat16 [8, 512, 1024], P(None, 'tensor'), may hold values from -1 to 1
- routes: int32 [16384, 4], P('dp'), may hold values from 0 to 7, all different within a row
- gate_weights: float32 [16384, 4], P('dp'), may hold values from 0.1 to 0.5
- segments: int32 [32, 512], P('dp'), may hold values from 0 to 3, never falling along the last dimension, each value on 1 to 320 neighbouring positions
- cotangent: bfloat16 [16384, 1024], P('dp'), may hold values from -6 to 6
Outputs:
- output: bfloat16 [16384, 1024], P('dp')
- input_grad: float32 [16384, 1024], P('dp')
- norm1_gain_grad: float32 [1024], replicated
- w_query_grad: float32 [1024, 1024], P(None, 'tensor')
- w_key_grad: float32 [1024, 512], P(None, 'tensor')
- w_value_grad: float32 [1024, 512], P(None, 'tensor')
- w_out_grad: float32 [1024, 1024], P('tensor')
- norm2_gain_grad: float32 [1024], replicated
- expert_gate_grad: float32 [8, 1024, 512], P(None, None, 'tensor')
- expert_up_grad: float32 [8, 1024, 512], P(None, None, 'tensor')
- expert_down_grad: float32 [8, 512, 1024], P(None, 'tensor')
Inputs may be any that keep to these rules, and one draw needn't show every extreme that they name: `routes`: each row names 4 different experts. `segments`: document numbers never fall along a sequence; each document has at most 320 tokens and one has exactly that many.
All inputs are finite; a program needn't handle non-finite values.
Results may differ from a plain program's by a relative error of at most 0.015.
Values sent between devices are 32-bit elements; how exact they have to be, the bound alone decides.
A program may use at most 128 MiB of HBM per device.

v0:
```python
import jax
import jax.numpy as jnp
from jax import lax
from jax.sharding import PartitionSpec as P

HD = 64


NORM_EPS = 1e-06
ROPE_THETA = 10000.0


def normalize(values, gain_vec):
    inverse = lax.rsqrt(jnp.mean(values * values, -1, keepdims=True) + NORM_EPS)
    scaled = values * inverse
    return (scaled * gain_vec, scaled, inverse)


def norm_back(gradient, scaled, inverse, gain_vec):
    scaled_grad = gradient * gain_vec
    inner_sum = jnp.mean(scaled_grad * scaled, -1, keepdims=True)
    return (inverse * (scaled_grad - scaled * inner_sum), jnp.sum(gradient * scaled, 0))


def tables(seq_count, seq_length, head_width):
    half_width = head_width // 2
    frequency = ROPE_THETA ** (-jnp.arange(half_width, dtype=jnp.float32) * 2.0 / head_width)
    position = jnp.tile(jnp.arange(seq_length), seq_count).astype(jnp.float32)
    angles = position[:, None] * frequency[None, :]
    return (jnp.cos(angles)[:, None, :], jnp.sin(angles)[:, None, :])


def rotate(values, cos_table, sin_table):
    half_width = values.shape[-1] // 2
    first_half = values[..., :half_width]
    second_half = values[..., half_width:]
    return jnp.concatenate(
        [
            first_half * cos_table - second_half * sin_table,
            second_half * cos_table + first_half * sin_table,
        ],
        -1,
    )


def unrotate(gradient, cos_table, sin_table):
    half_width = gradient.shape[-1] // 2
    first_half = gradient[..., :half_width]
    second_half = gradient[..., half_width:]
    return jnp.concatenate(
        [
            first_half * cos_table + second_half * sin_table,
            second_half * cos_table - first_half * sin_table,
        ],
        -1,
    )


def scores_of(query_blocks, key_blocks, segments):
    raw_scores = jnp.einsum(
        "bqngd,bknd->bngqk", query_blocks, key_blocks, preferred_element_type=jnp.float32
    ) * HD ** (-0.5)
    position = jnp.arange(segments.shape[1])
    allowed = (segments[:, :, None] == segments[:, None, :]) & (
        position[:, None] >= position[None, :]
    )
    return jnp.where(allowed[:, None, None, :, :], raw_scores, -1e30)


def left_product(first_op, second_op):
    return lax.dot_general(
        first_op, second_op, (((0,), (0,)), ((), ())), preferred_element_type=jnp.float32
    )


def right_product(first_op, second_op):
    return lax.dot_general(
        first_op, second_op, (((1,), (1,)), ((), ())), preferred_element_type=jnp.float32
    )


def local(
    tokens,
    norm1_gain,
    w_query,
    w_key,
    w_value,
    w_out,
    norm2_gain,
    expert_gate,
    expert_up,
    expert_down,
    routes,
    gate_weights,
    segments,
    cotangent,
):
    seq_count, seq_length = segments.shape
    tok_rows = tokens.shape[0]
    head_count = w_query.shape[1] // HD
    groups = w_key.shape[1] // HD
    group_size = head_count // groups
    experts = expert_gate.shape[0]
    cos_table, sin_table = tables(seq_count, seq_length, HD)
    inputs = tokens.astype(jnp.float32)
    normed1, scaled1, inverse1 = normalize(inputs, norm1_gain)
    hidden1 = normed1.astype(jnp.bfloat16)
    queries = rotate(
        jnp.dot(hidden1, w_query, preferred_element_type=jnp.float32).reshape(
            tok_rows, head_count, HD
        ),
        cos_table,
        sin_table,
    ).astype(jnp.bfloat16)
    keys = rotate(
        jnp.dot(hidden1, w_key, preferred_element_type=jnp.float32).reshape(tok_rows, groups, HD),
        cos_table,
        sin_table,
    ).astype(jnp.bfloat16)
    values = jnp.dot(hidden1, w_value, preferred_element_type=jnp.float32).astype(jnp.bfloat16)
    query_blocks = queries.reshape(seq_count, seq_length, groups, group_size, HD)
    key_blocks = keys.reshape(seq_count, seq_length, groups, HD)
    value_blocks = values.reshape(seq_count, seq_length, groups, HD)
    scores = scores_of(query_blocks, key_blocks, segments)
    row_max = jnp.max(scores, -1, keepdims=True)
    weights = jnp.exp(scores - row_max)
    row_total = jnp.sum(weights, -1, keepdims=True)
    probabilities = weights / row_total
    log_total = row_max + jnp.log(row_total)
    mixed_heads = jnp.einsum(
        "bngqk,bknd->bqngd",
        probabilities.astype(jnp.bfloat16),
        value_blocks,
        preferred_element_type=jnp.float32,
    )
    mixed_heads = mixed_heads.reshape(tok_rows, head_count * HD).astype(jnp.bfloat16)
    attention = lax.psum(jnp.dot(mixed_heads, w_out, preferred_element_type=jnp.float32), "tensor")
    residual = inputs + attention
    normed2, scaled2, inverse2 = normalize(residual, norm2_gain)
    hidden2 = normed2.astype(jnp.bfloat16)
    picked = (routes[:, :, None] == jnp.arange(experts)[None, None, :]).astype(jnp.float32)
    expert_share = jnp.sum(gate_weights[:, :, None] * picked, 1).T[:, :, None]
    gate_pre = jnp.einsum("td,edf->etf", hidden2, expert_gate, preferred_element_type=jnp.float32)
    up_pre = jnp.einsum("td,edf->etf", hidden2, expert_up, preferred_element_type=jnp.float32)
    sigmoid_gate = jax.nn.sigmoid(gate_pre)
    silu_gate = gate_pre * sigmoid_gate
    activated = (silu_gate * up_pre * expert_share).astype(jnp.bfloat16)
    expert_total = lax.psum(
        jnp.einsum("etf,efd->td", activated, expert_down, preferred_element_type=jnp.float32),
        "tensor",
    )
    output = (residual + expert_total).astype(jnp.bfloat16)
    grad_out = cotangent.astype(jnp.float32)
    grad_act = jnp.einsum("td,efd->etf", cotangent, expert_down, preferred_element_type=jnp.float32)
    grad_gate = (
        grad_act * expert_share * up_pre * (sigmoid_gate * (1.0 + gate_pre * (1.0 - sigmoid_gate)))
    ).astype(jnp.bfloat16)
    grad_up = (grad_act * expert_share * silu_gate).astype(jnp.bfloat16)
    gate_grad = jnp.einsum("td,etf->edf", hidden2, grad_gate, preferred_element_type=jnp.float32)
    up_grad = jnp.einsum("td,etf->edf", hidden2, grad_up, preferred_element_type=jnp.float32)
    down_grad = jnp.einsum("etf,td->efd", activated, cotangent, preferred_element_type=jnp.float32)
    grad_hidden2 = lax.psum(
        jnp.einsum("etf,edf->td", grad_gate, expert_gate, preferred_element_type=jnp.float32)
        + jnp.einsum("etf,edf->td", grad_up, expert_up, preferred_element_type=jnp.float32),
        "tensor",
    )
    back_two, gain2_grad = norm_back(grad_hidden2, scaled2, inverse2, norm2_gain)
    grad_residual = grad_out + back_two
    grad_branch = grad_residual.astype(jnp.bfloat16)
    out_w_grad = left_product(mixed_heads, grad_branch)
    grad_mixed = right_product(grad_branch, w_out).astype(jnp.bfloat16)
    grad_mixed = grad_mixed.reshape(seq_count, seq_length, groups, group_size, HD)
    scores = scores_of(query_blocks, key_blocks, segments)
    probabilities = jnp.exp(scores - log_total)
    grad_probs = jnp.einsum(
        "bqngd,bknd->bngqk", grad_mixed, value_blocks, preferred_element_type=jnp.float32
    )
    value_grad = jnp.einsum(
        "bngqk,bqngd->bknd",
        probabilities.astype(jnp.bfloat16),
        grad_mixed,
        preferred_element_type=jnp.float32,
    )
    value_grad = value_grad.reshape(tok_rows, groups * HD).astype(jnp.bfloat16)
    inner_sum = jnp.sum(probabilities * grad_probs, -1, keepdims=True)
    grad_scores = (probabilities * (grad_probs - inner_sum)).astype(jnp.bfloat16)
    query_grad = jnp.einsum(
        "bngqk,bknd->bqngd", grad_scores, key_blocks, preferred_element_type=jnp.float32
    ) * HD ** (-0.5)
    query_grad = unrotate(query_grad.reshape(tok_rows, head_count, HD), cos_table, sin_table)
    query_grad = query_grad.reshape(tok_rows, head_count * HD).astype(jnp.bfloat16)
    key_grad = jnp.einsum(
        "bngqk,bqngd->bknd", grad_scores, query_blocks, preferred_element_type=jnp.float32
    ) * HD ** (-0.5)
    key_grad = unrotate(key_grad.reshape(tok_rows, groups, HD), cos_table, sin_table)
    key_grad = key_grad.reshape(tok_rows, groups * HD).astype(jnp.bfloat16)
    query_w_grad = left_product(hidden1, query_grad)
    key_w_grad = left_product(hidden1, key_grad)
    value_w_grad = left_product(hidden1, value_grad)
    grad_hidden1 = lax.psum(
        right_product(query_grad, w_query)
        + right_product(key_grad, w_key)
        + right_product(value_grad, w_value),
        "tensor",
    )
    back_one, gain1_grad = norm_back(grad_hidden1, scaled1, inverse1, norm1_gain)
    input_grad = grad_residual + back_one
    summed = lax.psum(
        (query_w_grad, key_w_grad, value_w_grad, out_w_grad, gain1_grad, gain2_grad), "dp"
    )
    scattered = (
        lax.psum_scatter(gate_grad, "dp", scatter_dimension=1, tiled=True),
        lax.psum_scatter(up_grad, "dp", scatter_dimension=1, tiled=True),
        lax.psum_scatter(down_grad, "dp", scatter_dimension=2, tiled=True),
    )
    expert_grads = (
        lax.all_gather(scattered[0], "dp", axis=1, tiled=True),
        lax.all_gather(scattered[1], "dp", axis=1, tiled=True),
        lax.all_gather(scattered[2], "dp", axis=2, tiled=True),
    )
    return (
        output,
        input_grad,
        summed[4],
        summed[0],
        summed[1],
        summed[2],
        summed[3],
        summed[5],
        expert_grads[0],
        expert_grads[1],
        expert_grads[2],
    )


def solution(mesh):
    return jax.shard_map(
        local,
        mesh=mesh,
        in_specs=(
            P("dp", None),
            P(),
            P(None, "tensor"),
            P(None, "tensor"),
            P(None, "tensor"),
            P("tensor", None),
            P(),
            P(None, None, "tensor"),
            P(None, None, "tensor"),
            P(None, "tensor", None),
            P("dp", None),
            P("dp", None),
            P("dp", None),
            P("dp", None),
        ),
        out_specs=(
            P("dp", None),
            P("dp", None),
            P(),
            P(None, "tensor"),
            P(None, "tensor"),
            P(None, "tensor"),
            P("tensor", None),
            P(),
            P(None, None, "tensor"),
            P(None, None, "tensor"),
            P(None, "tensor", None),
        ),
        check_vma=False,
    )
```

profile of v0, /device:TPU:0, one launch (start us, length us, event | category | flops | bytes accessed | tf_op | source)
XLA Modules:
  0.0 1449.8 jit_solution(13171993959732221351)
XLA Ops:
  7.3 1.7 fusion.15
  9.0 2.0 fusion.62
  11.0 0.6 fusion.64
  11.6 0.3 multiply_cosine_fusion
  12.3 0.6 convolution_convert_fusion.1
  12.9 0.9 fusion.67
  13.9 0.6 fusion.3
  14.5 1.4 copy-done.2
  15.9 0.8 fusion.33
  16.7 0.7 copy-done.17
  17.4 1.8 fusion.68
  19.3 0.6 select_reduce_fusion
  19.9 59.4 %all-reduce.8.cloned.1.call-done = f32[512,1024]{1,0:T(8,128)} async-done(((f32[512,1024]{1,0:T(8,128)}), f32[512,1024]{1,0:T(8,128)}) %all-reduce.8.cloned.1.call-update) | async-done | bytes 2097168 | tf_op jit(solution)/shard_map/psum | solution.py:137
  79.4 1.9 multiply_reduce_fusion.2
  81.6 2.1 copy-done.45
  83.7 1.3 fusion.69
  84.9 0.7 copy-done.46
  85.6 1.3 fusion.70
  86.9 3.4 fusion.22
  90.4 1.3 fusion.71
  91.7 2.6 bitcast_add_fusion
  94.4 4.8 convolution_bitcast_fusion.1
  99.2 5.4 copy.59
  104.8 4.8 convolution_bitcast_fusion
  109.6 5.4 copy.61
  115.2 4.9 fusion.45
  120.1 0.7 log_add_fusion
  120.8 3.8 convolution_bitcast_fusion.2
  124.6 28.3 %all-reduce.10.cloned.1.call-done = f32[512,1024]{1,0:T(8,128)} async-done(((f32[512,1024]{1,0:T(8,128)}), f32[512,1024]{1,0:T(8,128)}) %all-reduce.10.cloned.1.call-update) | async-done | bytes 2097168 | tf_op jit(solution)/shard_map/psum | solution.py:162
  153.0 3.6 multiply_reduce_fusion
  156.6 2.0 multiply_add_fusion
  158.6 0.5 convolution_convert_fusion
  159.2 0.5 copy-done.32
  159.7 0.9 fusion
  160.7 1.2 fusion.19
  161.9 0.7 fusion.40
  162.8 0.5 convolution_multiply_fusion
  163.4 0.3 copy-done.24
  163.8 0.5 fusion.72
  164.2 0.8 fusion.41
  165.2 0.5 fusion.73
  165.6 0.5 copy-done.19
  166.1 1.8 add_add_fusion
  168.0 181.6 %reduce-scatter.4.cloned.1.call-done = f32[8,32,128]{2,0,1:T(8,128)} async-done(((f32[8,1024,128]{2,0,1:T(8,128)}), f32[8,32,128]{2,0,1:T(8,128)}) %reduce-scatter.4.cloned.1.call-update) | async-done | bytes 131088 | tf_op jit(solution)/shard_map/reduce_scatter | solution.py:212
  349.7 190.2 %reduce-scatter.6.cloned.1.call-done = f32[8,32,128]{2,0,1:T(8,128)} async-done(((f32[8,1024,128]{2,0,1:T(8,128)}), f32[8,32,128]{2,0,1:T(8,128)}) %reduce-scatter.6.cloned.1.call-update) | async-done | bytes 131088 | tf_op jit(solution)/shard_map/reduce_scatter | solution.py:213
  539.9 190.9 %reduce-scatter.8.cloned.1.call-done = f32[8,128,32]{1,2,0:T(8,128)} async-done(((f32[8,128,1024]{1,2,0:T(8,128)}), f32[8,128,32]{1,2,0:T(8,128)}) %reduce-scatter.8.cloned.1.call-update) | async-done | bytes 131088 | tf_op jit(solution)/shard_map/reduce_scatter | solution.py:214
  731.2 2.3 fusion.58
  733.5 1.4 fusion.56
  734.9 1.6 fusion.60
  736.5 1.4 fusion.50
  737.9 82.6 %all-reduce.14.cloned.1.call-done = (f32[512,1024]{1,0:T(8,128)}, f32[512,1024]{1,0:T(8,128)}) async-done(((f32[512,1024]{1,0:T(8,128)}, f32[512,1024]{1,0:T(8,128)}), (f32[512,1024]{1,0:T(8,128)}, f32[512,1024]{1,0:T(8,128)})) %all-reduce.14.cloned.1.call-update) | async-done | bytes 4194320 | tf_op jit(solution)/shard_map/psum | solution.py:148
  820.5 2.3 fusion.14
  822.8 98.1 %all-reduce = (f32[1024]{0:T(1024)}, f32[1024]{0:T(1024)}) all-reduce(f32[1024]{0:T(1024)S(1)} %get-tuple-element.46, f32[1024]{0:T(1024)S(1)} %copy-done.40), channel_id=1, replica_groups=mesh['dp'=32,'tensor'=4] {'dp'}, use_global_device_ids=true, to_apply=%region_13.14 | all-reduce | flops 2048 | bytes 16384 | tf_op jit(solution)/shard_map/psum | solution.py:208
  920.8 5.1 fusion.13
  925.9 5.0 copy.63
  930.9 61.0 %all-gather.6.cloned.1.call-done = f32[8,1024,128]{2,0,1:T(8,128)} async-done(((f32[8,32,128]{2,0,1:T(8,128)}), f32[8,1024,128]{2,0,1:T(8,128)}) %all-gather.6.cloned.1.call-update) | async-done | bytes 4194320 | tf_op jit(solution)/shard_map/all_gather | solution.py:218
  991.9 5.0 copy.64
  996.9 79.1 %all-gather.8.cloned.1.call-done = f32[8,128,1024]{1,2,0:T(8,128)} async-done(((f32[8,128,32]{1,2,0:T(8,128)}), f32[8,128,1024]{1,2,0:T(8,128)}) %all-gather.8.cloned.1.call-update) | async-done | bytes 4194320 | tf_op jit(solution)/shard_map/all_gather | solution.py:219
  1076.0 5.3 copy.65
  1081.3 356.7 %all-reduce.12.cloned.1.call-done = (f32[1024,256]{1,0:T(8,128)}, f32[1024,128]{1,0:T(8,128)}, f32[1024,128]{1,0:T(8,128)}, f32[256,1024]{1,0:T(8,128)}) async-done(((f32[1024,256]{1,0:T(8,128)}, f32[1024,128]{1,0:T(8,128)}, f32[1024,128]{1,0:T(8,128)}, f32[256,1024]{1,0:T(8,128)}), (f32[1024,256]{1,0:T(8,128)}, f32[1024,128]{1,0:T(8,128)}, f32[1024,128]{1,0:T(8,128)}, ...) | async-done | bytes 3145744 | tf_op jit(solution)/shard_map/psum | solution.py:208
  1438.0 2.4 copy.87
  1440.4 0.8 copy.88
  1441.2 0.8 copy.89
  1442.0 1.0 copy.90
  (122 shorter events, 2.3 us)
Async XLA Ops:
  7.2 79.7 %copy-start = (bf16[8,128,1024]{2,1,0:T(8,128)(2,1)S(1)}, bf16[8,128,1024]{2,1,0:T(8,128)(2,1)}, u32[]{:S(2)}) copy-start(bf16[8,128,1024]{2,1,0:T(8,128)(2,1)} %param.23) | copy-start | bytes 6291460
  7.2 3.8 copy-start.8
  7.2 3.8 copy-start.38
  7.2 3.8 copy-start.23
  7.2 72.1 %all-reduce.8.cloned.1.call-start = ((), (), s32[]{:S(2)}) async-start(), calls=%async_computation.3 | async-start | bytes 4194304 | tf_op jit(solution)/shard_map/psum | solution.py:137
  9.0 3.3 copy-start.36
  11.0 1.1 copy-start.42
  11.0 1.3 copy-start.25
  12.1 1.8 copy-start.27
  12.1 1.8 copy-start.29
  12.9 1.6 copy-start.31
  13.8 2.0 copy-start.2
  13.8 2.0 copy-start.34
  14.4 2.2 copy-start.35
  15.9 1.6 copy-start.12
  16.7 0.7 copy-start.17
  17.4 1.9 copy-start.43
  17.4 1.9 copy-start.44
  19.2 133.8 %all-reduce.10.cloned.1.call-start = ((), (), s32[]{:S(2)}) async-start(), calls=%async_computation.4 | async-start | bytes 4194304 | tf_op jit(solution)/shard_map/psum | solution.py:162
  19.9 61.4 %copy-start.33 = (f32[1024]{0:T(1024)S(1)}, f32[1024]{0:T(1024)}, u32[]{:S(2)}) copy-start(f32[1024]{0:T(1024)} %param.20) | copy-start | bytes 12292
  81.3 3.6 copy-start.4
  81.3 2.4 copy-start.45
  83.6 1.3 copy-start.9
  83.7 2.0 copy-start.46
  85.6 1.3 copy-start.11
  85.6 1.3 copy-start.41
  90.4 1.3 copy-start.16
  90.4 1.3 copy-start.15
  94.3 255.3 %reduce-scatter.4.cloned.1.call-start = ((), (), s32[]{:S(2)}) async-start(), calls=%async_computation.5 | async-start | bytes 4325376 | tf_op jit(solution)/shard_map/reduce_scatter | solution.py:212
  104.6 435.3 %reduce-scatter.6.cloned.1.call-start = ((), (), s32[]{:S(2)}) async-start(), calls=%async_computation.7 | async-start | bytes 4325376 | tf_op jit(solution)/shard_map/reduce_scatter | solution.py:213
  115.1 615.7 %reduce-scatter.8.cloned.1.call-start = ((), (), s32[]{:S(2)}) async-start(), calls=%async_computation.9 | async-start | bytes 4325376 | tf_op jit(solution)/shard_map/reduce_scatter | solution.py:214
  120.1 700.4 %all-reduce.14.cloned.1.call-start = ((), (), s32[]{:S(2)}) async-start(), calls=%async_computation.12 | async-start | bytes 8388608 | tf_op jit(solution)/shard_map/psum | solution.py:148
  124.6 31.9 %copy-start.5 = (f32[512,1024]{1,0:T(8,128)S(1)}, f32[512,1024]{1,0:T(8,128)}, u32[]{:S(2)}) copy-start(f32[512,1024]{1,0:T(8,128)} %copy-done.4) | copy-start | bytes 6291460
  153.0 3.6 copy-start.10
  156.5 2.0 copy-start.13
  156.5 2.7 copy-start.3
  158.6 2.1 copy-start.6
  158.6 1.2 copy-start.32
  161.9 0.8 copy-start.28
  161.9 0.9 copy-start.30
  162.8 0.7 copy-start.20
  162.8 1.0 copy-start.24
  164.2 1.0 copy-start.26
  165.0 1.1 copy-start.19
  167.9 563.2 %copy-start.37 = (f32[512]{0:T(512)S(1)}, f32[512]{0:T(512)}, u32[]{:S(2)}) copy-start(f32[512]{0:T(512)} %copy-done.36) | copy-start | bytes 6148
  167.9 563.2 %copy-start.39 = (f32[1024]{0:T(1024)S(1)}, f32[1024]{0:T(1024)}, u32[]{:S(2)}) copy-start(f32[1024]{0:T(1024)} %param.15) | copy-start | bytes 12292
  167.9 757.9 %all-gather.4.cloned.1.call-start = ((), (), s32[]{:S(2)}) async-start(), calls=%async_computation.6 | async-start | bytes 4325376 | tf_op jit(solution)/shard_map/all_gather | solution.py:217
  349.6 642.2 %all-gather.6.cloned.1.call-start = ((), (), s32[]{:S(2)}) async-start(), calls=%async_computation.8 | async-start | bytes 4325376 | tf_op jit(solution)/shard_map/all_gather | solution.py:218
  539.9 536.1 %all-gather.8.cloned.1.call-start = ((), (), s32[]{:S(2)}) async-start(), calls=%async_computation.10 | async-start | bytes 4325376 | tf_op jit(solution)/shard_map/all_gather | solution.py:219
  730.9 707.1 %all-reduce.12.cloned.1.call-start = ((), (), s32[]{:S(2)}) async-start(), calls=%async_computation.11 | async-start | bytes 6291456 | tf_op jit(solution)/shard_map/psum | solution.py:208
  733.5 3.0 copy-start.7
  733.5 3.0 copy-start.18
  737.9 84.8 %copy-start.40 = (f32[1024]{0:T(1024)S(1)}, f32[1024]{0:T(1024)}, u32[]{:S(2)}) copy-start(f32[1024]{0:T(1024)} %get-tuple-element.44) | copy-start | bytes 12292
  1438.0 2.4 copy-start.22
  1438.0 3.2 copy-start.21
  1438.0 4.0 copy-start.14
  1438.0 5.0 copy-start.1
Sparse Core Ops, SparseCore 0:
  19.3 59.9 all-reduce.7
  94.4 58.4 all-reduce.9
  155.9 193.6 reduce-scatter.3
  351.9 187.9 reduce-scatter.5
  542.7 188.1 reduce-scatter.7
  733.8 86.6 all-reduce.13
  823.9 84.9 all-gather.3
  912.3 79.5 all-gather.5
  995.5 80.4 all-gather.7
  1079.4 358.5 all-reduce.11
where the time goes:
time: 1450 us
  waiting for transfers between devices  1230 us (85%)
  blocking collectives  98.1 us (7%)
  matrix products  47.7 us (3%)
  local copies, waits for them, and re-layouts  37.9 us (3%)
  other arithmetic  20.6 us (1%)
  between operations  14.8 us (1%)
    psum x1, waiting for transfers between devices, local(): lax.psum((query_w_grad, key_w_grad, value_w_grad, out_w_grad, gain1_grad,...  357 us
    reduce_scatter x1, waiting for transfers between devices, local(): lax.psum_scatter(down_grad, 'dp', scatter_dimension=2, tiled=True)  191 us
    reduce_scatter x1, waiting for transfers between devices, local(): lax.psum_scatter(up_grad, 'dp', scatter_dimension=1, tiled=True)  190 us
    reduce_scatter x1, waiting for transfers between devices, local(): lax.psum_scatter(gate_grad, 'dp', scatter_dimension=1, tiled=True)  182 us
    psum x1, blocking collectives, local(): lax.psum((query_w_grad, key_w_grad, value_w_grad, out_w_grad, gain1_grad,...  98.1 us
    psum x1, waiting for transfers between devices, local(): lax.psum(jnp.einsum('etf,efd->td', activated, expert_down, preferred_elem...  82.6 us
    all_gather x1, waiting for transfers between devices, local(): lax.all_gather(scattered[2], 'dp', axis=2, tiled=True)  79.1 us
    all_gather x1, waiting for transfers between devices, local(): lax.all_gather(scattered[1], 'dp', axis=1, tiled=True)  61 us
  transfers between devices with their start and end apart: 10, of which 9 were waited for; matrix products, arithmetic and copies ran while one was open for 5% of the time, Pallas kernels for 0%

commit v1 on v0

--- a/solution.py
+++ b/solution.py
@@ -1,7 +1,205 @@
+import functools
+
 import jax
 import jax.numpy as jnp
 from jax import lax
+from jax.experimental import pallas as pl
+from jax.experimental.pallas import tpu as pltpu
 from jax.sharding import PartitionSpec as P
+
+MESH = pl.DeviceIdType.MESH
+
+
+def ring_pos(dp):
+    xy = dp // 2
+    x, y = xy % 4, xy // 4
+    turn = (x + y) % 4
+    return 4 * y + turn, 4 * x + turn
+
+
+def ring_dp(kind, pos, zhi):
+    a = pos // 4
+    b = (pos % 4 - a + 4) % 4
+    x, y = (b, a) if kind == 0 else (a, b)
+    return (y * 4 + x) * 2 + zhi
+
+
+FLOWS = ((0, 1), (0, -1), (1, 1), (1, -1))
+
+
+def dp_kernel(sub, g, out, land, zland, total, rs_s, rs_r, ag_s, ag_r, z_s, z_r, loc):
+    dp = lax.axis_index("dp")
+    tn = lax.axis_index("tensor")
+    zhi = dp % 2
+    zpeer = dp + 1 - 2 * zhi
+    pos = ring_pos(dp)
+    barrier = pltpu.get_barrier_semaphore()
+    peers = []
+    for kind in (0, 1):
+        for d in (1, -1):
+            peers.append(ring_dp(kind, (pos[kind] + d + 16) % 16, zhi))
+    for q in peers + [zpeer]:
+        pl.semaphore_signal(barrier, inc=1, device_id=(q, tn), device_id_type=MESH)
+    pl.semaphore_wait(barrier, 5)
+
+    def rs(u, f, s, src):
+        kind, d = FLOWS[f]
+        c = (pos[kind] - d * (1 + s) + 32) % 16
+        return pltpu.make_async_remote_copy(
+            src.at[u, f, c], land.at[u, f, c], rs_s.at[u, f, s], rs_r.at[u, f, s],
+            device_id=(peers[f], tn), device_id_type=MESH)
+
+    def ag(u, f, s, src):
+        kind, d = FLOWS[f]
+        c = (pos[kind] - d * s + 32) % 16
+        return pltpu.make_async_remote_copy(
+            src, out.at[u, f, c], ag_s.at[u, f, s], ag_r.at[u, f, s],
+            device_id=(peers[f], tn), device_id_type=MESH)
+
+    def rs_add(u, f, s):
+        kind, d = FLOWS[f]
+        c = (pos[kind] - d * (1 + s) + 32) % 16
+        land[u, f, c] = land[u, f, c] + g[u, f, c]
+        return c
+
+    def zcopy(u, f):
+        return pltpu.make_async_remote_copy(
+            land.at[u, f, pos[FLOWS[f][0]]], zland.at[u, f], z_s.at[u, f], z_r.at[u, f],
+            device_id=(zpeer, tn), device_id_type=MESH)
+
+    def keep(u, f):
+        return pltpu.make_async_copy(total.at[u, f], out.at[u, f, pos[FLOWS[f][0]]], loc.at[u, f])
+
+    for u in range(sub):
+        for f in range(4):
+            rs(u, f, 0, g).start()
+
+    def rs_step(s, _):
+        for u in range(sub):
+            for f in range(4):
+                rs(u, f, s - 1, land).wait_recv()
+                rs_add(u, f, s)
+                rs(u, f, s, land).start()
+        return 0
+    lax.fori_loop(1, 15, rs_step, 0)
+    for u in range(sub):
+        for f in range(4):
+            rs(u, f, 14, land).wait_recv()
+            rs_add(u, f, 15)
+            zcopy(u, f).start()
+    for u in range(sub):
+        for f in range(4):
+            zcopy(u, f).wait_recv()
+            total[u, f] = land[u, f, pos[FLOWS[f][0]]] + zland[u, f]
+            ag(u, f, 0, total.at[u, f]).start()
+            keep(u, f).start()
+
+    def ag_step(s, _):
+        for u in range(sub):
+            for f in range(4):
+                kind, d = FLOWS[f]
+                c = (pos[kind] - d * s + 32) % 16
+                ag(u, f, s - 1, out.at[u, f, c]).wait_recv()
+                ag(u, f, s, out.at[u, f, c]).start()
+        return 0
+    lax.fori_loop(1, 15, ag_step, 0)
+    for u in range(sub):
+        for f in range(4):
+            ag(u, f, 14, total.at[u, f]).wait_recv()
+
+    def drain(s, _):
+        for u in range(sub):
+            for f in range(4):
+                rs(u, f, s, land).wait_send()
+                ag(u, f, s, total.at[u, f]).wait_send()
+        return 0
+    lax.fori_loop(0, 15, drain, 0)
+    for u in range(sub):
+        for f in range(4):
+            zcopy(u, f).wait_send()
+            keep(u, f).wait()
+
+
+def dp_sum(g, cid=1):
+    sub, _, _, m, _ = g.shape
+    D = pltpu.SemaphoreType.DMA
+    return pl.pallas_call(
+        functools.partial(dp_kernel, sub),
+        out_shape=jax.ShapeDtypeStruct(g.shape, jnp.float32),
+        in_specs=[pl.BlockSpec(memory_space=pltpu.VMEM)],
+        out_specs=pl.BlockSpec(memory_space=pl.ANY),
+        scratch_shapes=[
+            pltpu.VMEM(g.shape, jnp.float32),
+            pltpu.VMEM((sub, 4, m, 128), jnp.float32),
+            pltpu.VMEM((sub, 4, m, 128), jnp.float32),
+            D((sub, 4, 15)), D((sub, 4, 15)), D((sub, 4, 15)), D((sub, 4, 15)),
+            D((sub, 4)), D((sub, 4)), D((sub, 4)),
+        ],
+        compiler_params=pltpu.CompilerParams(collective_id=cid, has_side_effects=True, vmem_limit_bytes=60 << 20),
+    )(g)
+
+
+def ar4_kernel(K, x, out, buf, land1, land2, s1, r1, s2, r2, s3, r3):
+    dp = lax.axis_index("dp")
+    tn = lax.axis_index("tensor")
+    core = tn % 2
+    buddy = tn + 1 - 2 * core
+    zlo = tn // 2
+    zpeer = tn + 2 - 4 * zlo
+    barrier = pltpu.get_barrier_semaphore()
+    for q in (buddy, zpeer):
+        pl.semaphore_signal(barrier, inc=1, device_id=(dp, q), device_id_type=MESH)
+    pl.semaphore_wait(barrier, 2)
+    half = x.shape[0] // 2
+    n = half // K
+
+    def one(k):
+        return pltpu.make_async_remote_copy(
+            x.at[pl.ds((1 - core) * half + k * n, n)], land1.at[pl.ds(k * n, n)], s1.at[k], r1.at[k],
+            device_id=(dp, buddy), device_id_type=MESH)
+
+    def two(k):
+        return pltpu.make_async_remote_copy(
+            buf.at[pl.ds(k * n, n)], land2.at[pl.ds(k * n, n)], s2.at[k], r2.at[k],
+            device_id=(dp, zpeer), device_id_type=MESH)
+
+    def three(k):
+        rows = pl.ds(core * half + k * n, n)
+        return pltpu.make_async_remote_copy(
+            out.at[rows], out.at[rows], s3.at[k], r3.at[k],
+            device_id=(dp, buddy), device_id_type=MESH)
+
+    for k in range(K):
+        one(k).start()
+    for k in range(K):
+        one(k).wait_recv()
+        buf[pl.ds(k * n, n)] = land1[pl.ds(k * n, n)] + x[pl.ds(core * half + k * n, n)]
+        two(k).start()
+    for k in range(K):
+        two(k).wait_recv()
+        out[pl.ds(core * half + k * n, n)] = buf[pl.ds(k * n, n)] + land2[pl.ds(k * n, n)]
+        three(k).start()
+    for k in range(K):
+        three(k).wait_recv()
+    for k in range(K):
+        one(k).wait_send()
+        two(k).wait_send()
+        three(k).wait_send()
+
+
+def ar4(x, K, cid):
+    D = pltpu.SemaphoreType.DMA
+    h = (x.shape[0] // 2, x.shape[1])
+    return pl.pallas_call(
+        functools.partial(ar4_kernel, K),
+        out_shape=jax.ShapeDtypeStruct(x.shape, jnp.float32),
+        in_specs=[pl.BlockSpec(memory_space=pltpu.VMEM)],
+        out_specs=pl.BlockSpec(memory_space=pltpu.VMEM),
+        scratch_shapes=[pltpu.VMEM(h, jnp.float32), pltpu.VMEM(h, jnp.float32), pltpu.VMEM(h, jnp.float32),
+            D((K,)), D((K,)), D((K,)), D((K,)), D((K,)), D((K,))],
+        compiler_params=pltpu.CompilerParams(collective_id=cid, has_side_effects=True, vmem_limit_bytes=60 << 20),
+    )(x)
+
 
 HD = 64
 
@@ -134,7 +332,7 @@
         preferred_element_type=jnp.float32,
     )
     mixed_heads = mixed_heads.reshape(tok_rows, head_count * HD).astype(jnp.bfloat16)
-    attention = lax.psum(jnp.dot(mixed_heads, w_out, preferred_element_type=jnp.float32), "tensor")
+    attention = ar4(jnp.dot(mixed_heads, w_out, preferred_element_type=jnp.float32), 4, 2)
     residual = inputs + attention
     normed2, scaled2, inverse2 = normalize(residual, norm2_gain)
     hidden2 = normed2.astype(jnp.bfloat16)
@@ -145,9 +343,10 @@
     sigmoid_gate = jax.nn.sigmoid(gate_pre)
     silu_gate = gate_pre * sigmoid_gate
     activated = (silu_gate * up_pre * expert_share).astype(jnp.bfloat16)
-    expert_total = lax.psum(
+    expert_total = ar4(
         jnp.einsum("etf,efd->td", activated, expert_down, preferred_element_type=jnp.float32),
-        "tensor",
+        4,
+        3,
     )
     output = (residual + expert_total).astype(jnp.bfloat16)
     grad_out = cotangent.astype(jnp.float32)
@@ -159,10 +358,11 @@
     gate_grad = jnp.einsum("td,etf->edf", hidden2, grad_gate, preferred_element_type=jnp.float32)
     up_grad = jnp.einsum("td,etf->edf", hidden2, grad_up, preferred_element_type=jnp.float32)
     down_grad = jnp.einsum("etf,td->efd", activated, cotangent, preferred_element_type=jnp.float32)
-    grad_hidden2 = lax.psum(
+    grad_hidden2 = ar4(
         jnp.einsum("etf,edf->td", grad_gate, expert_gate, preferred_element_type=jnp.float32)
         + jnp.einsum("etf,edf->td", grad_up, expert_up, preferred_element_type=jnp.float32),
-        "tensor",
+        4,
+        4,
     )
     back_two, gain2_grad = norm_back(grad_hidden2, scaled2, inverse2, norm2_gain)
     grad_residual = grad_out + back_two
@@ -197,39 +397,33 @@
     query_w_grad = left_product(hidden1, query_grad)
     key_w_grad = left_product(hidden1, key_grad)
     value_w_grad = left_product(hidden1, value_grad)
-    grad_hidden1 = lax.psum(
+    grad_hidden1 = ar4(
         right_product(query_grad, w_query)
         + right_product(key_grad, w_key)
         + right_product(value_grad, w_value),
-        "tensor",
+        4,
+        5,
     )
     back_one, gain1_grad = norm_back(grad_hidden1, scaled1, inverse1, norm1_gain)
     input_grad = grad_residual + back_one
-    summed = lax.psum(
-        (query_w_grad, key_w_grad, value_w_grad, out_w_grad, gain1_grad, gain2_grad), "dp"
-    )
-    scattered = (
-        lax.psum_scatter(gate_grad, "dp", scatter_dimension=1, tiled=True),
-        lax.psum_scatter(up_grad, "dp", scatter_dimension=1, tiled=True),
-        lax.psum_scatter(down_grad, "dp", scatter_dimension=2, tiled=True),
-    )
-    expert_grads = (
-        lax.all_gather(scattered[0], "dp", axis=1, tiled=True),
-        lax.all_gather(scattered[1], "dp", axis=1, tiled=True),
-        lax.all_gather(scattered[2], "dp", axis=2, tiled=True),
-    )
+    parts = (
+        gate_grad, up_grad, down_grad, query_w_grad, key_w_grad, value_w_grad, out_w_grad,
+        gain1_grad, gain2_grad,
+    )
+    rows = [part.size // 128 for part in parts]
+    short = -sum(rows) % 1024
+    packed = jnp.concatenate(
+        [part.reshape(-1, 128) for part in parts] + [jnp.zeros((short, 128), jnp.float32)]
+    )
+    summed = dp_sum(packed.reshape(2, 4, 16, -1, 128)).reshape(-1, 128)
+    done = []
+    at = 0
+    for part, count in zip(parts, rows):
+        done.append(summed[at : at + count].reshape(part.shape))
+        at += count
     return (
-        output,
-        input_grad,
-        summed[4],
-        summed[0],
-        summed[1],
-        summed[2],
-        summed[3],
-        summed[5],
-        expert_grads[0],
-        expert_grads[1],
-        expert_grads[2],
+        output, input_grad, done[7], done[3], done[4], done[5], done[6], done[8],
+        done[0], done[1], done[2],
     )
 
 

time: 1450 us -> 456 us (0.31)
  waiting for transfers between devices: 1230 us -> 0 us
  Pallas kernels: 0 us -> 328 us
  blocking collectives: 98.1 us -> 0 us
  local copies, waits for them, and re-layouts: 37.9 us -> 65.5 us
    reduce_scatter x3 -> x0, waiting for transfers between devices: 563 us -> none  [the longest x1 191 us: local(): lax.psum_scatter(down_grad, 'dp', scatter_dimension=2, tiled=True)]
    psum x4 -> x0, waiting for transfers between devices: 527 us -> none  [the longest x1 357 us: local(): lax.psum((query_w_grad, key_w_grad, value_w_grad, out_w_grad, gain1_grad,...]
    pallas_call x0 -> x5, Pallas kernels: none -> 328 us  [the longest x1 202 us: dp_sum(): pl.pallas_call(functools.partial(dp_kernel, sub), out_shape=jax.ShapeDtyp...]
    all_gather x3 -> x0, waiting for transfers between devices: 140 us -> none  [the longest x1 79.1 us: local(): lax.all_gather(scattered[2], 'dp', axis=2, tiled=True)]
    psum x1 -> x0, blocking collectives: 98.1 us -> none  [local(): lax.psum((query_w_grad, key_w_grad, value_w_grad, out_w_grad, gain1_grad,...]
    reshape x0 -> x7, local copies, waits for them, and re-layouts: none -> 16.1 us  [the longest x4 8.71 us: local(): done.append(summed[at:at + count].reshape(part.shape))]
  transfers between devices with their start and end apart: 10 -> 0, of which waited for: 9 -> 0; matrix products, arithmetic and copies ran while one was open for 5% -> 0% of each run, Pallas kernels for 0% -> 0%
where the time goes in v1:
time: 456 us; the launch traced here: 455 us
  Pallas kernels  328 us (72%)
  local copies, waits for them, and re-layouts  65.5 us (14%)
  matrix products  40.2 us (9%)
  other arithmetic  20.4 us (4%)
    pallas_call x1, Pallas kernels, dp_sum(): pl.pallas_call(functools.partial(dp_kernel, sub), out_shape=jax.ShapeDtyp...  202 us
    pallas_call x4, Pallas kernels, ar4(): pl.pallas_call(functools.partial(ar4_kernel, K), out_shape=jax.ShapeDtype...  125 us
    unnamed x93, local copies, waits for them, and re-layouts  24.5 us
    slice x3, local copies, waits for them, and re-layouts, local(): done.append(summed[at:at + count].reshape(part.shape))  13.5 us

profile of v1, /device:TPU:0, one launch (start us, length us, event | category | flops | bytes accessed | tf_op | source)
XLA Modules:
  0.0 455.1 jit_solution(11748668503539343326)
XLA Ops:
  0.7 0.9 select_reduce_fusion
  1.6 1.6 fusion.15
  3.2 1.9 convolution_convert_fusion.1
  5.1 0.6 fusion.60
  6.2 0.6 fusion.62
  7.0 0.9 fusion.68
  8.0 0.6 fusion.3
  8.6 1.4 copy-done.2
  10.0 0.8 fusion.33
  10.8 0.7 copy-done.21
  11.5 1.8 fusion.69.x
  13.3 31.2 %shard_map.221 = f32[512,1024]{1,0:T(8,128)} custom-call(f32[512,1024]{1,0:T(8,128)} %fusion.69.x), custom_call_target="tpu_custom_call" | custom-call | tf_op jit(solution)/shard_map/pallas_call | solution.py:193
  44.6 1.9 multiply_reduce_fusion.2
  46.8 2.1 copy-done.41
  48.9 1.3 fusion.70
  50.2 0.7 copy-done.42
  50.9 1.3 fusion.71
  52.2 3.4 fusion.22
  55.6 1.3 fusion.72
  56.9 2.6 bitcast_add_fusion.x
  59.5 31.3 %shard_map.223 = f32[512,1024]{1,0:T(8,128)} custom-call(f32[512,1024]{1,0:T(8,128)} %bitcast_add_fusion.x), custom_call_target="tpu_custom_call" | custom-call | tf_op jit(solution)/shard_map/pallas_call | solution.py:193
  90.8 2.9 multiply_reduce_fusion
  93.7 2.6 convolution_bitcast_fusion.2.x
  96.3 31.4 %shard_map.222 = f32[512,1024]{1,0:T(8,128)} custom-call(f32[512,1024]{1,0:T(8,128)} %convolution_bitcast_fusion.2.x), custom_call_target="tpu_custom_call" | custom-call | tf_op jit(solution)/shard_map/pallas_call | solution.py:193
  127.8 4.3 multiply_add_fusion
  132.1 0.5 convolution_convert_fusion
  132.6 0.8 fusion.41
  133.7 0.5 fusion.74
  134.3 0.9 fusion
  135.3 1.2 fusion.19
  136.5 0.8 fusion.40
  137.4 0.5 fusion.73
  138.2 0.5 convolution_multiply_fusion
  138.8 0.4 copy-done.24
  139.2 1.8 add_add_fusion.x
  141.0 31.3 %shard_map.224 = f32[512,1024]{1,0:T(8,128)} custom-call(f32[512,1024]{1,0:T(8,128)} %add_add_fusion.x), custom_call_target="tpu_custom_call" | custom-call | tf_op jit(solution)/shard_map/pallas_call | solution.py:193
  172.3 2.4 fusion.14
  174.7 3.6 fusion.13
  178.3 3.5 convolution_bitcast_fusion.1
  181.9 5.3 %copy.53 = f32[8,1024,128]{2,1,0:T(8,128)} copy(f32[8,1024,128]{1,2,0:T(8,128)} %convolution_bitcast_fusion.1) | data formatting | bytes 8388608 | tf_op jit(solution)/shard_map/td,etf->edf/transpose | solution.py:358
  187.2 4.6 %constant_dynamic-update-slice_fusion.6 = f32[31744,128]{1,0:T(8,128)} fusion(f32[8192,128]{1,0:T(8,128)} %bitcast.203), kind=kLoop, calls=%fused_computation.102 | loop fusion | bytes 8388608
  191.8 3.3 convolution_bitcast_fusion
  195.0 5.3 %copy.55 = f32[8,1024,128]{2,1,0:T(8,128)} copy(f32[8,1024,128]{1,2,0:T(8,128)} %convolution_bitcast_fusion) | data formatting | bytes 8388608 | tf_op jit(solution)/shard_map/td,etf->edf/transpose | solution.py:359
  200.4 4.6 %constant_dynamic-update-slice_fusion.5 = f32[31744,128]{1,0:T(8,128)} fusion(f32[31744,128]{1,0:T(8,128)} %constant_dynamic-update-slice_fusion.6, f32[8192,128]{1,0:T(8,128)} %bitcast.202), kind=kLoop, calls=%fused_computation.101 | loop fusion | bytes 8388608
  205.0 3.3 fusion.45
  208.3 4.9 %reshape.344 = f32[8192,128]{1,0:T(8,128)} reshape(f32[8,128,1024]{2,1,0:T(8,128)} %fusion.45) | data formatting | bytes 8388608 | tf_op jit(solution)/shard_map/reshape | solution.py:416
  213.2 4.4 constant_dynamic-update-slice_fusion.4
  217.6 1.6 fusion.58
  219.2 2.3 reshape.345
  221.5 2.3 constant_dynamic-update-slice_fusion.3
  223.8 1.4 convolution_dynamic-update-slice_fusion.1
  225.2 1.4 convolution_dynamic-update-slice_fusion
  227.3 1.1 constant_dynamic-update-slice_fusion.2
  228.3 0.6 constant_dynamic-update-slice_fusion.1
  228.9 0.6 constant_dynamic-update-slice_fusion
  229.5 0.8 broadcast_dynamic-update-slice_fusion
  230.4 202.5 %shard_map.225 = f32[2,4,16,248,128]{4,3,2,1,0:T(8,128)} custom-call(f32[2,4,16,248,128]{4,3,2,1,0:T(8,128)} %bitcast.201), custom_call_target="tpu_custom_call" | custom-call | tf_op jit(solution)/shard_map/pallas_call | solution.py:126
  432.9 1.3 slice_bitcast_fusion
  434.2 1.7 fusion.66
  435.8 1.3 reshape.352
  437.1 2.2 fusion.67
  439.3 1.1 reshape.353
  440.5 9.6 %fusion.65 = (f32[8192,128]{1,0:T(8,128)}, f32[8192,128]{1,0:T(8,128)}, f32[8192,128]{1,0:T(8,128)}) fusion(f32[31744,128]{1,0:T(8,128)} %bitcast.200), kind=kLoop, calls=%fused_computation.118 | loop fusion | bytes 25165824 | tf_op jit(solution)/shard_map/slice | solution.py:422
  450.1 5.0 %reshape.357 = f32[8,128,1024]{2,1,0:T(8,128)} reshape(f32[8192,128]{1,0:T(8,128)} %get-tuple-element.17) | data formatting | bytes 8388608 | tf_op jit(solution)/shard_map/reshape | solution.py:422
  (99 shorter events, 2.7 us)
Async XLA Ops:
  0.6 51.5 %copy-start = (bf16[8,128,1024]{2,1,0:T(8,128)(2,1)S(1)}, bf16[8,128,1024]{2,1,0:T(8,128)(2,1)}, u32[]{:S(2)}) copy-start(bf16[8,128,1024]{2,1,0:T(8,128)(2,1)} %param.23) | copy-start | bytes 6291460
  0.7 4.4 copy-start.8
  0.7 4.4 copy-start.39
  0.7 4.4 copy-start.23
  5.0 3.5 copy-start.36
  5.0 1.1 copy-start.30
  5.7 1.1 copy-start.40
  6.1 1.8 copy-start.25
  6.8 1.1 copy-start.32
  6.8 1.1 copy-start.34
  8.0 2.0 copy-start.2
  10.0 1.6 copy-start.14
  10.8 0.7 copy-start.21
  44.6 2.0 copy-start.38
  46.5 3.6 copy-start.4
  46.5 2.4 copy-start.41
  48.9 1.3 copy-start.9
  48.9 2.0 copy-start.42
  50.9 1.3 copy-start.12
  55.6 1.3 copy-start.19
  55.6 1.3 copy-start.17
  90.8 2.9 copy-start.15
  96.3 31.4 %copy-start.5 = (f32[512,1024]{1,0:T(8,128)S(1)}, f32[512,1024]{1,0:T(8,128)}, u32[]{:S(2)}) copy-start(f32[512,1024]{1,0:T(8,128)} %copy-done.4) | copy-start | bytes 6291460
  127.7 4.8 %copy-start.3 = (f32[1,2,2,512,512]{3,4,2,1,0:T(8,128)S(1)}, f32[1,2,2,512,512]{3,4,2,1,0:T(8,128)}, u32[]{:S(2)}) copy-start(f32[1,2,2,512,512]{3,4,2,1,0:T(8,128)} %copy-done.2) | copy-start | bytes 12582916
  132.1 1.3 copy-start.6
  132.6 1.1 copy-start.29
  133.4 0.9 copy-start.37
  135.3 1.2 copy-start.26
  136.5 1.0 copy-start.31
  137.3 0.9 copy-start.33
  137.3 0.9 copy-start.35
  137.3 1.3 copy-start.27
  138.2 1.0 copy-start.24
  172.3 2.4 copy-start.7
  174.7 3.6 copy-start.10
  174.7 3.6 copy-start.20
  187.2 4.6 %copy-start.11 = (bf16[512,1024,1]{1,0,2:T(8,128)(2,1)S(1)}, bf16[512,1024,1]{1,0,2:T(8,128)(2,1)}, u32[]{:S(2)}) copy-start(bf16[512,1024,1]{1,0,2:T(8,128)(2,1)} %copy-done.9) | copy-start | bytes 3145732
  187.2 4.6 %copy-start.18 = (bf16[8,512,128]{2,1,0:T(8,128)(2,1)S(1)}, bf16[8,512,128]{2,1,0:T(8,128)(2,1)}, u32[]{:S(2)}) copy-start(bf16[8,512,128]{2,1,0:T(8,128)(2,1)} %copy-done.17) | copy-start | bytes 3145732
  200.4 4.6 %copy-start.13 = (bf16[512,1024]{1,0:T(8,128)(2,1)S(1)}, bf16[512,1024]{1,0:T(8,128)(2,1)}, u32[]{:S(2)}) copy-start(bf16[512,1024]{1,0:T(8,128)(2,1)} %param.27) | copy-start | bytes 3145732
  200.4 4.6 %copy-start.16 = (bf16[8,512,128]{2,1,0:T(8,128)(2,1)S(1)}, bf16[8,512,128]{2,1,0:T(8,128)(2,1)}, u32[]{:S(2)}) copy-start(bf16[8,512,128]{2,1,0:T(8,128)(2,1)} %get-tuple-element.28) | copy-start | bytes 3145732
  219.2 4.6 %copy-start.28 = (bf16[512,2,64]{0,2,1:T(8,128)(2,1)S(1)}, bf16[512,2,64]{0,2,1:T(8,128)(2,1)}, u32[]{:S(2)}) copy-start(bf16[512,2,64]{0,2,1:T(8,128)(2,1)} %copy-done.27) | copy-start | bytes 393220
  223.8 2.8 copy-start.22
  450.1 5.0 %copy-start.1 = (bf16[8,128,1024]{2,1,0:T(8,128)(2,1)S(1)}, bf16[8,128,1024]{2,1,0:T(8,128)(2,1)}, u32[]{:S(2)}) copy-start(bf16[8,128,1024]{2,1,0:T(8,128)(2,1)} %param.23) | copy-start | bytes 6291460

commit v2 on v0

v2 whole, which is shorter than its diff:
```python
import functools

import jax
import jax.numpy as jnp
from jax import lax
from jax.experimental import pallas as pl
from jax.experimental.pallas import tpu as pltpu
from jax.sharding import PartitionSpec as P

MESH = pl.DeviceIdType.MESH
DMA = pltpu.SemaphoreType.DMA
F32 = jnp.float32
BF16 = jnp.bfloat16

HD = 64
NORM_EPS = 1e-06
ROPE_THETA = 10000.0
FLOWS = ((0, 1), (0, -1), (1, 1), (1, -1))
PIECES = 4
VMEM = pl.BlockSpec(memory_space=pltpu.VMEM)
ANY = pl.BlockSpec(memory_space=pl.ANY)


def dot_nn(first_op, second_op):
    return jnp.dot(first_op, second_op, preferred_element_type=F32)


def dot_tn(first_op, second_op):
    return lax.dot_general(
        first_op, second_op, (((0,), (0,)), ((), ())), preferred_element_type=F32
    )


def dot_nt(first_op, second_op):
    return lax.dot_general(
        first_op, second_op, (((1,), (1,)), ((), ())), preferred_element_type=F32
    )


def ring_pos(dp):
    xy = dp // 2
    x, y = xy % 4, xy // 4
    turn = (x + y) % 4
    return 4 * y + turn, 4 * x + turn


def ring_dp(kind, pos, zhi):
    along = pos // 4
    across = (pos % 4 - along + 4) % 4
    x, y = (across, along) if kind == 0 else (along, across)
    return (y * 4 + x) * 2 + zhi


class Place:
    def __init__(self):
        self.dp = lax.axis_index("dp")
        self.tensor = lax.axis_index("tensor")
        zhi = self.dp % 2
        self.z_far = self.dp + 1 - 2 * zhi
        self.pos = ring_pos(self.dp)
        self.next = [
            ring_dp(kind, (self.pos[kind] + step + 16) % 16, zhi) for kind, step in FLOWS
        ]
        self.core = self.tensor % 2
        self.buddy = self.tensor + 1 - 2 * self.core
        self.z_near = self.tensor + 2 - 4 * (self.tensor // 2)


class Ring:
    def __init__(self, place, first, mine, land, zland, total, out, sems):
        self.place, self.first, self.mine, self.land = place, first, mine, land
        self.zland, self.total, self.out = zland, total, out
        self.rs_s, self.rs_r, self.ag_s, self.ag_r, self.z_s, self.z_r, self.keep_s = sems

    def chunk(self, f, back):
        kind, step = FLOWS[f]
        return (self.place.pos[kind] - step * back + 32) % 16

    def rs(self, f, s, src):
        c = self.chunk(f, 1 + s)
        return pltpu.make_async_remote_copy(
            src.at[f, c], self.land.at[f, c], self.rs_s.at[f, s], self.rs_r.at[f, s],
            device_id=(self.place.next[f], self.place.tensor), device_id_type=MESH,
        )

    def ag(self, f, s, src):
        return pltpu.make_async_remote_copy(
            src, self.out.at[f, self.chunk(f, s)], self.ag_s.at[f, s], self.ag_r.at[f, s],
            device_id=(self.place.next[f], self.place.tensor), device_id_type=MESH,
        )

    def zcopy(self, f):
        return pltpu.make_async_remote_copy(
            self.land.at[f, self.chunk(f, 0)], self.zland.at[f], self.z_s.at[f], self.z_r.at[f],
            device_id=(self.place.z_far, self.place.tensor), device_id_type=MESH,
        )

    def keep(self, f):
        return pltpu.make_async_copy(
            self.total.at[f], self.out.at[f, self.chunk(f, 0)], self.keep_s.at[f]
        )

    def begin(self, f):
        self.rs(f, 0, self.first).start()

    def rs_step(self, s):
        for f in range(4):
            self.rs(f, s - 1, self.land).wait_recv()
            c = self.chunk(f, 1 + s)
            self.land[f, c] = self.land[f, c] + self.mine[f, c]
            self.rs(f, s, self.land).start()

    def turn(self):
        for f in range(4):
            self.rs(f, 14, self.land).wait_recv()
            c = self.chunk(f, 0)
            self.land[f, c] = self.land[f, c] + self.mine[f, c]
            self.zcopy(f).start()

    def back(self):
        for f in range(4):
            self.zcopy(f).wait_recv()
            self.total[f] = self.land[f, self.chunk(f, 0)] + self.zland[f]
            self.ag(f, 0, self.total.at[f]).start()
            self.keep(f).start()

    def ag_step(self, s):
        for f in range(4):
            held = self.out.at[f, self.chunk(f, s)]
            self.ag(f, s - 1, held).wait_recv()
            self.ag(f, s, held).start()

    def end(self):
        for f in range(4):
            self.ag(f, 14, self.total.at[f]).wait_recv()
            self.zcopy(f).wait_send()
            self.keep(f).wait()

    def drain(self, s):
        for f in range(4):
            self.rs(f, s, self.land).wait_send()
            self.ag(f, s, self.total.at[f]).wait_send()


class Sum4:
    def __init__(self, place, part, land1, land2, sems):
        self.place, self.part, self.land1, self.land2 = place, part, land1, land2
        self.s1, self.r1, self.s2, self.r2, self.s3, self.r3 = sems
        self.half = part.shape[0] // 2
        self.n = self.half // PIECES

    def local(self, k):
        return pl.ds(pl.multiple_of(k * self.n, self.n), self.n)

    def rows(self, k, core):
        return pl.ds(pl.multiple_of(core * self.half + k * self.n, self.n), self.n)

    def own(self, k):
        return self.rows(k, self.place.core)

    def other(self, k):
        return self.rows(k, 1 - self.place.core)

    def one(self, k):
        return pltpu.make_async_remote_copy(
            self.part.at[self.other(k)], self.land1.at[self.local(k)],
            self.s1.at[k], self.r1.at[k],
            device_id=(self.place.dp, self.place.buddy), device_id_type=MESH,
        )

    def two(self, k):
        return pltpu.make_async_remote_copy(
            self.land1.at[self.local(k)], self.land2.at[self.local(k)],
            self.s2.at[k], self.r2.at[k],
            device_id=(self.place.dp, self.place.z_near), device_id_type=MESH,
        )

    def three(self, k, src, dst):
        return pltpu.make_async_remote_copy(
            src, dst, self.s3.at[k], self.r3.at[k],
            device_id=(self.place.dp, self.place.buddy), device_id_type=MESH,
        )

    def begin(self):
        for k in range(PIECES):
            self.one(k).start()

    def middle(self, k):
        self.one(k).wait_recv()
        at = self.local(k)
        self.land1[at] = self.land1[at] + self.part[self.own(k)]
        self.two(k).start()

    def total(self, k):
        self.two(k).wait_recv()
        self.two(k).wait_send()
        at = self.local(k)
        return self.land1[at] + self.land2[at]


def greet(place, rings):
    barrier = pltpu.get_barrier_semaphore()
    peers = [(place.dp, place.buddy), (place.dp, place.z_near)]
    if rings:
        peers += [(q, place.tensor) for q in place.next + [place.z_far]]
    for peer in peers:
        pl.semaphore_signal(barrier, inc=1, device_id=peer, device_id_type=MESH)
    pl.semaphore_wait(barrier, len(peers))


def loop(low, high, body):
    def one(i, carry):
        body(i)
        return carry

    lax.fori_loop(low, high, one, 0)


def sum4_kernel(part, out, land1, land2, *sems):
    place = Place()
    greet(place, False)
    work = Sum4(place, part, land1, land2, sems)
    work.begin()
    loop(0, PIECES, work.middle)

    def finish(k):
        out[work.own(k)] = work.total(k)
        work.three(k, out.at[work.own(k)], out.at[work.own(k)]).start()

    loop(0, PIECES, finish)

    def close(k):
        work.three(k, out.at[work.own(k)], out.at[work.own(k)]).wait()
        work.one(k).wait_send()

    loop(0, PIECES, close)


def sum4(part):
    half = (part.shape[0] // 2, part.shape[1])
    return pl.pallas_call(
        sum4_kernel,
        out_shape=jax.ShapeDtypeStruct(part.shape, F32),
        in_specs=[VMEM],
        out_specs=VMEM,
        scratch_shapes=[pltpu.VMEM(half, F32)] * 2 + [DMA((PIECES,))] * 6,
        compiler_params=pltpu.CompilerParams(
            collective_id=1, has_side_effects=True, vmem_limit_bytes=32 << 20
        ),
    )(part)


def expert_kernel(
    hidden2, dy, w_gate, w_up, w_down, share, grads, dhidden2, out, hidden2_t
):
    step = pl.program_id(0)

    @pl.when(step == 0)
    def _():
        hidden2_t[...] = hidden2[...].T
        dhidden2[...] = jnp.zeros_like(dhidden2)
        out[...] = jnp.zeros_like(out)

    down_pair = w_down[...].reshape(256, 1024)
    dact_pair = dot_nt(dy[...], down_pair)
    acts = []
    for i in range(2):
        both_w = jnp.concatenate([w_gate[i], w_up[i]], 1)
        both = dot_nn(hidden2[...], both_w)
        gate, up = both[:, :128], both[:, 128:]
        sig = 1.0 / (1.0 + jnp.exp(-gate))
        silu = gate * sig
        weight = share[i]
        acts.append((silu * up * weight).astype(BF16))
        dact = dact_pair[:, 128 * i : 128 * i + 128] * weight
        dgate = (dact * up * (sig * (1.0 + gate * (1.0 - sig)))).astype(BF16)
        dup = (dact * silu).astype(BF16)
        dboth = jnp.concatenate([dgate, dup], 1)
        grad = dot_nn(hidden2_t[...], dboth)
        grads[i, :, 0:64] = grad[:, :128].reshape(16, 64, 128)
        grads[i, :, 64:128] = grad[:, 128:].reshape(16, 64, 128)
        dhidden2[...] += dot_nt(dboth, both_w)
    act_pair = jnp.concatenate(acts, 1)
    out[...] += dot_nn(act_pair, down_pair)
    down_grad = dot_tn(act_pair, dy[...])
    for i in range(2):
        for j in range(8):
            for half in range(2):
                at = 128 * i + 64 * half
                grads[i, 2 * j + half, 128:192] = down_grad[at : at + 64, 128 * j : 128 * j + 128]


def experts_part(hidden2, dy, w_gate, w_up, w_down, share):
    rows, width = hidden2.shape
    count = w_gate.shape[0]
    whole = pl.BlockSpec((rows, width), lambda p: (0, 0))
    return pl.pallas_call(
        expert_kernel,
        grid=(count // 2,),
        out_shape=(
            jax.ShapeDtypeStruct((count, 16, 192, 128), F32),
            jax.ShapeDtypeStruct((rows, width), F32),
            jax.ShapeDtypeStruct((rows, width), F32),
        ),
        in_specs=[
            whole,
            whole,
            pl.BlockSpec((2, width, 128), lambda p: (p, 0, 0)),
            pl.BlockSpec((2, width, 128), lambda p: (p, 0, 0)),
            pl.BlockSpec((2, 128, width), lambda p: (p, 0, 0)),
            pl.BlockSpec((2, rows, 1), lambda p: (p, 0, 0)),
        ],
        out_specs=(
            pl.BlockSpec((2, 16, 192, 128), lambda p: (p, 0, 0, 0)),
            whole,
            whole,
        ),
        scratch_shapes=[pltpu.VMEM((width, rows), BF16)],
        compiler_params=pltpu.CompilerParams(vmem_limit_bytes=48 << 20),
    )(hidden2, dy, w_gate, w_up, w_down, share)


def row_norm(values):
    inverse = lax.rsqrt(jnp.mean(values * values, -1, keepdims=True) + NORM_EPS)
    return values * inverse, inverse


def norm_back(gradient, scaled, inverse, gain_vec):
    scaled_grad = gradient * gain_vec
    inner_sum = jnp.mean(scaled_grad * scaled, -1, keepdims=True)
    return inverse * (scaled_grad - scaled * inner_sum)


def fold(values):
    return jnp.sum(values.reshape(-1, 8, values.shape[-1]), 0)


def back_kernel(
    grads, dhidden2, out_part, residual, tokens, dy, gain1, gain2, mixed, w_out, queries, keys,
    values, lse, seg_col, seg_row, cos_table, sin_table, hidden1, w_query, w_key, w_value,
    output, input_grad, grads_sum, attn_sum,
    mine, land, zland, total, attn, attn_land, attn_zland, attn_total,
    land1, land2, land3, dresidual, dhidden1, dqkv, gains, gains_in, *sems
):
    place = Place()
    greet(place, True)
    ring_sems, sems = sems[:7], sems[7:]
    attn_sems, sems = sems[:7], sems[7:]
    sum_sems, sems = sems[:6], sems[6:]
    load_sem, gain_s, gain_r = sems
    rings = [
        Ring(
            place, grads.at[u], mine.at[u], land.at[u], zland.at[u], total.at[u],
            grads_sum.at[u], [sem.at[u] for sem in ring_sems],
        )
        for u in range(2)
    ]
    attn_ring = Ring(
        place, attn, attn, attn_land, attn_zland, attn_total, attn_sum, attn_sems
    )
    sums = [
        Sum4(place, part, land1.at[i], land2.at[i], [sem.at[i] for sem in sum_sems])
        for i, part in enumerate((dhidden2, out_part, dhidden1))
    ]
    back2, forward2, back1 = sums

    back2.begin()
    for ring in rings:
        for f in range(4):
            ring.begin(f)
    loads = [pltpu.make_async_copy(grads.at[u], mine.at[u], load_sem.at[u]) for u in range(2)]
    for load in loads:
        load.start()
    gains[...] = jnp.zeros_like(gains)

    def step(s):
        for ring in rings:
            ring.rs_step(s)

    loop(0, PIECES, back2.middle)
    forward2.begin()
    for load in loads:
        load.wait()
    step(1)
    loop(0, PIECES, forward2.middle)
    step(2)

    def finish2(k):
        step(3 + k)
        d = back2.total(k)
        at = back2.own(k)
        scaled, inverse = row_norm(residual[at])
        gains[8:16] += fold(d * scaled)
        dresidual[at] = dy[at].astype(F32) + norm_back(d, scaled, inverse, gain2[...])
        back2.three(k, dresidual.at[at], dresidual.at[at]).start()

    loop(0, PIECES, finish2)

    def close2(k):
        at = back2.own(k)
        back2.three(k, dresidual.at[at], dresidual.at[at]).wait_recv()

    loop(0, PIECES, close2)

    dbranch = dresidual[...].astype(BF16)
    dmixed = dot_nt(dbranch, w_out[...]).astype(BF16)
    out_grad = dot_tn(mixed[...], dbranch)
    for j in range(8):
        piece = out_grad[:, 128 * j : 128 * j + 128].reshape(8, 32, 128)
        attn[j // 2, 8 * (j % 2) : 8 * (j % 2) + 8, 64:96] = piece
    attn[:, :, 96:104] = jnp.zeros((4, 16, 8, 128), F32)

    lane = lax.broadcasted_iota(jnp.int32, (512, 128), 1)
    first_half = lane % 64 < 32

    def unrotate(grad):
        swapped = jnp.where(first_half, pltpu.roll(grad, 96, 1), pltpu.roll(grad, 32, 1))
        return (grad * cos_table[...] + swapped * sin_table[...]).astype(BF16)

    dkeys, dvalues = [], []
    for g in range(2):
        key = keys[:, 64 * g : 64 * g + 64]
        value = values[:, 64 * g : 64 * g + 64]
        dkey = [0.0, 0.0]
        dvalue = [0.0, 0.0]
        dquery = []
        for h in (2 * g, 2 * g + 1):
            blocks = []
            for b in range(2):
                at = slice(256 * b, 256 * b + 256)
                until = 256 * b + 256
                query = queries[at, 64 * h : 64 * h + 64]
                dmix = dmixed[at, 64 * h : 64 * h + 64]
                raw = dot_nt(key[:until], query) * HD ** (-0.5)
                allowed = (seg_col[:until] == seg_row[:, at]) & (
                    lax.broadcasted_iota(jnp.int32, raw.shape, 0)
                    <= lax.broadcasted_iota(jnp.int32, raw.shape, 1) + 256 * b
                )
                probs = jnp.exp(jnp.where(allowed, raw, -1e30) - lse[h : h + 1, at])
                dprobs = dot_nt(value[:until], dmix)
                inner = jnp.sum(probs * dprobs, 0, keepdims=True)
                dscores = (probs * (dprobs - inner)).astype(BF16)
                dvalue_part = dot_nn(probs.astype(BF16), dmix)
                dkey_part = dot_nn(dscores, query)
                for t in range(b + 1):
                    dvalue[t] = dvalue[t] + dvalue_part[256 * t : 256 * t + 256]
                    dkey[t] = dkey[t] + dkey_part[256 * t : 256 * t + 256]
                blocks.append(dot_tn(dscores, key[:until]))
            dquery.append(jnp.concatenate(blocks, 0) * HD ** (-0.5))
            step(7 + h)
        dqkv[:, 128 * g : 128 * g + 128] = unrotate(jnp.concatenate(dquery, 1))
        dkeys.append(jnp.concatenate(dkey, 0) * HD ** (-0.5))
        dvalues.append(jnp.concatenate(dvalue, 0))
    dqkv[:, 256:384] = unrotate(jnp.concatenate(dkeys, 1))
    dqkv[:, 384:512] = jnp.concatenate(dvalues, 1).astype(BF16)

    dhidden1[...] = (
        dot_nt(dqkv[:, :256], w_query[...])
        + dot_nt(dqkv[:, 256:384], w_key[...])
        + dot_nt(dqkv[:, 384:512], w_value[...])
    )
    back1.begin()
    step(11)

    def finish_out(k):
        done = forward2.total(k) + residual[forward2.own(k)]
        at = forward2.local(k)
        output[forward2.own(k)] = done.astype(BF16)
        forward2.land1[at] = done
        forward2.three(k, forward2.land1.at[at], land3.at[at]).start()

    loop(0, PIECES, finish_out)
    loop(0, PIECES, back1.middle)
    step(12)
    hidden_grad = dot_tn(hidden1[...], dqkv[...])
    for j in range(4):
        piece = hidden_grad[:, 128 * j : 128 * j + 128].reshape(4, 16, 16, 128)
        attn[:, :, 16 * j : 16 * j + 16] = piece
    step(13)
    step(14)
    for ring in rings:
        ring.turn()

    def close_out(k):
        at = forward2.local(k)
        forward2.three(k, forward2.land1.at[at], land3.at[at]).wait_recv()
        output[forward2.other(k)] = land3[at].astype(BF16)

    loop(0, PIECES, close_out)
    for ring in rings:
        ring.back()

    def finish1(k):
        d = back1.total(k)
        at = back1.own(k)
        scaled, inverse = row_norm(tokens[at].astype(F32))
        gains[0:8] += fold(d * scaled)
        input_grad[at] = dresidual[at] + norm_back(d, scaled, inverse, gain1[...])
        back1.three(k, input_grad.at[at], input_grad.at[at]).start()

    loop(0, PIECES, finish1)
    swap = pltpu.make_async_remote_copy(
        gains, gains_in, gain_s, gain_r,
        device_id=(place.dp, place.buddy), device_id_type=MESH,
    )
    swap.start()
    for ring in rings:
        ring.ag_step(1)
    swap.wait_recv()
    for j in range(16):
        rows = slice(8 * (j // 8), 8 * (j // 8) + 8)
        lanes = slice(128 * (j % 8), 128 * (j % 8) + 128)
        attn[0, j, 96:104] = gains[rows, lanes] + gains_in[rows, lanes]
    for f in range(4):
        attn_ring.begin(f)

    def both(s):
        for ring in rings:
            ring.ag_step(s)
        attn_ring.rs_step(s - 1)

    loop(2, 15, both)
    attn_ring.rs_step(14)
    attn_ring.turn()
    for ring in rings:
        ring.end()
    attn_ring.back()
    loop(1, 15, attn_ring.ag_step)
    attn_ring.end()

    def drain(s):
        for ring in rings + [attn_ring]:
            ring.drain(s)

    loop(0, 15, drain)
    swap.wait_send()

    def close(k):
        for work in sums:
            work.one(k).wait_send()
        at = back2.own(k)
        back2.three(k, dresidual.at[at], dresidual.at[at]).wait_send()
        here = forward2.local(k)
        forward2.three(k, forward2.land1.at[here], land3.at[here]).wait_send()
        back1.three(k, input_grad.at[at], input_grad.at[at]).wait()

    loop(0, PIECES, close)


def back_part(grads, *rest):
    rows, width = rest[0].shape
    half = (rows // 2, width)
    m, n = grads.shape[3], 104
    S = pltpu.VMEM
    ring_sems = [DMA((2, 4, 15))] * 4 + [DMA((2, 4))] * 3
    attn_sems = [DMA((4, 15))] * 4 + [DMA((4,))] * 3
    return pl.pallas_call(
        back_kernel,
        out_shape=(
            jax.ShapeDtypeStruct((rows, width), BF16),
            jax.ShapeDtypeStruct((rows, width), F32),
            jax.ShapeDtypeStruct(grads.shape, F32),
            jax.ShapeDtypeStruct((4, 16, n, 128), F32),
        ),
        in_specs=[ANY] + [VMEM] * len(rest),
        out_specs=(VMEM, VMEM, ANY, ANY),
        scratch_shapes=[
            S(grads.shape, F32), S(grads.shape, F32), S((2, 4, m, 128), F32),
            S((2, 4, m, 128), F32),
            S((4, 16, n, 128), F32), S((4, 16, n, 128), F32), S((4, n, 128), F32),
            S((4, n, 128), F32),
            S((3,) + half, F32), S((3,) + half, F32), S(half, F32),
            S((rows, width), F32), S((rows, width), F32), S((rows, 512), BF16),
            S((16, width), F32), S((16, width), F32),
        ]
        + ring_sems
        + attn_sems
        + [DMA((3, PIECES))] * 6
        + [DMA((2,)), DMA, DMA],
        compiler_params=pltpu.CompilerParams(
            collective_id=2, has_side_effects=True, vmem_limit_bytes=63 << 20
        ),
    )(grads, *rest)


def tables(seq_count, seq_length, head_width):
    half_width = head_width // 2
    frequency = ROPE_THETA ** (-jnp.arange(half_width, dtype=jnp.float32) * 2.0 / head_width)
    position = jnp.tile(jnp.arange(seq_length), seq_count).astype(jnp.float32)
    angles = position[:, None] * frequency[None, :]
    return (jnp.cos(angles), jnp.sin(angles))


def rotate(values, cos_table, sin_table):
    half_width = values.shape[-1] // 2
    first_half = values[..., :half_width]
    second_half = values[..., half_width:]
    return jnp.concatenate(
        [
            first_half * cos_table - second_half * sin_table,
            second_half * cos_table + first_half * sin_table,
        ],
        -1,
    )


def local(
    tokens,
    norm1_gain,
    w_query,
    w_key,
    w_value,
    w_out,
    norm2_gain,
    expert_gate,
    expert_up,
    expert_down,
    routes,
    gate_weights,
    segments,
    cotangent,
):
    seq_count, seq_length = segments.shape
    tok_rows = tokens.shape[0]
    head_count = w_query.shape[1] // HD
    groups = w_key.shape[1] // HD
    group_size = head_count // groups
    experts = expert_gate.shape[0]
    cos_half, sin_half = tables(seq_count, seq_length, HD)
    cos_table, sin_table = cos_half[:, None, :], sin_half[:, None, :]
    inputs = tokens.astype(F32)
    scaled1, inverse1 = row_norm(inputs)
    hidden1 = (scaled1 * norm1_gain).astype(BF16)
    queries = rotate(
        dot_nn(hidden1, w_query).reshape(tok_rows, head_count, HD), cos_table, sin_table
    ).astype(BF16)
    keys = rotate(
        dot_nn(hidden1, w_key).reshape(tok_rows, groups, HD), cos_table, sin_table
    ).astype(BF16)
    values = dot_nn(hidden1, w_value).astype(BF16)
    query_blocks = queries.reshape(seq_count, seq_length, groups, group_size, HD)
    key_blocks = keys.reshape(seq_count, seq_length, groups, HD)
    value_blocks = values.reshape(seq_count, seq_length, groups, HD)
    raw_scores = jnp.einsum(
        "bqngd,bknd->bngqk", query_blocks, key_blocks, preferred_element_type=F32
    ) * HD ** (-0.5)
    position = jnp.arange(seq_length)
    allowed = (segments[:, :, None] == segments[:, None, :]) & (
        position[:, None] >= position[None, :]
    )
    scores = jnp.where(allowed[:, None, None, :, :], raw_scores, -1e30)
    row_max = jnp.max(scores, -1, keepdims=True)
    weights = jnp.exp(scores - row_max)
    row_total = jnp.sum(weights, -1, keepdims=True)
    probabilities = weights / row_total
    log_total = (row_max + jnp.log(row_total)).reshape(head_count, tok_rows)
    mixed_heads = jnp.einsum(
        "bngqk,bknd->bqngd",
        probabilities.astype(BF16),
        value_blocks,
        preferred_element_type=F32,
    )
    mixed_heads = mixed_heads.reshape(tok_rows, head_count * HD).astype(BF16)
    residual = inputs + sum4(dot_nn(mixed_heads, w_out))
    hidden2 = (row_norm(residual)[0] * norm2_gain).astype(BF16)
    picked = (routes[:, :, None] == jnp.arange(experts)[None, None, :]).astype(F32)
    expert_share = jnp.sum(gate_weights[:, :, None] * picked, 1).T[:, :, None]
    expert_grads, dhidden2, out_part = experts_part(
        hidden2, cotangent, expert_gate, expert_up, expert_down, expert_share
    )
    output, input_grad, grads, attn = back_part(
        expert_grads.reshape(2, 4, 16, 192, 128),
        dhidden2,
        out_part,
        residual,
        tokens,
        cotangent,
        norm1_gain[None],
        norm2_gain[None],
        mixed_heads,
        w_out,
        queries.reshape(tok_rows, -1),
        keys.reshape(tok_rows, -1),
        values,
        log_total,
        segments.reshape(tok_rows, 1),
        segments,
        jnp.tile(cos_half, (1, 4)),
        jnp.tile(jnp.concatenate([sin_half, -sin_half], 1), (1, 2)),
        hidden1,
        w_query,
        w_key,
        w_value,
    )
    grads = grads.reshape(experts, 16, 192, 128)
    gate_grad = grads[:, :, 0:64].reshape(experts, -1, 128)
    up_grad = grads[:, :, 64:128].reshape(experts, -1, 128)
    down_grad = grads[:, :, 128:192].reshape(experts, 8, 128, 128)
    down_grad = down_grad.transpose(0, 2, 1, 3).reshape(experts, 128, -1)
    attn = attn.reshape(64, 104, 128)
    query_grad = jnp.concatenate(
        [attn[:, 0:16].reshape(-1, 128), attn[:, 16:32].reshape(-1, 128)], 1
    )
    key_grad = attn[:, 32:48].reshape(-1, 128)
    value_grad = attn[:, 48:64].reshape(-1, 128)
    out_grad = attn[:, 64:96].reshape(8, 256, 128).transpose(1, 0, 2).reshape(256, -1)
    gain1_grad = jnp.sum(attn[0:8, 96:104], 1).reshape(-1)
    gain2_grad = jnp.sum(attn[8:16, 96:104], 1).reshape(-1)
    return (
        output,
        input_grad,
        gain1_grad,
        query_grad,
        key_grad,
        value_grad,
        out_grad,
        gain2_grad,
        gate_grad,
        up_grad,
        down_grad,
    )


def solution(mesh):
    return jax.shard_map(
        local,
        mesh=mesh,
        in_specs=(
            P("dp", None),
            P(),
            P(None, "tensor"),
            P(None, "tensor"),
            P(None, "tensor"),
            P("tensor", None),
            P(),
            P(None, None, "tensor"),
            P(None, None, "tensor"),
            P(None, "tensor", None),
            P("dp", None),
            P("dp", None),
            P("dp", None),
            P("dp", None),
        ),
        out_specs=(
            P("dp", None),
            P("dp", None),
            P(),
            P(None, "tensor"),
            P(None, "tensor"),
            P(None, "tensor"),
            P("tensor", None),
            P(),
            P(None, None, "tensor"),
            P(None, None, "tensor"),
            P(None, "tensor", None),
        ),
        check_vma=False,
    )
```

time: 1450 us -> 361 us (0.25)
  waiting for transfers between devices: 1230 us -> 0 us
  Pallas kernels: 0 us -> 307 us
  blocking collectives: 98.1 us -> 0 us
  matrix products: 47.7 us -> 4.11 us
    reduce_scatter x3 -> x0, waiting for transfers between devices: 563 us -> none  [the longest x1 191 us: local(): lax.psum_scatter(down_grad, 'dp', scatter_dimension=2, tiled=True)]
    psum x4 -> x0, waiting for transfers between devices: 527 us -> none  [the longest x1 357 us: local(): lax.psum((query_w_grad, key_w_grad, value_w_grad, out_w_grad, gain1_grad,...]
    pallas_call x0 -> x3, Pallas kernels: none -> 307 us  [the longest x1 261 us: back_part(): pl.pallas_call(back_kernel, out_shape=(jax.ShapeDtypeStruct((rows, width)...]
    all_gather x3 -> x0, waiting for transfers between devices: 140 us -> none  [the longest x1 79.1 us: local(): lax.all_gather(scattered[2], 'dp', axis=2, tiled=True)]
    psum x1 -> x0, blocking collectives: 98.1 us -> none  [local(): lax.psum((query_w_grad, key_w_grad, value_w_grad, out_w_grad, gain1_grad,...]
    dot_general x27 -> x6, matrix products: 47.7 us -> 4.11 us  [the longest x4 1.85 us: dot_nn(): return jnp.dot(first_op, second_op, preferred_element_type=F32)]
    unnamed x101 -> x31, local copies, waits for them, and re-layouts: 27.1 us -> 6.14 us
  transfers between devices with their start and end apart: 10 -> 0, of which waited for: 9 -> 0; matrix products, arithmetic and copies ran while one was open for 5% -> 0% of each run, Pallas kernels for 0% -> 0%
where the time goes in v2:
time: 361 us; the launch traced here: 360 us
  Pallas kernels  307 us (85%)
  local copies, waits for them, and re-layouts  38.8 us (11%)
  other arithmetic  9.45 us (3%)
  matrix products  4.11 us (1%)
    pallas_call x1, Pallas kernels, back_part(): pl.pallas_call(back_kernel, out_shape=(jax.ShapeDtypeStruct((rows, width)...  261 us
    pallas_call x1, Pallas kernels, sum4(): pl.pallas_call(sum4_kernel, out_shape=jax.ShapeDtypeStruct(part.shape, F3...  28.4 us
    pallas_call x1, Pallas kernels, experts_part(): pl.pallas_call(expert_kernel, grid=(count // 2,), out_shape=(jax.ShapeDty...  17.1 us
    slice x1, local copies, waits for them, and re-layouts, local(): down_grad = grads[:, :, 128:192].reshape(experts, 8, 128, 128)  10.4 us

profile of v2, /device:TPU:0, one launch (start us, length us, event | category | flops | bytes accessed | tf_op | source)
XLA Modules:
  0.0 360.1 jit_solution(1152006022117564297)
XLA Ops:
  0.6 0.0 copy-start.4
  0.7 0.0 copy-start.9
  0.7 0.0 copy-start.10
  0.7 1.6 fusion.2
  2.3 0.7 select_reduce_fusion
  3.1 0.3 fusion.16
  3.4 0.0 copy-start.6
  3.4 0.8 copy.64.sin_table
  4.3 1.7 fusion.10
  6.0 0.8 copy.63.cos_table
  6.8 1.5 copy.62.seg_col
  8.3 0.0 copy-done.4
  8.3 1.0 fusion.4.hidden1
  9.3 0.0 copy-done.9
  9.3 0.0 copy-start.2
  9.3 0.4 convolution_convert_fusion.values
  9.8 0.0 copy-start.8
  9.8 0.1 copy.56
  9.9 0.0 copy-done.10
  9.9 0.0 copy-start.11
  9.9 0.5 fusion.22
  10.5 0.8 copy.61.keys
  11.3 0.0 copy-done.6
  11.3 0.5 fusion.23
  11.7 0.1 subtract_convert_fusion
  11.9 0.8 copy.60.queries
  12.7 0.0 copy-done.2
  12.7 2.0 copy.58.share
  14.7 0.0 copy-done.8
  14.7 0.0 copy-done.11
  14.7 0.9 fusion.1
  15.6 0.9 fusion
  16.5 0.0 copy-start.7
  16.5 1.4 fusion.7
  17.9 0.6 add.40.lse
  18.5 0.8 copy.59.mixed
  19.4 0.0 copy-done.7
  19.4 0.5 fusion.24.part
  19.8 0.0 copy-start.13
  19.8 28.4 %shard_map.221 = f32[512,1024]{1,0:T(8,128)S(1)} custom-call(f32[512,1024]{1,0:T(8,128)S(1)} %fusion.24.part), custom_call_target="tpu_custom_call" | custom-call | tf_op jit(solution)/shard_map/pallas_call | solution.py:241
  48.2 0.0 copy-start
  48.3 0.3 multiply_reduce_fusion
  48.6 0.0 copy-start.3
  48.6 1.3 copy-done.3
  49.9 0.0 copy-done.13
  49.9 0.2 multiply_convert_fusion.hidden2
  50.2 0.0 copy-done
  50.2 17.1 %shard_map.222 = (f32[8,16,192,128]{3,2,1,0:T(8,128)}, f32[512,1024]{1,0:T(8,128)S(1)}, f32[512,1024]{1,0:T(8,128)}) custom-call(bf16[512,1024]{1,0:T(8,128)(2,1)S(1)} %multiply_convert_fusion.hidden2, bf16[512,1024]{1,0:T(8,128)(2,1)S(1)} %copy-done, bf16[8,1024,128]{2,1,0:T(8,128)(2,1)} %w_gate.1, bf16[8,1024,128]{2,1,0:T(8,128)(2,1)} %w_up.1, ...), custom_call_target="tpu_custom_call" | custom-call | tf_op jit(solution)/shard_map/pallas_call | solution.py:297
  67.3 0.0 copy-start.1
  67.3 1.3 copy-done.1
  68.6 261.3 %shard_map.223 = (bf16[512,1024]{1,0:T(8,128)(2,1)}, f32[512,1024]{1,0:T(8,128)}, f32[2,4,16,192,128]{4,3,2,1,0:T(8,128)}, f32[4,16,104,128]{3,2,1,0:T(8,128)}) custom-call(f32[2,4,16,192,128]{4,3,2,1,0:T(8,128)} %bitcast.87, f32[512,1024]{1,0:T(8,128)} %copy-done.1, f32[512,1024]{1,0:T(8,128)} %get-tuple-element.20.out_part, f32[512,1024]{1,0:T(8,128)} %copy-done.3, ...), custom_call_target="tpu_custom_call" | custom-call | tf_op jit(solution)/shard_map/pallas_call | solution.py:557
  329.9 1.4 slice_reduce_fusion
  331.3 1.3 slice.65
  332.6 2.6 fusion.21
  335.2 0.6 copy.65
  335.9 1.2 copy.75
  337.0 1.0 pad_maximum_fusion
  338.1 10.4 %fusion.20 = (f32[8,16,64,128]{3,2,1,0:T(8,128)S(1)}, f32[8,16,64,128]{3,2,1,0:T(8,128)}, f32[8,16,64,128]{3,2,1,0:T(8,128)}) fusion(f32[8,16,192,128]{3,2,1,0:T(8,128)} %bitcast.86), kind=kLoop, calls=%fused_computation.49 | loop fusion | bytes 25165824 | tf_op jit(solution)/shard_map/slice | solution.py:698
  348.4 4.3 %copy.74 = f32[8,8,128,128]{3,1,2,0:T(8,128)} copy(f32[8,8,128,128]{3,2,1,0:T(8,128)S(1)} %bitcast.85) | data formatting | bytes 8388608 | tf_op jit(solution)/shard_map/reshape | solution.py:698
  352.7 5.1 %reshape.330 = f32[8,128,1024]{2,1,0:T(8,128)} reshape(f32[8,128,8,128]{3,2,1,0:T(8,128)} %bitcast.84) | data formatting | bytes 8388608 | tf_op jit(solution)/shard_map/reshape | solution.py:699
  357.8 0.0 copy-done.12
  357.8 1.0 copy.78
  358.8 0.0 copy-done.5
  358.8 1.3 copy.79
  (13 shorter events, 0.2 us)
Async XLA Ops:
  0.6 7.7 %copy-start.4 = (bf16[512,1024]{1,0:T(8,128)(2,1)S(1)}, bf16[512,1024]{1,0:T(8,128)(2,1)}, u32[]{:S(2)}) copy-start(bf16[512,1024]{1,0:T(8,128)(2,1)} %tokens.1) | copy-start | bytes 3145732
  0.7 8.7 %copy-start.9 = (bf16[1024,128]{1,0:T(8,128)(2,1)S(1)}, bf16[1024,128]{1,0:T(8,128)(2,1)}, u32[]{:S(2)}) copy-start(bf16[1024,128]{1,0:T(8,128)(2,1)} %w_value.1) | copy-start | bytes 786436
  0.7 9.3 %copy-start.10 = (bf16[1024,128]{1,0:T(8,128)(2,1)S(1)}, bf16[1024,128]{1,0:T(8,128)(2,1)}, u32[]{:S(2)}) copy-start(bf16[1024,128]{1,0:T(8,128)(2,1)} %w_key.1) | copy-start | bytes 786436
  3.4 7.8 %copy-start.6 = (bf16[1024,256]{1,0:T(8,128)(2,1)S(1)}, bf16[1024,256]{1,0:T(8,128)(2,1)}, u32[]{:S(2)}) copy-start(bf16[1024,256]{1,0:T(8,128)(2,1)} %w_query.1) | copy-start | bytes 1572868
  9.3 3.4 copy-start.2
  9.8 4.9 %copy-start.8 = (bf16[512,128]{1,0:T(8,128)(2,1)}, bf16[512,128]{1,0:T(8,128)(2,1)S(1)}, u32[]{:S(2)}) copy-start(bf16[512,128]{1,0:T(8,128)(2,1)S(1)} %convolution_convert_fusion.values) | copy-start | bytes 393220
  9.9 4.7 %copy-start.11 = (pred[512,512]{0,1:T(8,128)(4,1)S(1)}, pred[512,512]{0,1:T(8,128)(4,1)}, u32[]{:S(2)}) copy-start(pred[512,512]{0,1:T(8,128)(4,1)} %fusion.10) | copy-start | bytes 786436
  16.5 2.9 copy-start.7
  19.8 30.1 %copy-start.13 = (f32[1024]{0:T(1024)S(1)}, f32[1024]{0:T(1024)}, u32[]{:S(2)}) copy-start(f32[1024]{0:T(1024)} %param.20) | copy-start | bytes 12292
  48.2 1.9 copy-start
  48.6 1.3 copy-start.3
  67.3 1.3 copy-start.1
  352.7 5.1 %copy-start.12 = (bf16[512,1024]{1,0:T(8,128)(2,1)S(1)}, bf16[512,1024]{1,0:T(8,128)(2,1)}, u32[]{:S(2)}) copy-start(bf16[512,1024]{1,0:T(8,128)(2,1)} %get-tuple-element.56) | copy-start | bytes 3145732
  352.7 6.0 %copy-start.5 = (f32[512,1024]{1,0:T(8,128)S(1)}, f32[512,1024]{1,0:T(8,128)}, u32[]{:S(2)}) copy-start(f32[512,1024]{1,0:T(8,128)} %get-tuple-element.57) | copy-start | bytes 6291460

commit v3 on v2

--- a/solution.py
+++ b/solution.py
@@ -61,6 +61,17 @@
         self.next = [
             ring_dp(kind, (self.pos[kind] + step + 16) % 16, zhi) for kind, step in FLOWS
         ]
+        xy = self.dp // 2
+        x, y = xy % 4, xy // 4
+        self.x, self.y = x, y
+
+        def at(dx, dy):
+            return (((y + dy + 4) % 4) * 4 + (x + dx + 4) % 4) * 2 + zhi
+
+        self.across = [at(1, 0), at(-1, 0), at(0, 1), at(0, -1)]
+        self.pairs = [
+            at(1 - 2 * (x % 2), 0), at(2, 0), at(0, 1 - 2 * (y % 2)), at(0, 2), self.z_far
+        ]
         self.core = self.tensor % 2
         self.buddy = self.tensor + 1 - 2 * self.core
         self.z_near = self.tensor + 2 - 4 * (self.tensor // 2)
@@ -140,6 +151,114 @@
         for f in range(4):
             self.rs(f, s, self.land).wait_send()
             self.ag(f, s, self.total.at[f]).wait_send()
+
+
+class AxisRing:
+    def __init__(self, place, mine, land, land2, zland, total, out, sems):
+        self.place, self.mine, self.land, self.land2 = place, mine, land, land2
+        self.zland, self.total, self.out, self.sems = zland, total, out, sems
+
+    def spots(self, f, back1, back2):
+        step = 1 - 2 * (f % 2)
+        pos1, pos2 = self.place.x, self.place.y
+        if f >= 2:
+            pos1, pos2 = pos2, pos1
+        return (pos1 - step * back1 + 8) % 4, (pos2 - step * back2 + 8) % 4
+
+    def send(self, f, s, stage, src, dst):
+        axis = f // 2 if stage in (0, 3) else 1 - f // 2
+        return pltpu.make_async_remote_copy(
+            src, dst, self.sems[2 * stage].at[f, s], self.sems[2 * stage + 1].at[f, s],
+            device_id=(self.place.across[2 * axis + f % 2], self.place.tensor),
+            device_id_type=MESH,
+        )
+
+    def rs1(self, f, s, src):
+        i = self.spots(f, 1 + s, 0)[0]
+        return self.send(f, s, 0, src.at[f, i], self.land.at[f, i])
+
+    def rs2(self, f, s, src):
+        j = self.spots(f, 0, 1 + s)[1]
+        return self.send(f, s, 1, src.at[j], self.land2.at[f, j])
+
+    def ag2(self, f, s, src):
+        i, j = self.spots(f, 0, s)
+        return self.send(f, s, 2, src, self.out.at[f, i, j])
+
+    def ag1(self, f, s, src):
+        return self.send(f, s, 3, src, self.out.at[f, self.spots(f, s, 0)[0]])
+
+    def zcopy(self, f):
+        return pltpu.make_async_remote_copy(
+            self.land2.at[f, self.spots(f, 0, 0)[1]], self.zland.at[f],
+            self.sems[8].at[f], self.sems[9].at[f],
+            device_id=(self.place.z_far, self.place.tensor), device_id_type=MESH,
+        )
+
+    def keep(self, f):
+        i, j = self.spots(f, 0, 0)
+        return pltpu.make_async_copy(
+            self.total.at[f], self.out.at[f, i, j], self.sems[10].at[f]
+        )
+
+    def begin(self):
+        for f in range(4):
+            self.rs1(f, 0, self.mine).start()
+
+    def rs1_step(self, s):
+        for f in range(4):
+            self.rs1(f, s - 1, self.land).wait_recv()
+            i = self.spots(f, 1 + s, 0)[0]
+            self.land[f, i] = self.land[f, i] + self.mine[f, i]
+            if s < 3:
+                self.rs1(f, s, self.land).start()
+            else:
+                self.rs2(f, 0, self.land.at[f, i]).start()
+
+    def rs2_step(self, s):
+        for f in range(4):
+            i, j = self.spots(f, 0, 1 + s)
+            self.rs2(f, s - 1, self.land2.at[f]).wait_recv()
+            self.land2[f, j] = self.land2[f, j] + self.land[f, i, j]
+            if s < 3:
+                self.rs2(f, s, self.land2.at[f]).start()
+            else:
+                self.zcopy(f).start()
+
+    def back(self):
+        for f in range(4):
+            self.zcopy(f).wait_recv()
+            self.total[f] = self.land2[f, self.spots(f, 0, 0)[1]] + self.zland[f]
+            self.ag2(f, 0, self.total.at[f]).start()
+            self.keep(f).start()
+
+    def ag2_step(self, s):
+        for f in range(4):
+            self.ag2(f, s - 1, self.total.at[f]).wait_recv()
+            i, j = self.spots(f, 0, s)
+            if s < 3:
+                self.ag2(f, s, self.out.at[f, i, j]).start()
+            else:
+                self.keep(f).wait()
+                self.ag1(f, 0, self.out.at[f, i]).start()
+
+    def ag1_step(self, s):
+        for f in range(4):
+            held = self.out.at[f, self.spots(f, s, 0)[0]]
+            self.ag1(f, s - 1, held).wait_recv()
+            if s < 3:
+                self.ag1(f, s, held).start()
+
+    def drain(self, s):
+        for f in range(4):
+            self.rs1(f, s, self.land).wait_send()
+            self.rs2(f, s, self.land2.at[f]).wait_send()
+            self.ag2(f, s, self.total.at[f]).wait_send()
+            self.ag1(f, s, self.out.at[f, 0]).wait_send()
+
+    def close(self):
+        for f in range(4):
+            self.zcopy(f).wait_send()
 
 
 class Sum4:
@@ -202,7 +321,8 @@
     barrier = pltpu.get_barrier_semaphore()
     peers = [(place.dp, place.buddy), (place.dp, place.z_near)]
     if rings:
-        peers += [(q, place.tensor) for q in place.next + [place.z_far]]
+        peers += [(q, place.tensor) for q in place.across + [place.z_far]]
+        peers += [(place.pairs[1], place.tensor), (place.pairs[3], place.tensor)]
     for peer in peers:
         pl.semaphore_signal(barrier, inc=1, device_id=peer, device_id_type=MESH)
     pl.semaphore_wait(barrier, len(peers))
@@ -338,14 +458,14 @@
 def back_kernel(
     grads, dhidden2, out_part, residual, tokens, dy, gain1, gain2, mixed, w_out, queries, keys,
     values, lse, seg_col, seg_row, cos_table, sin_table, hidden1, w_query, w_key, w_value,
-    output, input_grad, grads_sum, attn_sum,
-    mine, land, zland, total, attn, attn_land, attn_zland, attn_total,
-    land1, land2, land3, dresidual, dhidden1, dqkv, gains, gains_in, *sems
+    output, input_grad, gain_sums, grads_sum, attn_sum,
+    mine, land, zland, total, attn, attn_land, attn_land2, attn_zland, attn_total,
+    land1, land2, land3, dresidual, dhidden1, dqkv, folded, gains, gains_in, *sems
 ):
     place = Place()
     greet(place, True)
     ring_sems, sems = sems[:7], sems[7:]
-    attn_sems, sems = sems[:7], sems[7:]
+    attn_sems, sems = sems[:11], sems[11:]
     sum_sems, sems = sems[:6], sems[6:]
     load_sem, gain_s, gain_r = sems
     rings = [
@@ -355,8 +475,8 @@
         )
         for u in range(2)
     ]
-    attn_ring = Ring(
-        place, attn, attn, attn_land, attn_zland, attn_total, attn_sum, attn_sems
+    attn_ring = AxisRing(
+        place, attn, attn_land, attn_land2, attn_zland, attn_total, attn_sum, attn_sems
     )
     sums = [
         Sum4(place, part, land1.at[i], land2.at[i], [sem.at[i] for sem in sum_sems])
@@ -371,26 +491,27 @@
     loads = [pltpu.make_async_copy(grads.at[u], mine.at[u], load_sem.at[u]) for u in range(2)]
     for load in loads:
         load.start()
-    gains[...] = jnp.zeros_like(gains)
+    folded[...] = jnp.zeros_like(folded)
 
     def step(s):
         for ring in rings:
             ring.rs_step(s)
 
+    def gather(s):
+        for ring in rings:
+            ring.ag_step(s)
+
     loop(0, PIECES, back2.middle)
-    forward2.begin()
     for load in loads:
         load.wait()
     step(1)
-    loop(0, PIECES, forward2.middle)
-    step(2)
 
     def finish2(k):
-        step(3 + k)
+        step(2 + k)
         d = back2.total(k)
         at = back2.own(k)
         scaled, inverse = row_norm(residual[at])
-        gains[8:16] += fold(d * scaled)
+        folded[8:16] += fold(d * scaled)
         dresidual[at] = dy[at].astype(F32) + norm_back(d, scaled, inverse, gain2[...])
         back2.three(k, dresidual.at[at], dresidual.at[at]).start()
 
@@ -406,9 +527,8 @@
     dmixed = dot_nt(dbranch, w_out[...]).astype(BF16)
     out_grad = dot_tn(mixed[...], dbranch)
     for j in range(8):
-        piece = out_grad[:, 128 * j : 128 * j + 128].reshape(8, 32, 128)
-        attn[j // 2, 8 * (j % 2) : 8 * (j % 2) + 8, 64:96] = piece
-    attn[:, :, 96:104] = jnp.zeros((4, 16, 8, 128), F32)
+        piece = out_grad[:, 128 * j : 128 * j + 128].reshape(2, 4, 32, 128)
+        attn[j // 2, 2 * (j % 2) : 2 * (j % 2) + 2, :, 64:96] = piece
 
     lane = lax.broadcasted_iota(jnp.int32, (512, 128), 1)
     first_half = lane % 64 < 32
@@ -446,21 +566,72 @@
                     dvalue[t] = dvalue[t] + dvalue_part[256 * t : 256 * t + 256]
                     dkey[t] = dkey[t] + dkey_part[256 * t : 256 * t + 256]
                 blocks.append(dot_tn(dscores, key[:until]))
+                step(6 + 2 * h + b)
             dquery.append(jnp.concatenate(blocks, 0) * HD ** (-0.5))
-            step(7 + h)
         dqkv[:, 128 * g : 128 * g + 128] = unrotate(jnp.concatenate(dquery, 1))
         dkeys.append(jnp.concatenate(dkey, 0) * HD ** (-0.5))
         dvalues.append(jnp.concatenate(dvalue, 0))
     dqkv[:, 256:384] = unrotate(jnp.concatenate(dkeys, 1))
     dqkv[:, 384:512] = jnp.concatenate(dvalues, 1).astype(BF16)
 
+    hidden_grad = dot_tn(hidden1[...], dqkv[...])
+    for j in range(4):
+        piece = hidden_grad[:, 128 * j : 128 * j + 128].reshape(4, 4, 4, 16, 128)
+        attn[:, :, :, 16 * j : 16 * j + 16] = piece
+    attn_ring.begin()
+    step(14)
+    for ring in rings:
+        ring.turn()
     dhidden1[...] = (
         dot_nt(dqkv[:, :256], w_query[...])
         + dot_nt(dqkv[:, 256:384], w_key[...])
         + dot_nt(dqkv[:, 384:512], w_value[...])
     )
     back1.begin()
-    step(11)
+    attn_ring.rs1_step(1)
+    loop(0, PIECES, back1.middle)
+    forward2.begin()
+    attn_ring.rs1_step(2)
+    for ring in rings:
+        ring.back()
+    loop(0, PIECES, forward2.middle)
+    gather(1)
+    attn_ring.rs1_step(3)
+    gather(2)
+    attn_ring.rs2_step(1)
+
+    def finish1(k):
+        gather(3 + k)
+        d = back1.total(k)
+        at = back1.own(k)
+        scaled, inverse = row_norm(tokens[at].astype(F32))
+        folded[0:8] += fold(d * scaled)
+        input_grad[at] = dresidual[at] + norm_back(d, scaled, inverse, gain1[...])
+        back1.three(k, input_grad.at[at], input_grad.at[at]).start()
+
+    loop(0, 2, finish1)
+    attn_ring.rs2_step(2)
+    loop(2, PIECES, finish1)
+    attn_ring.rs2_step(3)
+    gains[0] = jnp.concatenate(
+        [
+            jnp.sum(folded[0:8], 0, keepdims=True),
+            jnp.sum(folded[8:16], 0, keepdims=True),
+            jnp.zeros((6, gains.shape[2]), F32),
+        ],
+        0,
+    )
+
+    def swap(i):
+        device = (place.dp, place.buddy) if i == 0 else (place.pairs[i - 1], place.tensor)
+        return pltpu.make_async_remote_copy(
+            gains.at[i], gains_in.at[i], gain_s.at[i], gain_r.at[i],
+            device_id=device, device_id_type=MESH,
+        )
+
+    def add_swap(i):
+        swap(i).wait_recv()
+        gains[i + 1] = gains[i] + gains_in[i]
 
     def finish_out(k):
         done = forward2.total(k) + residual[forward2.own(k)]
@@ -469,71 +640,53 @@
         forward2.land1[at] = done
         forward2.three(k, forward2.land1.at[at], land3.at[at]).start()
 
-    loop(0, PIECES, finish_out)
-    loop(0, PIECES, back1.middle)
-    step(12)
-    hidden_grad = dot_tn(hidden1[...], dqkv[...])
-    for j in range(4):
-        piece = hidden_grad[:, 128 * j : 128 * j + 128].reshape(4, 16, 16, 128)
-        attn[:, :, 16 * j : 16 * j + 16] = piece
-    step(13)
-    step(14)
-    for ring in rings:
-        ring.turn()
-
     def close_out(k):
         at = forward2.local(k)
         forward2.three(k, forward2.land1.at[at], land3.at[at]).wait_recv()
         output[forward2.other(k)] = land3[at].astype(BF16)
 
+    swap(0).start()
+    gather(7)
+    attn_ring.back()
+    add_swap(0)
+    swap(1).start()
+    gather(8)
+    attn_ring.ag2_step(1)
+    add_swap(1)
+    swap(2).start()
+    gather(9)
+    attn_ring.ag2_step(2)
+    add_swap(2)
+    swap(3).start()
+    gather(10)
+    attn_ring.ag2_step(3)
+    add_swap(3)
+    swap(4).start()
+    loop(0, PIECES, finish_out)
+    gather(11)
+    attn_ring.ag1_step(1)
+    add_swap(4)
+    swap(5).start()
+    gather(12)
+    attn_ring.ag1_step(2)
+    add_swap(5)
+    gain_sums[...] = gains[6]
+    gather(13)
     loop(0, PIECES, close_out)
-    for ring in rings:
-        ring.back()
-
-    def finish1(k):
-        d = back1.total(k)
-        at = back1.own(k)
-        scaled, inverse = row_norm(tokens[at].astype(F32))
-        gains[0:8] += fold(d * scaled)
-        input_grad[at] = dresidual[at] + norm_back(d, scaled, inverse, gain1[...])
-        back1.three(k, input_grad.at[at], input_grad.at[at]).start()
-
-    loop(0, PIECES, finish1)
-    swap = pltpu.make_async_remote_copy(
-        gains, gains_in, gain_s, gain_r,
-        device_id=(place.dp, place.buddy), device_id_type=MESH,
-    )
-    swap.start()
-    for ring in rings:
-        ring.ag_step(1)
-    swap.wait_recv()
-    for j in range(16):
-        rows = slice(8 * (j // 8), 8 * (j // 8) + 8)
-        lanes = slice(128 * (j % 8), 128 * (j % 8) + 128)
-        attn[0, j, 96:104] = gains[rows, lanes] + gains_in[rows, lanes]
-    for f in range(4):
-        attn_ring.begin(f)
-
-    def both(s):
-        for ring in rings:
-            ring.ag_step(s)
-        attn_ring.rs_step(s - 1)
-
-    loop(2, 15, both)
-    attn_ring.rs_step(14)
-    attn_ring.turn()
+    gather(14)
+    attn_ring.ag1_step(3)
     for ring in rings:
         ring.end()
-    attn_ring.back()
-    loop(1, 15, attn_ring.ag_step)
-    attn_ring.end()
 
     def drain(s):
-        for ring in rings + [attn_ring]:
+        for ring in rings:
             ring.drain(s)
 
     loop(0, 15, drain)
-    swap.wait_send()
+    loop(0, 3, attn_ring.drain)
+    attn_ring.close()
+    for i in range(6):
+        swap(i).wait_send()
 
     def close(k):
         for work in sums:
@@ -550,37 +703,90 @@
 def back_part(grads, *rest):
     rows, width = rest[0].shape
     half = (rows // 2, width)
-    m, n = grads.shape[3], 104
+    m, n = grads.shape[3], 96
     S = pltpu.VMEM
     ring_sems = [DMA((2, 4, 15))] * 4 + [DMA((2, 4))] * 3
-    attn_sems = [DMA((4, 15))] * 4 + [DMA((4,))] * 3
+    attn_sems = [DMA((4, 3))] * 8 + [DMA((4,))] * 3
+    attn = (4, 4, 4, n, 128)
     return pl.pallas_call(
         back_kernel,
         out_shape=(
             jax.ShapeDtypeStruct((rows, width), BF16),
             jax.ShapeDtypeStruct((rows, width), F32),
+            jax.ShapeDtypeStruct((8, width), F32),
             jax.ShapeDtypeStruct(grads.shape, F32),
-            jax.ShapeDtypeStruct((4, 16, n, 128), F32),
+            jax.ShapeDtypeStruct(attn, F32),
         ),
         in_specs=[ANY] + [VMEM] * len(rest),
-        out_specs=(VMEM, VMEM, ANY, ANY),
+        out_specs=(VMEM, VMEM, VMEM, ANY, ANY),
         scratch_shapes=[
             S(grads.shape, F32), S(grads.shape, F32), S((2, 4, m, 128), F32),
             S((2, 4, m, 128), F32),
-            S((4, 16, n, 128), F32), S((4, 16, n, 128), F32), S((4, n, 128), F32),
+            S(attn, F32), S(attn, F32), S((4, 4, n, 128), F32), S((4, n, 128), F32),
             S((4, n, 128), F32),
             S((3,) + half, F32), S((3,) + half, F32), S(half, F32),
             S((rows, width), F32), S((rows, width), F32), S((rows, 512), BF16),
-            S((16, width), F32), S((16, width), F32),
+            S((16, width), F32), S((7, 8, width), F32), S((6, 8, width), F32),
         ]
         + ring_sems
         + attn_sems
         + [DMA((3, PIECES))] * 6
-        + [DMA((2,)), DMA, DMA],
+        + [DMA((2,)), DMA((6,)), DMA((6,))],
         compiler_params=pltpu.CompilerParams(
             collective_id=2, has_side_effects=True, vmem_limit_bytes=63 << 20
         ),
     )(grads, *rest)
+
+
+def unpack_kernel(grads, attn, gains, gate, up, down, query, key, value, out, gain1, gain2):
+    gate[0] = grads[0, :, 0:64].reshape(1024, 128)
+    up[0] = grads[0, :, 64:128].reshape(1024, 128)
+    for j in range(8):
+        lanes = slice(128 * j, 128 * j + 128)
+        for half in range(2):
+            down[0, 64 * half : 64 * half + 64, lanes] = grads[0, 2 * j + half, 128:192]
+    query[:, 0:128] = attn[:, 0:16].reshape(128, 128)
+    query[:, 128:256] = attn[:, 16:32].reshape(128, 128)
+    key[...] = attn[:, 32:48].reshape(128, 128)
+    value[...] = attn[:, 48:64].reshape(128, 128)
+    out[...] = attn[:, 64:96].reshape(256, 128)
+    gain1[...] = gains[0:1]
+    gain2[...] = gains[1:2]
+
+
+def unpack(grads, attn, gains):
+    return pl.pallas_call(
+        unpack_kernel,
+        grid=(8,),
+        out_shape=(
+            jax.ShapeDtypeStruct((8, 1024, 128), F32),
+            jax.ShapeDtypeStruct((8, 1024, 128), F32),
+            jax.ShapeDtypeStruct((8, 128, 1024), F32),
+            jax.ShapeDtypeStruct((1024, 256), F32),
+            jax.ShapeDtypeStruct((1024, 128), F32),
+            jax.ShapeDtypeStruct((1024, 128), F32),
+            jax.ShapeDtypeStruct((256, 1024), F32),
+            jax.ShapeDtypeStruct((1, 1024), F32),
+            jax.ShapeDtypeStruct((1, 1024), F32),
+        ),
+        in_specs=[
+            pl.BlockSpec((1, 16, 192, 128), lambda p: (p, 0, 0, 0)),
+            pl.BlockSpec((8, 96, 128), lambda p: (p, 0, 0)),
+            pl.BlockSpec((8, 128), lambda p: (0, p)),
+        ],
+        out_specs=(
+            pl.BlockSpec((1, 1024, 128), lambda p: (p, 0, 0)),
+            pl.BlockSpec((1, 1024, 128), lambda p: (p, 0, 0)),
+            pl.BlockSpec((1, 128, 1024), lambda p: (p, 0, 0)),
+            pl.BlockSpec((128, 256), lambda p: (p, 0)),
+            pl.BlockSpec((128, 128), lambda p: (p, 0)),
+            pl.BlockSpec((128, 128), lambda p: (p, 0)),
+            pl.BlockSpec((256, 128), lambda p: (0, p)),
+            pl.BlockSpec((1, 128), lambda p: (0, p)),
+            pl.BlockSpec((1, 128), lambda p: (0, p)),
+        ),
+        compiler_params=pltpu.CompilerParams(vmem_limit_bytes=32 << 20),
+    )(grads, attn, gains)
 
 
 def tables(seq_count, seq_length, head_width):
@@ -668,7 +874,7 @@
     expert_grads, dhidden2, out_part = experts_part(
         hidden2, cotangent, expert_gate, expert_up, expert_down, expert_share
     )
-    output, input_grad, grads, attn = back_part(
+    output, input_grad, gains, grads, attn = back_part(
         expert_grads.reshape(2, 4, 16, 192, 128),
         dhidden2,
         out_part,
@@ -692,29 +898,19 @@
         w_key,
         w_value,
     )
-    grads = grads.reshape(experts, 16, 192, 128)
-    gate_grad = grads[:, :, 0:64].reshape(experts, -1, 128)
-    up_grad = grads[:, :, 64:128].reshape(experts, -1, 128)
-    down_grad = grads[:, :, 128:192].reshape(experts, 8, 128, 128)
-    down_grad = down_grad.transpose(0, 2, 1, 3).reshape(experts, 128, -1)
-    attn = attn.reshape(64, 104, 128)
-    query_grad = jnp.concatenate(
-        [attn[:, 0:16].reshape(-1, 128), attn[:, 16:32].reshape(-1, 128)], 1
-    )
-    key_grad = attn[:, 32:48].reshape(-1, 128)
-    value_grad = attn[:, 48:64].reshape(-1, 128)
-    out_grad = attn[:, 64:96].reshape(8, 256, 128).transpose(1, 0, 2).reshape(256, -1)
-    gain1_grad = jnp.sum(attn[0:8, 96:104], 1).reshape(-1)
-    gain2_grad = jnp.sum(attn[8:16, 96:104], 1).reshape(-1)
+    (
+        gate_grad, up_grad, down_grad, query_grad, key_grad, value_grad, out_grad, gain1_grad,
+        gain2_grad,
+    ) = unpack(grads.reshape(experts, 16, 192, 128), attn.reshape(64, 96, 128), gains)
     return (
         output,
         input_grad,
-        gain1_grad,
+        gain1_grad.reshape(-1),
         query_grad,
         key_grad,
         value_grad,
         out_grad,
-        gain2_grad,
+        gain2_grad.reshape(-1),
         gate_grad,
         up_grad,
         down_grad,

time: 361 us -> 292 us (0.81)
  Pallas kernels: 307 us -> 259 us
  local copies, waits for them, and re-layouts: 38.8 us -> 20.9 us
    pallas_call x1, Pallas kernels: 261 us -> 208 us  [back_part(): pl.pallas_call(back_kernel, out_shape=(jax.ShapeDtypeStruct((rows, width)...]
    slice x3 -> x0, local copies, waits for them, and re-layouts: 14.3 us -> none  [the longest x1 10.4 us: local(): down_grad = grads[:, :, 128:192].reshape(experts, 8, 128, 128)]
    reshape x3 -> x0, local copies, waits for them, and re-layouts: 9.99 us -> none  [the longest x1 5.06 us: local(): down_grad = down_grad.transpose(0, 2, 1, 3).reshape(experts, 128, -1)]
    unnamed x31 -> x40, local copies, waits for them, and re-layouts: 6.14 us -> 13.2 us
    pallas_call x0 -> x1, Pallas kernels: none -> 6.24 us  [unpack(): pl.pallas_call(unpack_kernel, grid=(8,), out_shape=(jax.ShapeDtypeStruct(...]
where the time goes in v3:
time: 292 us
  Pallas kernels  259 us (89%)
  local copies, waits for them, and re-layouts  20.9 us (7%)
  other arithmetic  6.31 us (2%)
  matrix products  4.11 us (1%)
    pallas_call x1, Pallas kernels, back_part(): pl.pallas_call(back_kernel, out_shape=(jax.ShapeDtypeStruct((rows, width)...  208 us
    pallas_call x1, Pallas kernels, sum4(): pl.pallas_call(sum4_kernel, out_shape=jax.ShapeDtypeStruct(part.shape, F3...  28.4 us
    pallas_call x1, Pallas kernels, experts_part(): pl.pallas_call(expert_kernel, grid=(count // 2,), out_shape=(jax.ShapeDty...  17.1 us
    unnamed x40, local copies, waits for them, and re-layouts  13.2 us
    pallas_call x1, Pallas kernels, unpack(): pl.pallas_call(unpack_kernel, grid=(8,), out_shape=(jax.ShapeDtypeStruct(...  6.24 us

profile of v3, /device:TPU:0, one launch (start us, length us, event | category | flops | bytes accessed | tf_op | source)
XLA Modules:
  0.0 291.7 jit_solution(5508263848273335236)
XLA Ops:
  0.6 0.0 copy-start.7
  0.7 0.0 copy-start.16
  0.7 0.0 copy-start.12
  0.7 0.0 copy-start.17
  0.7 1.6 fusion.2
  2.3 0.7 select_reduce_fusion
  3.1 0.3 fusion.16
  3.4 0.0 copy-start.13
  3.4 0.8 copy.60.sin_table
  4.3 1.7 fusion.10
  6.0 0.8 copy.59.cos_table
  6.8 0.0 copy-done.16
  6.8 0.9 copy.58.seg_col
  7.7 0.0 copy-done.7
  7.7 0.0 copy-done.17
  7.7 0.0 copy-start.9
  7.7 0.3 fusion.4.hidden1
  8.0 0.0 copy-done.12
  8.0 0.0 copy-start.5
  8.0 0.4 convolution_convert_fusion.values
  8.4 0.0 copy-start.11
  8.4 0.1 copy.52
  8.6 0.0 copy-done.13
  8.6 0.5 fusion.20
  9.1 0.8 copy.57.keys
  9.9 0.0 copy-done.9
  9.9 0.0 copy-start.14
  9.9 0.5 fusion.21
  10.4 0.0 copy-done.5
  10.4 0.1 subtract_convert_fusion
  10.5 0.0 copy-done.11
  10.5 0.8 copy.56.queries
  11.4 2.0 copy.54.share
  13.3 0.0 copy-done.14
  13.3 0.9 fusion.1
  14.2 0.9 fusion
  15.1 0.0 copy-start.10
  15.2 1.4 fusion.7
  16.6 0.6 add.40.lse
  17.2 0.8 copy.55.mixed
  18.0 0.0 copy-done.10
  18.0 0.5 fusion.22.part
  18.5 28.4 %shard_map.221 = f32[512,1024]{1,0:T(8,128)S(1)} custom-call(f32[512,1024]{1,0:T(8,128)S(1)} %fusion.22.part), custom_call_target="tpu_custom_call" | custom-call | tf_op jit(solution)/shard_map/pallas_call | solution.py:361
  46.9 0.0 copy-start.18
  46.9 0.0 copy-start.1
  46.9 0.3 multiply_reduce_fusion
  47.3 0.0 copy-start.6
  47.3 1.3 copy-done.6
  48.6 0.0 copy-done.18
  48.6 0.2 multiply_convert_fusion.hidden2
  48.8 0.0 copy-done.1
  48.8 17.1 %shard_map.222 = (f32[8,16,192,128]{3,2,1,0:T(8,128)}, f32[512,1024]{1,0:T(8,128)S(1)}, f32[512,1024]{1,0:T(8,128)}) custom-call(bf16[512,1024]{1,0:T(8,128)(2,1)S(1)} %multiply_convert_fusion.hidden2, bf16[512,1024]{1,0:T(8,128)(2,1)S(1)} %copy-done.1, bf16[8,1024,128]{2,1,0:T(8,128)(2,1)} %w_gate.1, bf16[8,1024,128]{2,1,0:T(8,128)(2,1)} %w_up.1, ...), custom_call_target="tpu_custom_call" | custom-call | tf_op jit(solution)/shard_map/pallas_call | solution.py:417
  65.9 1.3 copy-done.3
  67.3 207.6 %shard_map.223 = (bf16[512,1024]{1,0:T(8,128)(2,1)}, f32[512,1024]{1,0:T(8,128)}, f32[8,1024]{1,0:T(8,128)}, f32[2,4,16,192,128]{4,3,2,1,0:T(8,128)}, f32[4,4,4,96,128]{4,3,2,1,0:T(8,128)}) custom-call(f32[2,4,16,192,128]{4,3,2,1,0:T(8,128)} %bitcast.68, f32[512,1024]{1,0:T(8,128)} %copy-done.3, f32[512,1024]{1,0:T(8,128)} %get-tuple-element.30.out_part, ...), custom_call_target="tpu_custom_call" | custom-call | tf_op jit(solution)/shard_map/pallas_call | solution.py:711
  274.9 0.0 copy-start
  274.9 4.6 %copy-done = f32[2,4,16,192,128]{4,3,2,1,0:T(8,128)S(1)} copy-done((f32[2,4,16,192,128]{4,3,2,1,0:T(8,128)S(1)}, f32[2,4,16,192,128]{4,3,2,1,0:T(8,128)}, u32[]{:S(2)}) %copy-start) | copy-done | bytes 12582936
  279.5 1.9 copy-done.2
  281.4 0.8 copy-done.4
  282.1 6.2 %shard_map.224 = (f32[8,1024,128]{2,1,0:T(8,128)}, f32[8,1024,128]{2,1,0:T(8,128)}, f32[8,128,1024]{2,1,0:T(8,128)}, f32[1024,256]{1,0:T(8,128)}, f32[1024,128]{...) custom-call(f32[8,16,192,128]{3,2,1,0:T(8,128)S(1)} %bitcast.66, ...), custom_call_target="tpu_custom_call" | custom-call | tf_op jit(solution)/shard_map/pallas_call | solution.py:758
  288.4 0.0 copy-start.8
  288.4 0.0 copy-done.15
  288.4 1.0 copy.67
  289.4 1.0 copy-done.8
  290.4 1.3 copy.68
  (15 shorter events, 0.2 us)
Async XLA Ops:
  0.6 7.0 %copy-start.7 = (bf16[512,1024]{1,0:T(8,128)(2,1)S(1)}, bf16[512,1024]{1,0:T(8,128)(2,1)}, u32[]{:S(2)}) copy-start(bf16[512,1024]{1,0:T(8,128)(2,1)} %tokens.1) | copy-start | bytes 3145732
  0.7 6.1 %copy-start.16 = (s32[1,512]{1,0:T(1,128)S(1)}, s32[1,512]{1,0:T(1,128)}, u32[]{:S(2)}) copy-start(s32[1,512]{1,0:T(1,128)} %seg_row.1) | copy-start | bytes 6148
  0.7 7.3 %copy-start.12 = (bf16[1024,128]{1,0:T(8,128)(2,1)S(1)}, bf16[1024,128]{1,0:T(8,128)(2,1)}, u32[]{:S(2)}) copy-start(bf16[1024,128]{1,0:T(8,128)(2,1)} %w_value.1) | copy-start | bytes 786436
  0.7 7.0 %copy-start.17 = (f32[1024]{0:T(1024)S(1)}, f32[1024]{0:T(1024)}, u32[]{:S(2)}) copy-start(f32[1024]{0:T(1024)} %param.15) | copy-start | bytes 12292
  3.4 5.2 %copy-start.13 = (bf16[1024,128]{1,0:T(8,128)(2,1)S(1)}, bf16[1024,128]{1,0:T(8,128)(2,1)}, u32[]{:S(2)}) copy-start(bf16[1024,128]{1,0:T(8,128)(2,1)} %w_key.1) | copy-start | bytes 786436
  7.7 2.2 copy-start.9
  8.0 2.4 copy-start.5
  8.4 2.1 copy-start.11
  9.9 3.4 %copy-start.14 = (pred[512,512]{0,1:T(8,128)(4,1)S(1)}, pred[512,512]{0,1:T(8,128)(4,1)}, u32[]{:S(2)}) copy-start(pred[512,512]{0,1:T(8,128)(4,1)} %fusion.10) | copy-start | bytes 786436
  15.1 2.9 copy-start.10
  46.9 1.7 copy-start.18
  46.9 1.9 copy-start.1
  47.3 1.3 copy-start.6
  65.9 1.3 copy-start.3
  274.9 4.6 %copy-start = (f32[2,4,16,192,128]{4,3,2,1,0:T(8,128)S(1)}, f32[2,4,16,192,128]{4,3,2,1,0:T(8,128)}, u32[]{:S(2)}) copy-start(f32[2,4,16,192,128]{4,3,2,1,0:T(8,128)} %get-tuple-element.33) | copy-start | bytes 37748740
  279.5 1.9 copy-start.2
  281.4 0.8 copy-start.4
  282.1 6.3 %copy-start.15 = (bf16[512,1024]{1,0:T(8,128)(2,1)S(1)}, bf16[512,1024]{1,0:T(8,128)(2,1)}, u32[]{:S(2)}) copy-start(bf16[512,1024]{1,0:T(8,128)(2,1)} %get-tuple-element.67) | copy-start | bytes 3145732
  288.4 2.0 copy-start.8

commit v4 on v3

--- a/solution.py
+++ b/solution.py
@@ -2,6 +2,7 @@
 
 import jax
 import jax.numpy as jnp
+import numpy as np
 from jax import lax
 from jax.experimental import pallas as pl
 from jax.experimental.pallas import tpu as pltpu
@@ -208,6 +209,8 @@
     def rs1_step(self, s):
         for f in range(4):
             self.rs1(f, s - 1, self.land).wait_recv()
+            if s == 1:
+                self.rs1(f, 0, self.mine).wait_send()
             i = self.spots(f, 1 + s, 0)[0]
             self.land[f, i] = self.land[f, i] + self.mine[f, i]
             if s < 3:
@@ -251,7 +254,8 @@
 
     def drain(self, s):
         for f in range(4):
-            self.rs1(f, s, self.land).wait_send()
+            if s > 0:
+                self.rs1(f, s, self.land).wait_send()
             self.rs2(f, s, self.land2.at[f]).wait_send()
             self.ag2(f, s, self.total.at[f]).wait_send()
             self.ag1(f, s, self.out.at[f, 0]).wait_send()
@@ -272,7 +276,7 @@
         return pl.ds(pl.multiple_of(k * self.n, self.n), self.n)
 
     def rows(self, k, core):
-        return pl.ds(pl.multiple_of(core * self.half + k * self.n, self.n), self.n)
+        return pl.ds(pl.multiple_of((2 * k + core) * self.n, self.n), self.n)
 
     def own(self, k):
         return self.rows(k, self.place.core)
@@ -336,42 +340,152 @@
     lax.fori_loop(low, high, one, 0)
 
 
-def sum4_kernel(part, out, land1, land2, *sems):
+def swap_halves(values):
+    lane = lax.broadcasted_iota(jnp.int32, values.shape, 1)
+    return jnp.where(lane % 64 < 32, pltpu.roll(values, 96, 1), pltpu.roll(values, 32, 1))
+
+
+def allowed_pairs(seg_col, seg_row, until, block):
+    shape = (until, 256)
+    return (seg_col[:until] == seg_row[:, 256 * block : 256 * block + 256]) & (
+        lax.broadcasted_iota(jnp.int32, shape, 0)
+        <= lax.broadcasted_iota(jnp.int32, shape, 1) + 256 * block
+    )
+
+
+def front_kernel(
+    *refs
+):
+    given, refs = refs[:12], refs[12:]
+    kept, refs = refs[:9], refs[9:]
+    inside, refs = refs[:12], refs[12:]
+    made, refs = refs[:9], refs[9:]
+    part, land1, land2, in_sem, out_sem = refs[:5]
+    (
+        tokens, gain1, cos_table, sin_table, w_query, w_key, w_value, seg_row, w_out, gain2,
+        routes, route_weights,
+    ) = inside
+    hidden1, queries, keys, values, lse, mixed, residual, hidden2, side = made
+    loads = [
+        pltpu.make_async_copy(src, dst, in_sem.at[i])
+        for i, (src, dst) in enumerate(zip(given, inside))
+    ]
+    stores = [
+        pltpu.make_async_copy(src, dst, out_sem.at[i])
+        for i, (src, dst) in enumerate(zip(made, kept))
+    ]
+    for load in loads:
+        load.start()
     place = Place()
     greet(place, False)
-    work = Sum4(place, part, land1, land2, sems)
-    work.begin()
-    loop(0, PIECES, work.middle)
+    work = Sum4(place, part, land1, land2, refs[5:])
+    for load in loads:
+        load.wait()
+    rows = [
+        jnp.sum(
+            jnp.where(routes[...] == e, route_weights[...], 0.0), 0, keepdims=True
+        )
+        for e in range(8)
+    ]
+    rows.append(seg_row[...].astype(F32))
+    rows.append(jnp.zeros((119, 512), F32))
+    side[...] = jnp.concatenate(rows, 0).T
+    stores[8].start()
+    seg_col = side[:, 8:9].astype(jnp.int32)
+    for b in range(2):
+        at = slice(256 * b, 256 * b + 256)
+        until = 256 * b + 256
+
+        def rotate(projected):
+            turned = projected * cos_table[at] - swap_halves(projected) * sin_table[at]
+            return turned.astype(BF16)
+
+        normed = (row_norm(tokens[at].astype(F32))[0] * gain1[...]).astype(BF16)
+        hidden1[at] = normed
+        projected = dot_nn(normed, w_query[...])
+        for g in range(2):
+            queries[at, 128 * g : 128 * g + 128] = rotate(projected[:, 128 * g : 128 * g + 128])
+        keys[at] = rotate(dot_nn(normed, w_key[...]))
+        values[at] = dot_nn(normed, w_value[...]).astype(BF16)
+        if b == 1:
+            work.middle(0)
+            work.middle(1)
+        allowed = allowed_pairs(seg_col, seg_row, until, b)
+        heads = []
+        for h in range(4):
+            own = slice(64 * (h // 2), 64 * (h // 2) + 64)
+            raw = dot_nt(keys[:until, own], queries[at, 64 * h : 64 * h + 64]) * HD ** (-0.5)
+            scores = jnp.where(allowed, raw, -1e30)
+            top = jnp.max(scores, 0, keepdims=True)
+            weights = jnp.exp(scores - top)
+            row_total = jnp.sum(weights, 0, keepdims=True)
+            lse[h : h + 1, at] = top + jnp.log(row_total)
+            heads.append(dot_tn((weights / row_total).astype(BF16), values[:until, own]))
+        mixed[at] = jnp.concatenate(heads, 1).astype(BF16)
+        part[at] = dot_nn(mixed[at], w_out[...])
+        work.one(2 * b).start()
+        work.one(2 * b + 1).start()
+    work.middle(2)
+    work.middle(3)
+    for store in stores[:6]:
+        store.start()
+
+    def give(rows):
+        hidden2[rows] = (row_norm(residual[rows])[0] * gain2[...]).astype(BF16)
 
     def finish(k):
-        out[work.own(k)] = work.total(k)
-        work.three(k, out.at[work.own(k)], out.at[work.own(k)]).start()
+        at = work.own(k)
+        residual[at] = tokens[at].astype(F32) + work.total(k)
+        work.three(k, residual.at[at], residual.at[at]).start()
+        give(at)
 
     loop(0, PIECES, finish)
 
     def close(k):
-        work.three(k, out.at[work.own(k)], out.at[work.own(k)]).wait()
+        at = work.own(k)
+        work.three(k, residual.at[at], residual.at[at]).wait()
+        give(work.other(k))
         work.one(k).wait_send()
 
     loop(0, PIECES, close)
-
-
-def sum4(part):
-    half = (part.shape[0] // 2, part.shape[1])
+    for store in stores[6:8]:
+        store.start()
+    for store in stores:
+        store.wait()
+
+
+def front_part(*given):
+    rows, width = given[0].shape
+    half = (rows // 2, width)
+    made = (
+        jax.ShapeDtypeStruct((rows, width), BF16),
+        jax.ShapeDtypeStruct((rows, 256), BF16),
+        jax.ShapeDtypeStruct((rows, 128), BF16),
+        jax.ShapeDtypeStruct((rows, 128), BF16),
+        jax.ShapeDtypeStruct((8, rows), F32),
+        jax.ShapeDtypeStruct((rows, 256), BF16),
+        jax.ShapeDtypeStruct((rows, width), F32),
+        jax.ShapeDtypeStruct((rows, width), BF16),
+        jax.ShapeDtypeStruct((rows, 128), F32),
+    )
     return pl.pallas_call(
-        sum4_kernel,
-        out_shape=jax.ShapeDtypeStruct(part.shape, F32),
-        in_specs=[VMEM],
-        out_specs=VMEM,
-        scratch_shapes=[pltpu.VMEM(half, F32)] * 2 + [DMA((PIECES,))] * 6,
+        front_kernel,
+        out_shape=made,
+        in_specs=[ANY] * len(given),
+        out_specs=(ANY,) * len(made),
+        scratch_shapes=[pltpu.VMEM(a.shape, a.dtype) for a in given + made]
+        + [pltpu.VMEM((rows, width), F32)]
+        + [pltpu.VMEM(half, F32)] * 2
+        + [DMA((len(given),)), DMA((len(made),))]
+        + [DMA((PIECES,))] * 6,
         compiler_params=pltpu.CompilerParams(
-            collective_id=1, has_side_effects=True, vmem_limit_bytes=32 << 20
+            collective_id=1, has_side_effects=True, vmem_limit_bytes=60 << 20
         ),
-    )(part)
+    )(*given)
 
 
 def expert_kernel(
-    hidden2, dy, w_gate, w_up, w_down, share, grads, dhidden2, out, hidden2_t
+    hidden2, dy, w_gate, w_up, w_down, side, grads, dhidden2, out, hidden2_t
 ):
     step = pl.program_id(0)
 
@@ -390,7 +504,9 @@
         gate, up = both[:, :128], both[:, 128:]
         sig = 1.0 / (1.0 + jnp.exp(-gate))
         silu = gate * sig
-        weight = share[i]
+        lane = lax.broadcasted_iota(jnp.int32, side.shape, 1)
+        chosen = jnp.where(lane == 2 * step + i, side[...], 0.0)
+        weight = jnp.sum(chosen, 1, keepdims=True)
         acts.append((silu * up * weight).astype(BF16))
         dact = dact_pair[:, 128 * i : 128 * i + 128] * weight
         dgate = (dact * up * (sig * (1.0 + gate * (1.0 - sig)))).astype(BF16)
@@ -410,7 +526,7 @@
                 grads[i, 2 * j + half, 128:192] = down_grad[at : at + 64, 128 * j : 128 * j + 128]
 
 
-def experts_part(hidden2, dy, w_gate, w_up, w_down, share):
+def experts_part(hidden2, dy, w_gate, w_up, w_down, side):
     rows, width = hidden2.shape
     count = w_gate.shape[0]
     whole = pl.BlockSpec((rows, width), lambda p: (0, 0))
@@ -428,7 +544,7 @@
             pl.BlockSpec((2, width, 128), lambda p: (p, 0, 0)),
             pl.BlockSpec((2, width, 128), lambda p: (p, 0, 0)),
             pl.BlockSpec((2, 128, width), lambda p: (p, 0, 0)),
-            pl.BlockSpec((2, rows, 1), lambda p: (p, 0, 0)),
+            pl.BlockSpec(side.shape, lambda p: (0, 0)),
         ],
         out_specs=(
             pl.BlockSpec((2, 16, 192, 128), lambda p: (p, 0, 0, 0)),
@@ -437,7 +553,7 @@
         ),
         scratch_shapes=[pltpu.VMEM((width, rows), BF16)],
         compiler_params=pltpu.CompilerParams(vmem_limit_bytes=48 << 20),
-    )(hidden2, dy, w_gate, w_up, w_down, share)
+    )(hidden2, dy, w_gate, w_up, w_down, side)
 
 
 def row_norm(values):
@@ -457,10 +573,10 @@
 
 def back_kernel(
     grads, dhidden2, out_part, residual, tokens, dy, gain1, gain2, mixed, w_out, queries, keys,
-    values, lse, seg_col, seg_row, cos_table, sin_table, hidden1, w_query, w_key, w_value,
-    output, input_grad, gain_sums, grads_sum, attn_sum,
-    mine, land, zland, total, attn, attn_land, attn_land2, attn_zland, attn_total,
-    land1, land2, land3, dresidual, dhidden1, dqkv, folded, gains, gains_in, *sems
+    values, lse, side, seg_row, cos_table, sin_table, hidden1, w_query, w_key, w_value,
+    output, input_grad, gain_sums, mine, attn,
+    land, zland, total, attn_land, attn_land2, attn_zland, attn_total,
+    land1, land2, dresidual, dhidden1, dqkv, folded, gains, gains_in, *sems
 ):
     place = Place()
     greet(place, True)
@@ -471,18 +587,19 @@
     rings = [
         Ring(
             place, grads.at[u], mine.at[u], land.at[u], zland.at[u], total.at[u],
-            grads_sum.at[u], [sem.at[u] for sem in ring_sems],
+            mine.at[u], [sem.at[u] for sem in ring_sems],
         )
         for u in range(2)
     ]
     attn_ring = AxisRing(
-        place, attn, attn_land, attn_land2, attn_zland, attn_total, attn_sum, attn_sems
+        place, attn, attn_land, attn_land2, attn_zland, attn_total, attn, attn_sems
     )
     sums = [
         Sum4(place, part, land1.at[i], land2.at[i], [sem.at[i] for sem in sum_sems])
         for i, part in enumerate((dhidden2, out_part, dhidden1))
     ]
     back2, forward2, back1 = sums
+    land3 = back2.land1
 
     back2.begin()
     for ring in rings:
@@ -492,6 +609,7 @@
     for load in loads:
         load.start()
     folded[...] = jnp.zeros_like(folded)
+    seg_col = side[:, 8:9].astype(jnp.int32)
 
     def step(s):
         for ring in rings:
@@ -507,7 +625,6 @@
     step(1)
 
     def finish2(k):
-        step(2 + k)
         d = back2.total(k)
         at = back2.own(k)
         scaled, inverse = row_norm(residual[at])
@@ -515,13 +632,23 @@
         dresidual[at] = dy[at].astype(F32) + norm_back(d, scaled, inverse, gain2[...])
         back2.three(k, dresidual.at[at], dresidual.at[at]).start()
 
-    loop(0, PIECES, finish2)
+    step(2)
+    finish2(0)
+    step(3)
+    finish2(1)
+    step(4)
+    step(5)
+    finish2(2)
+    step(6)
+    finish2(3)
+    step(7)
 
     def close2(k):
         at = back2.own(k)
         back2.three(k, dresidual.at[at], dresidual.at[at]).wait_recv()
 
     loop(0, PIECES, close2)
+    forward2.begin()
 
     dbranch = dresidual[...].astype(BF16)
     dmixed = dot_nt(dbranch, w_out[...]).astype(BF16)
@@ -530,12 +657,11 @@
         piece = out_grad[:, 128 * j : 128 * j + 128].reshape(2, 4, 32, 128)
         attn[j // 2, 2 * (j % 2) : 2 * (j % 2) + 2, :, 64:96] = piece
 
-    lane = lax.broadcasted_iota(jnp.int32, (512, 128), 1)
-    first_half = lane % 64 < 32
+    step(8)
+    loop(0, PIECES, forward2.middle)
 
     def unrotate(grad):
-        swapped = jnp.where(first_half, pltpu.roll(grad, 96, 1), pltpu.roll(grad, 32, 1))
-        return (grad * cos_table[...] + swapped * sin_table[...]).astype(BF16)
+        return (grad * cos_table[...] + swap_halves(grad) * sin_table[...]).astype(BF16)
 
     dkeys, dvalues = [], []
     for g in range(2):
@@ -552,10 +678,7 @@
                 query = queries[at, 64 * h : 64 * h + 64]
                 dmix = dmixed[at, 64 * h : 64 * h + 64]
                 raw = dot_nt(key[:until], query) * HD ** (-0.5)
-                allowed = (seg_col[:until] == seg_row[:, at]) & (
-                    lax.broadcasted_iota(jnp.int32, raw.shape, 0)
-                    <= lax.broadcasted_iota(jnp.int32, raw.shape, 1) + 256 * b
-                )
+                allowed = allowed_pairs(seg_col, seg_row, until, b)
                 probs = jnp.exp(jnp.where(allowed, raw, -1e30) - lse[h : h + 1, at])
                 dprobs = dot_nt(value[:until], dmix)
                 inner = jnp.sum(probs * dprobs, 0, keepdims=True)
@@ -566,7 +689,8 @@
                     dvalue[t] = dvalue[t] + dvalue_part[256 * t : 256 * t + 256]
                     dkey[t] = dkey[t] + dkey_part[256 * t : 256 * t + 256]
                 blocks.append(dot_tn(dscores, key[:until]))
-                step(6 + 2 * h + b)
+                if 2 * h + b < 6:
+                    step(9 + 2 * h + b)
             dquery.append(jnp.concatenate(blocks, 0) * HD ** (-0.5))
         dqkv[:, 128 * g : 128 * g + 128] = unrotate(jnp.concatenate(dquery, 1))
         dkeys.append(jnp.concatenate(dkey, 0) * HD ** (-0.5))
@@ -579,7 +703,6 @@
         piece = hidden_grad[:, 128 * j : 128 * j + 128].reshape(4, 4, 4, 16, 128)
         attn[:, :, :, 16 * j : 16 * j + 16] = piece
     attn_ring.begin()
-    step(14)
     for ring in rings:
         ring.turn()
     dhidden1[...] = (
@@ -589,12 +712,10 @@
     )
     back1.begin()
     attn_ring.rs1_step(1)
-    loop(0, PIECES, back1.middle)
-    forward2.begin()
     attn_ring.rs1_step(2)
     for ring in rings:
         ring.back()
-    loop(0, PIECES, forward2.middle)
+    loop(0, PIECES, back1.middle)
     gather(1)
     attn_ring.rs1_step(3)
     gather(2)
@@ -683,7 +804,8 @@
             ring.drain(s)
 
     loop(0, 15, drain)
-    loop(0, 3, attn_ring.drain)
+    for s in range(3):
+        attn_ring.drain(s)
     attn_ring.close()
     for i in range(6):
         swap(i).wait_send()
@@ -718,13 +840,13 @@
             jax.ShapeDtypeStruct(attn, F32),
         ),
         in_specs=[ANY] + [VMEM] * len(rest),
-        out_specs=(VMEM, VMEM, VMEM, ANY, ANY),
+        out_specs=(VMEM,) * 5,
         scratch_shapes=[
-            S(grads.shape, F32), S(grads.shape, F32), S((2, 4, m, 128), F32),
+            S(grads.shape, F32), S((2, 4, m, 128), F32),
             S((2, 4, m, 128), F32),
-            S(attn, F32), S(attn, F32), S((4, 4, n, 128), F32), S((4, n, 128), F32),
+            S(attn, F32), S((4, 4, n, 128), F32), S((4, n, 128), F32),
             S((4, n, 128), F32),
-            S((3,) + half, F32), S((3,) + half, F32), S(half, F32),
+            S((3,) + half, F32), S((3,) + half, F32),
             S((rows, width), F32), S((rows, width), F32), S((rows, 512), BF16),
             S((16, width), F32), S((7, 8, width), F32), S((6, 8, width), F32),
         ]
@@ -738,7 +860,10 @@
     )(grads, *rest)
 
 
-def unpack_kernel(grads, attn, gains, gate, up, down, query, key, value, out, gain1, gain2):
+def unpack_kernel(
+    grads, attn, gains, forward, backward, gate, up, down, query, key, value, out, gain1, gain2,
+    output, input_grad
+):
     gate[0] = grads[0, :, 0:64].reshape(1024, 128)
     up[0] = grads[0, :, 64:128].reshape(1024, 128)
     for j in range(8):
@@ -752,9 +877,11 @@
     out[...] = attn[:, 64:96].reshape(256, 128)
     gain1[...] = gains[0:1]
     gain2[...] = gains[1:2]
-
-
-def unpack(grads, attn, gains):
+    output[...] = forward[...]
+    input_grad[...] = backward[...]
+
+
+def unpack(grads, attn, gains, forward, backward):
     return pl.pallas_call(
         unpack_kernel,
         grid=(8,),
@@ -768,11 +895,15 @@
             jax.ShapeDtypeStruct((256, 1024), F32),
             jax.ShapeDtypeStruct((1, 1024), F32),
             jax.ShapeDtypeStruct((1, 1024), F32),
+            jax.ShapeDtypeStruct(forward.shape, BF16),
+            jax.ShapeDtypeStruct(backward.shape, F32),
         ),
         in_specs=[
             pl.BlockSpec((1, 16, 192, 128), lambda p: (p, 0, 0, 0)),
             pl.BlockSpec((8, 96, 128), lambda p: (p, 0, 0)),
             pl.BlockSpec((8, 128), lambda p: (0, p)),
+            pl.BlockSpec((64, 1024), lambda p: (p, 0)),
+            pl.BlockSpec((64, 1024), lambda p: (p, 0)),
         ],
         out_specs=(
             pl.BlockSpec((1, 1024, 128), lambda p: (p, 0, 0)),
@@ -784,29 +915,22 @@
             pl.BlockSpec((256, 128), lambda p: (0, p)),
             pl.BlockSpec((1, 128), lambda p: (0, p)),
             pl.BlockSpec((1, 128), lambda p: (0, p)),
+            pl.BlockSpec((64, 1024), lambda p: (p, 0)),
+            pl.BlockSpec((64, 1024), lambda p: (p, 0)),
         ),
-        compiler_params=pltpu.CompilerParams(vmem_limit_bytes=32 << 20),
-    )(grads, attn, gains)
-
-
-def tables(seq_count, seq_length, head_width):
-    half_width = head_width // 2
-    frequency = ROPE_THETA ** (-jnp.arange(half_width, dtype=jnp.float32) * 2.0 / head_width)
-    position = jnp.tile(jnp.arange(seq_length), seq_count).astype(jnp.float32)
-    angles = position[:, None] * frequency[None, :]
-    return (jnp.cos(angles), jnp.sin(angles))
-
-
-def rotate(values, cos_table, sin_table):
-    half_width = values.shape[-1] // 2
-    first_half = values[..., :half_width]
-    second_half = values[..., half_width:]
-    return jnp.concatenate(
-        [
-            first_half * cos_table - second_half * sin_table,
-            second_half * cos_table + first_half * sin_table,
-        ],
-        -1,
+        compiler_params=pltpu.CompilerParams(vmem_limit_bytes=62 << 20),
+    )(grads, attn, gains, forward, backward)
+
+
+def tables(seq_length):
+    half_width = HD // 2
+    exponent = -np.arange(half_width, dtype=np.float32) * np.float32(2.0) / np.float32(HD)
+    frequency = np.power(np.float32(ROPE_THETA), exponent)
+    angles = np.arange(seq_length, dtype=np.float32)[:, None] * frequency[None, :]
+    cosine, sine = np.cos(angles), np.sin(angles)
+    return (
+        jnp.asarray(np.concatenate([cosine] * 4, 1)),
+        jnp.asarray(np.concatenate([sine, -sine] * 2, 1)),
     )
 
 
@@ -826,82 +950,27 @@
     segments,
     cotangent,
 ):
-    seq_count, seq_length = segments.shape
-    tok_rows = tokens.shape[0]
-    head_count = w_query.shape[1] // HD
-    groups = w_key.shape[1] // HD
-    group_size = head_count // groups
     experts = expert_gate.shape[0]
-    cos_half, sin_half = tables(seq_count, seq_length, HD)
-    cos_table, sin_table = cos_half[:, None, :], sin_half[:, None, :]
-    inputs = tokens.astype(F32)
-    scaled1, inverse1 = row_norm(inputs)
-    hidden1 = (scaled1 * norm1_gain).astype(BF16)
-    queries = rotate(
-        dot_nn(hidden1, w_query).reshape(tok_rows, head_count, HD), cos_table, sin_table
-    ).astype(BF16)
-    keys = rotate(
-        dot_nn(hidden1, w_key).reshape(tok_rows, groups, HD), cos_table, sin_table
-    ).astype(BF16)
-    values = dot_nn(hidden1, w_value).astype(BF16)
-    query_blocks = queries.reshape(seq_count, seq_length, groups, group_size, HD)
-    key_blocks = keys.reshape(seq_count, seq_length, groups, HD)
-    value_blocks = values.reshape(seq_count, seq_length, groups, HD)
-    raw_scores = jnp.einsum(
-        "bqngd,bknd->bngqk", query_blocks, key_blocks, preferred_element_type=F32
-    ) * HD ** (-0.5)
-    position = jnp.arange(seq_length)
-    allowed = (segments[:, :, None] == segments[:, None, :]) & (
-        position[:, None] >= position[None, :]
-    )
-    scores = jnp.where(allowed[:, None, None, :, :], raw_scores, -1e30)
-    row_max = jnp.max(scores, -1, keepdims=True)
-    weights = jnp.exp(scores - row_max)
-    row_total = jnp.sum(weights, -1, keepdims=True)
-    probabilities = weights / row_total
-    log_total = (row_max + jnp.log(row_total)).reshape(head_count, tok_rows)
-    mixed_heads = jnp.einsum(
-        "bngqk,bknd->bqngd",
-        probabilities.astype(BF16),
-        value_blocks,
-        preferred_element_type=F32,
-    )
-    mixed_heads = mixed_heads.reshape(tok_rows, head_count * HD).astype(BF16)
-    residual = inputs + sum4(dot_nn(mixed_heads, w_out))
-    hidden2 = (row_norm(residual)[0] * norm2_gain).astype(BF16)
-    picked = (routes[:, :, None] == jnp.arange(experts)[None, None, :]).astype(F32)
-    expert_share = jnp.sum(gate_weights[:, :, None] * picked, 1).T[:, :, None]
+    cos_table, sin_table = tables(tokens.shape[0])
+    gain1, gain2 = norm1_gain[None], norm2_gain[None]
+    hidden1, queries, keys, values, lse, mixed, residual, hidden2, side = front_part(
+        tokens, gain1, cos_table, sin_table, w_query, w_key, w_value, segments, w_out, gain2,
+        routes.T, gate_weights.T,
+    )
     expert_grads, dhidden2, out_part = experts_part(
-        hidden2, cotangent, expert_gate, expert_up, expert_down, expert_share
+        hidden2, cotangent, expert_gate, expert_up, expert_down, side
     )
     output, input_grad, gains, grads, attn = back_part(
-        expert_grads.reshape(2, 4, 16, 192, 128),
-        dhidden2,
-        out_part,
-        residual,
-        tokens,
-        cotangent,
-        norm1_gain[None],
-        norm2_gain[None],
-        mixed_heads,
-        w_out,
-        queries.reshape(tok_rows, -1),
-        keys.reshape(tok_rows, -1),
-        values,
-        log_total,
-        segments.reshape(tok_rows, 1),
-        segments,
-        jnp.tile(cos_half, (1, 4)),
-        jnp.tile(jnp.concatenate([sin_half, -sin_half], 1), (1, 2)),
-        hidden1,
-        w_query,
-        w_key,
-        w_value,
+        expert_grads.reshape(2, 4, 16, 192, 128), dhidden2, out_part, residual, tokens,
+        cotangent, gain1, gain2, mixed, w_out, queries, keys, values, lse, side, segments,
+        cos_table, sin_table, hidden1, w_query, w_key, w_value,
     )
     (
         gate_grad, up_grad, down_grad, query_grad, key_grad, value_grad, out_grad, gain1_grad,
-        gain2_grad,
-    ) = unpack(grads.reshape(experts, 16, 192, 128), attn.reshape(64, 96, 128), gains)
+        gain2_grad, output, input_grad,
+    ) = unpack(
+        grads.reshape(experts, 16, 192, 128), attn.reshape(64, 96, 128), gains, output, input_grad
+    )
     return (
         output,
         input_grad,

time: 292 us -> 271 us (0.928)
  local copies, waits for them, and re-layouts: 20.9 us -> 3.49 us
  Pallas kernels: 259 us -> 266 us
  other arithmetic: 6.31 us -> 0 us
  matrix products: 4.11 us -> 0 us
    unnamed x40 -> x8, local copies, waits for them, and re-layouts: 13.2 us -> 3.49 us
    pallas_call x1, Pallas kernels: 6.24 us -> 14.8 us  [unpack(): pl.pallas_call(unpack_kernel, grid=(8,), out_shape=(jax.ShapeDtypeStruct(...]
    pallas_call x1, Pallas kernels: 208 us -> 200 us  [back_part(): pl.pallas_call(back_kernel, out_shape=(jax.ShapeDtypeStruct((rows, width)...]
    pallas_call x1, Pallas kernels: 28.4 us -> 34.2 us  [front_part(): pl.pallas_call(front_kernel, out_shape=made, in_specs=[ANY] * len(given),...]
    dot_general x6 -> x0, matrix products: 4.11 us -> none  [the longest x4 1.85 us: dot_nn(): return jnp.dot(first_op, second_op, preferred_element_type=F32)]
    reduce_sum x4 -> x0, other arithmetic: 3.6 us -> none  [the longest x2 1.95 us: row_norm(): inverse = lax.rsqrt(jnp.mean(values * values, -1, keepdims=True) + NORM_EPS)]
where the time goes in v4:
time: 271 us
  Pallas kernels  266 us (98%)
  local copies, waits for them, and re-layouts  3.49 us (1%)
    pallas_call x1, Pallas kernels, back_part(): pl.pallas_call(back_kernel, out_shape=(jax.ShapeDtypeStruct((rows, width)...  200 us
    pallas_call x1, Pallas kernels, front_part(): pl.pallas_call(front_kernel, out_shape=made, in_specs=[ANY] * len(given),...  34.2 us
    pallas_call x1, Pallas kernels, experts_part(): pl.pallas_call(expert_kernel, grid=(count // 2,), out_shape=(jax.ShapeDty...  16.9 us
    pallas_call x1, Pallas kernels, unpack(): pl.pallas_call(unpack_kernel, grid=(8,), out_shape=(jax.ShapeDtypeStruct(...  14.8 us

profile of v4, /device:TPU:0, one launch (start us, length us, event | category | flops | bytes accessed | tf_op | source)
XLA Modules:
  0.0 270.6 jit_solution(6653885603669305844)
XLA Ops:
  0.6 0.0 copy-start
  0.7 34.2 %shard_map.239 = (bf16[512,1024]{1,0:T(8,128)(2,1)}, bf16[512,256]{1,0:T(8,128)(2,1)}, bf16[512,128]{1,0:T(8,128)(2,1)}, bf16[512,128]{1,0:T(8,128)(2,1)}, f32[8...) custom-call(bf16[512,1024]{1,0:T(8,128)(2,1)} %tokens.1, ...), custom_call_target="tpu_custom_call" | custom-call | tf_op jit(solution)/shard_map/pallas_call | solution.py:471
  34.8 0.0 copy-done
  34.8 0.0 copy-start.2
  34.8 0.9 copy-done.2
  35.8 0.0 copy-start.3
  35.8 1.2 copy-done.3
  37.0 16.9 %shard_map.240 = (f32[8,16,192,128]{3,2,1,0:T(8,128)}, f32[512,1024]{1,0:T(8,128)S(1)}, f32[512,1024]{1,0:T(8,128)}) custom-call(bf16[512,1024]{1,0:T(8,128)(2,1)S(1)} %copy-done.3, bf16[512,1024]{1,0:T(8,128)(2,1)S(1)} %copy-done, bf16[8,1024,128]{2,1,0:T(8,128)(2,1)} %w_gate.1, bf16[8,1024,128]{2,1,0:T(8,128)(2,1)} %w_up.1, bf16[8,128,1024]{2,1,0:T(8,128)(2,1)} %w_down.1, ...), custom_call_target="tpu_custom_call" | custom-call | tf_op jit(solution)/shard_map/pallas_call | solution.py:533
  53.9 0.0 copy-start.1
  53.9 1.3 copy-done.1
  55.2 200.4 %shard_map.241 = (bf16[512,1024]{1,0:T(8,128)(2,1)}, f32[512,1024]{1,0:T(8,128)}, f32[8,1024]{1,0:T(8,128)}, f32[2,4,16,192,128]{4,3,2,1,0:T(8,128)}, f32[4,4,4,96,128]{4,3,2,1,0:T(8,128)}) custom-call(f32[2,4,16,192,128]{4,3,2,1,0:T(8,128)} %bitcast.10, f32[512,1024]{1,0:T(8,128)} %copy-done.1, f32[512,1024]{1,0:T(8,128)} %get-tuple-element.43.out_part, ...), custom_call_target="tpu_custom_call" | custom-call | tf_op jit(solution)/shard_map/pallas_call | solution.py:833
  255.7 14.8 %shard_map.242 = (f32[8,1024,128]{2,1,0:T(8,128)}, f32[8,1024,128]{2,1,0:T(8,128)}, f32[8,128,1024]{2,1,0:T(8,128)}, f32[1024,256]{1,0:T(8,128)}, f32[1024,128]{...) custom-call(f32[8,16,192,128]{3,2,1,0:T(8,128)} %bitcast.9, ...), custom_call_target="tpu_custom_call" | custom-call | tf_op jit(solution)/shard_map/pallas_call | solution.py:885
Async XLA Ops:
  0.6 34.2 %copy-start = (bf16[512,1024]{1,0:T(8,128)(2,1)S(1)}, bf16[512,1024]{1,0:T(8,128)(2,1)}, u32[]{:S(2)}) copy-start(bf16[512,1024]{1,0:T(8,128)(2,1)} %dy.3) | copy-start | bytes 3145732
  34.8 1.0 copy-start.2
  35.8 1.2 copy-start.3
  53.9 1.3 copy-start.1

commit v5 on v4

--- a/solution.py
+++ b/solution.py
@@ -16,7 +16,6 @@
 HD = 64
 NORM_EPS = 1e-06
 ROPE_THETA = 10000.0
-FLOWS = ((0, 1), (0, -1), (1, 1), (1, -1))
 PIECES = 4
 VMEM = pl.BlockSpec(memory_space=pltpu.VMEM)
 ANY = pl.BlockSpec(memory_space=pl.ANY)
@@ -36,20 +35,6 @@
     return lax.dot_general(
         first_op, second_op, (((1,), (1,)), ((), ())), preferred_element_type=F32
     )
-
-
-def ring_pos(dp):
-    xy = dp // 2
-    x, y = xy % 4, xy // 4
-    turn = (x + y) % 4
-    return 4 * y + turn, 4 * x + turn
-
-
-def ring_dp(kind, pos, zhi):
-    along = pos // 4
-    across = (pos % 4 - along + 4) % 4
-    x, y = (across, along) if kind == 0 else (along, across)
-    return (y * 4 + x) * 2 + zhi
 
 
 class Place:
@@ -58,10 +43,6 @@
         self.tensor = lax.axis_index("tensor")
         zhi = self.dp % 2
         self.z_far = self.dp + 1 - 2 * zhi
-        self.pos = ring_pos(self.dp)
-        self.next = [
-            ring_dp(kind, (self.pos[kind] + step + 16) % 16, zhi) for kind, step in FLOWS
-        ]
         xy = self.dp // 2
         x, y = xy % 4, xy // 4
         self.x, self.y = x, y
@@ -78,86 +59,10 @@
         self.z_near = self.tensor + 2 - 4 * (self.tensor // 2)
 
 
-class Ring:
-    def __init__(self, place, first, mine, land, zland, total, out, sems):
-        self.place, self.first, self.mine, self.land = place, first, mine, land
-        self.zland, self.total, self.out = zland, total, out
-        self.rs_s, self.rs_r, self.ag_s, self.ag_r, self.z_s, self.z_r, self.keep_s = sems
-
-    def chunk(self, f, back):
-        kind, step = FLOWS[f]
-        return (self.place.pos[kind] - step * back + 32) % 16
-
-    def rs(self, f, s, src):
-        c = self.chunk(f, 1 + s)
-        return pltpu.make_async_remote_copy(
-            src.at[f, c], self.land.at[f, c], self.rs_s.at[f, s], self.rs_r.at[f, s],
-            device_id=(self.place.next[f], self.place.tensor), device_id_type=MESH,
-        )
-
-    def ag(self, f, s, src):
-        return pltpu.make_async_remote_copy(
-            src, self.out.at[f, self.chunk(f, s)], self.ag_s.at[f, s], self.ag_r.at[f, s],
-            device_id=(self.place.next[f], self.place.tensor), device_id_type=MESH,
-        )
-
-    def zcopy(self, f):
-        return pltpu.make_async_remote_copy(
-            self.land.at[f, self.chunk(f, 0)], self.zland.at[f], self.z_s.at[f], self.z_r.at[f],
-            device_id=(self.place.z_far, self.place.tensor), device_id_type=MESH,
-        )
-
-    def keep(self, f):
-        return pltpu.make_async_copy(
-            self.total.at[f], self.out.at[f, self.chunk(f, 0)], self.keep_s.at[f]
-        )
-
-    def begin(self, f):
-        self.rs(f, 0, self.first).start()
-
-    def rs_step(self, s):
-        for f in range(4):
-            self.rs(f, s - 1, self.land).wait_recv()
-            c = self.chunk(f, 1 + s)
-            self.land[f, c] = self.land[f, c] + self.mine[f, c]
-            self.rs(f, s, self.land).start()
-
-    def turn(self):
-        for f in range(4):
-            self.rs(f, 14, self.land).wait_recv()
-            c = self.chunk(f, 0)
-            self.land[f, c] = self.land[f, c] + self.mine[f, c]
-            self.zcopy(f).start()
-
-    def back(self):
-        for f in range(4):
-            self.zcopy(f).wait_recv()
-            self.total[f] = self.land[f, self.chunk(f, 0)] + self.zland[f]
-            self.ag(f, 0, self.total.at[f]).start()
-            self.keep(f).start()
-
-    def ag_step(self, s):
-        for f in range(4):
-            held = self.out.at[f, self.chunk(f, s)]
-            self.ag(f, s - 1, held).wait_recv()
-            self.ag(f, s, held).start()
-
-    def end(self):
-        for f in range(4):
-            self.ag(f, 14, self.total.at[f]).wait_recv()
-            self.zcopy(f).wait_send()
-            self.keep(f).wait()
-
-    def drain(self, s):
-        for f in range(4):
-            self.rs(f, s, self.land).wait_send()
-            self.ag(f, s, self.total.at[f]).wait_send()
-
-
 class AxisRing:
-    def __init__(self, place, mine, land, land2, zland, total, out, sems):
+    def __init__(self, place, mine, land, land2, zland, out, sems):
         self.place, self.mine, self.land, self.land2 = place, mine, land, land2
-        self.zland, self.total, self.out, self.sems = zland, total, out, sems
+        self.zland, self.out, self.sems = zland, out, sems
 
     def spots(self, f, back1, back2):
         step = 1 - 2 * (f % 2)
@@ -184,7 +89,7 @@
 
     def ag2(self, f, s, src):
         i, j = self.spots(f, 0, s)
-        return self.send(f, s, 2, src, self.out.at[f, i, j])
+        return self.send(f, s, 2, src.at[f, i, j], self.out.at[f, i, j])
 
     def ag1(self, f, s, src):
         return self.send(f, s, 3, src, self.out.at[f, self.spots(f, s, 0)[0]])
@@ -199,7 +104,7 @@
     def keep(self, f):
         i, j = self.spots(f, 0, 0)
         return pltpu.make_async_copy(
-            self.total.at[f], self.out.at[f, i, j], self.sems[10].at[f]
+            self.mine.at[f, i, j], self.out.at[f, i, j], self.sems[10].at[f]
         )
 
     def begin(self):
@@ -231,16 +136,17 @@
     def back(self):
         for f in range(4):
             self.zcopy(f).wait_recv()
-            self.total[f] = self.land2[f, self.spots(f, 0, 0)[1]] + self.zland[f]
-            self.ag2(f, 0, self.total.at[f]).start()
+            i, j = self.spots(f, 0, 0)
+            self.mine[f, i, j] = self.land2[f, j] + self.zland[f]
+            self.ag2(f, 0, self.mine).start()
             self.keep(f).start()
 
     def ag2_step(self, s):
         for f in range(4):
-            self.ag2(f, s - 1, self.total.at[f]).wait_recv()
-            i, j = self.spots(f, 0, s)
+            self.ag2(f, s - 1, self.out).wait_recv()
+            i = self.spots(f, 0, s)[0]
             if s < 3:
-                self.ag2(f, s, self.out.at[f, i, j]).start()
+                self.ag2(f, s, self.out).start()
             else:
                 self.keep(f).wait()
                 self.ag1(f, 0, self.out.at[f, i]).start()
@@ -252,12 +158,26 @@
             if s < 3:
                 self.ag1(f, s, held).start()
 
+    def op(self, k):
+        if k == 0:
+            self.begin()
+        elif k <= 3:
+            self.rs1_step(k)
+        elif k <= 6:
+            self.rs2_step(k - 3)
+        elif k == 7:
+            self.back()
+        elif k <= 10:
+            self.ag2_step(k - 7)
+        else:
+            self.ag1_step(k - 10)
+
     def drain(self, s):
         for f in range(4):
             if s > 0:
                 self.rs1(f, s, self.land).wait_send()
             self.rs2(f, s, self.land2.at[f]).wait_send()
-            self.ag2(f, s, self.total.at[f]).wait_send()
+            self.ag2(f, s, self.mine if s == 0 else self.out).wait_send()
             self.ag1(f, s, self.out.at[f, 0]).wait_send()
 
     def close(self):
@@ -360,7 +280,7 @@
     kept, refs = refs[:9], refs[9:]
     inside, refs = refs[:12], refs[12:]
     made, refs = refs[:9], refs[9:]
-    part, land1, land2, in_sem, out_sem = refs[:5]
+    part, land1, land2, in_sem, out_sem, own_sem = refs[:6]
     (
         tokens, gain1, cos_table, sin_table, w_query, w_key, w_value, seg_row, w_out, gain2,
         routes, route_weights,
@@ -373,12 +293,14 @@
     stores = [
         pltpu.make_async_copy(src, dst, out_sem.at[i])
         for i, (src, dst) in enumerate(zip(made, kept))
+        if i != 6
     ]
+    stores.insert(6, None)
     for load in loads:
         load.start()
     place = Place()
     greet(place, False)
-    work = Sum4(place, part, land1, land2, refs[5:])
+    work = Sum4(place, part, land1, land2, refs[6:])
     for load in loads:
         load.wait()
     rows = [
@@ -441,17 +363,24 @@
 
     loop(0, PIECES, finish)
 
+    def own_rows(k):
+        return pltpu.make_async_copy(
+            residual.at[work.own(k)], kept[6].at[work.local(k)], own_sem.at[k]
+        )
+
     def close(k):
         at = work.own(k)
         work.three(k, residual.at[at], residual.at[at]).wait()
+        own_rows(k).start()
         give(work.other(k))
         work.one(k).wait_send()
 
     loop(0, PIECES, close)
-    for store in stores[6:8]:
-        store.start()
-    for store in stores:
-        store.wait()
+    stores[7].start()
+    for i, store in enumerate(stores):
+        if i != 6:
+            store.wait()
+    loop(0, PIECES, lambda k: own_rows(k).wait())
 
 
 def front_part(*given):
@@ -470,13 +399,13 @@
     )
     return pl.pallas_call(
         front_kernel,
-        out_shape=made,
+        out_shape=made[:6] + (jax.ShapeDtypeStruct(half, F32),) + made[7:],
         in_specs=[ANY] * len(given),
         out_specs=(ANY,) * len(made),
         scratch_shapes=[pltpu.VMEM(a.shape, a.dtype) for a in given + made]
         + [pltpu.VMEM((rows, width), F32)]
         + [pltpu.VMEM(half, F32)] * 2
-        + [DMA((len(given),)), DMA((len(made),))]
+        + [DMA((len(given),)), DMA((len(made),)), DMA((PIECES,))]
         + [DMA((PIECES,))] * 6,
         compiler_params=pltpu.CompilerParams(
             collective_id=1, has_side_effects=True, vmem_limit_bytes=60 << 20
@@ -484,78 +413,6 @@
     )(*given)
 
 
-def expert_kernel(
-    hidden2, dy, w_gate, w_up, w_down, side, grads, dhidden2, out, hidden2_t
-):
-    step = pl.program_id(0)
-
-    @pl.when(step == 0)
-    def _():
-        hidden2_t[...] = hidden2[...].T
-        dhidden2[...] = jnp.zeros_like(dhidden2)
-        out[...] = jnp.zeros_like(out)
-
-    down_pair = w_down[...].reshape(256, 1024)
-    dact_pair = dot_nt(dy[...], down_pair)
-    acts = []
-    for i in range(2):
-        both_w = jnp.concatenate([w_gate[i], w_up[i]], 1)
-        both = dot_nn(hidden2[...], both_w)
-        gate, up = both[:, :128], both[:, 128:]
-        sig = 1.0 / (1.0 + jnp.exp(-gate))
-        silu = gate * sig
-        lane = lax.broadcasted_iota(jnp.int32, side.shape, 1)
-        chosen = jnp.where(lane == 2 * step + i, side[...], 0.0)
-        weight = jnp.sum(chosen, 1, keepdims=True)
-        acts.append((silu * up * weight).astype(BF16))
-        dact = dact_pair[:, 128 * i : 128 * i + 128] * weight
-        dgate = (dact * up * (sig * (1.0 + gate * (1.0 - sig)))).astype(BF16)
-        dup = (dact * silu).astype(BF16)
-        dboth = jnp.concatenate([dgate, dup], 1)
-        grad = dot_nn(hidden2_t[...], dboth)
-        grads[i, :, 0:64] = grad[:, :128].reshape(16, 64, 128)
-        grads[i, :, 64:128] = grad[:, 128:].reshape(16, 64, 128)
-        dhidden2[...] += dot_nt(dboth, both_w)
-    act_pair = jnp.concatenate(acts, 1)
-    out[...] += dot_nn(act_pair, down_pair)
-    down_grad = dot_tn(act_pair, dy[...])
-    for i in range(2):
-        for j in range(8):
-            for half in range(2):
-                at = 128 * i + 64 * half
-                grads[i, 2 * j + half, 128:192] = down_grad[at : at + 64, 128 * j : 128 * j + 128]
-
-
-def experts_part(hidden2, dy, w_gate, w_up, w_down, side):
-    rows, width = hidden2.shape
-    count = w_gate.shape[0]
-    whole = pl.BlockSpec((rows, width), lambda p: (0, 0))
-    return pl.pallas_call(
-        expert_kernel,
-        grid=(count // 2,),
-        out_shape=(
-            jax.ShapeDtypeStruct((count, 16, 192, 128), F32),
-            jax.ShapeDtypeStruct((rows, width), F32),
-            jax.ShapeDtypeStruct((rows, width), F32),
-        ),
-        in_specs=[
-            whole,
-            whole,
-            pl.BlockSpec((2, width, 128), lambda p: (p, 0, 0)),
-            pl.BlockSpec((2, width, 128), lambda p: (p, 0, 0)),
-            pl.BlockSpec((2, 128, width), lambda p: (p, 0, 0)),
-            pl.BlockSpec(side.shape, lambda p: (0, 0)),
-        ],
-        out_specs=(
-            pl.BlockSpec((2, 16, 192, 128), lambda p: (p, 0, 0, 0)),
-            whole,
-            whole,
-        ),
-        scratch_shapes=[pltpu.VMEM((width, rows), BF16)],
-        compiler_params=pltpu.CompilerParams(vmem_limit_bytes=48 << 20),
-    )(hidden2, dy, w_gate, w_up, w_down, side)
-
-
 def row_norm(values):
     inverse = lax.rsqrt(jnp.mean(values * values, -1, keepdims=True) + NORM_EPS)
     return values * inverse, inverse
@@ -571,81 +428,152 @@
     return jnp.sum(values.reshape(-1, 8, values.shape[-1]), 0)
 
 
-def back_kernel(
-    grads, dhidden2, out_part, residual, tokens, dy, gain1, gain2, mixed, w_out, queries, keys,
-    values, lse, side, seg_row, cos_table, sin_table, hidden1, w_query, w_key, w_value,
-    output, input_grad, gain_sums, mine, attn,
-    land, zland, total, attn_land, attn_land2, attn_zland, attn_total,
-    land1, land2, dresidual, dhidden1, dqkv, folded, gains, gains_in, *sems
-):
+def back_kernel(*refs):
+    given, refs = refs[:23], refs[23:]
+    output_hbm, input_grad_hbm, gain_sums, grads_sum, attn_sum = refs[:5]
+    inside, refs = refs[5:24], refs[24:]
+    (
+        hidden2, dy, side, residual, gain2, mixed, w_out, queries, keys, values, lse, seg_row,
+        cos_table, sin_table, w_query, w_key, w_value, tokens, gain1,
+    ) = inside
+    gate_w, up_w, down_w = refs[:3]
+    (
+        mine, land, ring_land2, zland, attn, attn_land, attn_land2, attn_zland, output, dresidual,
+        dhidden2, out_part, hidden2_t, land1, land2, land3, folded, gains, gains_in,
+    ) = refs[3:22]
+    sems = refs[22:]
+    ring_sems, sems = sems[:11], sems[11:]
+    attn_sems, sems = sems[:11], sems[11:]
+    sum_sems, sems = sems[:6], sems[6:]
+    load_sem, weight_sem, late_sem, gain_s, gain_r = sems
+    dqkv = hidden2_t.at[0:512]
+    weights = given[19:22]
+    hidden1_hbm = given[22]
+
+    def weight_loads(p):
+        slot = p % 2
+        return [
+            pltpu.make_async_copy(
+                src.at[2 * p : 2 * p + 2], dst.at[slot], weight_sem.at[slot, i]
+            )
+            for i, (src, dst) in enumerate(zip(weights, (gate_w, up_w, down_w)))
+        ]
+
+    loads = [
+        pltpu.make_async_copy(src, dst, load_sem.at[i])
+        for i, (src, dst) in enumerate(zip(given[:19], inside))
+    ]
+    for load in loads[:3]:
+        load.start()
+    for p in range(2):
+        for load in weight_loads(p):
+            load.start()
+    for load in loads[3:]:
+        load.start()
     place = Place()
     greet(place, True)
-    ring_sems, sems = sems[:7], sems[7:]
-    attn_sems, sems = sems[:11], sems[11:]
-    sum_sems, sems = sems[:6], sems[6:]
-    load_sem, gain_s, gain_r = sems
     rings = [
-        Ring(
-            place, grads.at[u], mine.at[u], land.at[u], zland.at[u], total.at[u],
-            mine.at[u], [sem.at[u] for sem in ring_sems],
+        AxisRing(
+            place, mine.at[u], land.at[u], ring_land2.at[u], zland.at[u], grads_sum.at[u],
+            [sem.at[u] for sem in ring_sems],
         )
-        for u in range(2)
+        for u in range(4)
     ]
-    attn_ring = AxisRing(
-        place, attn, attn_land, attn_land2, attn_zland, attn_total, attn, attn_sems
-    )
+    rings.append(
+        AxisRing(place, attn, attn_land, attn_land2, attn_zland, attn_sum, attn_sems)
+    )
+
+    def go(k, *units):
+        for u in units:
+            rings[u].op(k)
+
     sums = [
-        Sum4(place, part, land1.at[i], land2.at[i], [sem.at[i] for sem in sum_sems])
-        for i, part in enumerate((dhidden2, out_part, dhidden1))
+        Sum4(place, part, land1.at[which], land2.at[which], [sem.at[i] for sem in sum_sems])
+        for i, (part, which) in enumerate(((dhidden2, 0), (out_part, 1), (dhidden2, 0)))
     ]
     back2, forward2, back1 = sums
-    land3 = back2.land1
-
+
+    folded[...] = jnp.zeros_like(folded)
+    for load in loads[:3]:
+        load.wait()
+    hidden2_t[...] = hidden2[...].T
+    for p in range(4):
+        slot = p % 2
+        for load in weight_loads(p):
+            load.wait()
+        down_pair = down_w[slot].reshape(256, 1024)
+        dact_pair = dot_nt(dy[...], down_pair)
+        acts, dboths, both_ws = [], [], []
+        for i in range(2):
+            e = 2 * p + i
+            both_w = jnp.concatenate([gate_w[slot, i], up_w[slot, i]], 1)
+            both = dot_nn(hidden2[...], both_w)
+            gate, up = both[:, :128], both[:, 128:]
+            sig = 1.0 / (1.0 + jnp.exp(-gate))
+            silu = gate * sig
+            weight = side[:, e : e + 1]
+            acts.append((silu * up * weight).astype(BF16))
+            dact = dact_pair[:, 128 * i : 128 * i + 128] * weight
+            dgate = (dact * up * (sig * (1.0 + gate * (1.0 - sig)))).astype(BF16)
+            dup = (dact * silu).astype(BF16)
+            dboth = jnp.concatenate([dgate, dup], 1)
+            grad = dot_nn(hidden2_t[...], dboth)
+            for h in range(2):
+                rows = slice(512 * h, 512 * h + 512)
+                mine[p, 2 * i + h, :, :, 0:32] = grad[rows, :128].reshape(4, 4, 32, 128)
+                mine[p, 2 * i + h, :, :, 32:64] = grad[rows, 128:].reshape(4, 4, 32, 128)
+            part = dot_nt(dboth, both_w)
+            dhidden2[...] = part if e == 0 else dhidden2[...] + part
+        act_pair = jnp.concatenate(acts, 1)
+        down_grad = dot_tn(act_pair, dy[...])
+        for i in range(2):
+            for j in range(8):
+                piece = down_grad[128 * i : 128 * i + 128, 128 * j : 128 * j + 128]
+                mine[p, 2 * i + j // 4, j % 4, :, 64:96] = piece.reshape(4, 32, 128)
+        if p >= 2:
+            go(1, p - 2)
+        go(0, p)
+        part = dot_nn(act_pair, down_pair)
+        out_part[...] = part if p == 0 else out_part[...] + part
+        if p < 2:
+            for load in weight_loads(p + 2):
+                load.start()
+    late = [
+        pltpu.make_async_copy(hidden1_hbm, hidden2, late_sem.at[0]),
+    ]
+    for load in late:
+        load.start()
     back2.begin()
-    for ring in rings:
-        for f in range(4):
-            ring.begin(f)
-    loads = [pltpu.make_async_copy(grads.at[u], mine.at[u], load_sem.at[u]) for u in range(2)]
-    for load in loads:
-        load.start()
-    folded[...] = jnp.zeros_like(folded)
+    for load in loads[3:]:
+        load.wait()
     seg_col = side[:, 8:9].astype(jnp.int32)
-
-    def step(s):
-        for ring in rings:
-            ring.rs_step(s)
-
-    def gather(s):
-        for ring in rings:
-            ring.ag_step(s)
-
     loop(0, PIECES, back2.middle)
-    for load in loads:
-        load.wait()
-    step(1)
+    go(2, 0)
 
     def finish2(k):
         d = back2.total(k)
         at = back2.own(k)
-        scaled, inverse = row_norm(residual[at])
+        scaled, inverse = row_norm(residual[back2.local(k)])
         folded[8:16] += fold(d * scaled)
         dresidual[at] = dy[at].astype(F32) + norm_back(d, scaled, inverse, gain2[...])
         back2.three(k, dresidual.at[at], dresidual.at[at]).start()
 
-    step(2)
     finish2(0)
-    step(3)
+    go(2, 1)
     finish2(1)
-    step(4)
-    step(5)
+    go(1, 2, 3)
+    go(3, 0)
     finish2(2)
-    step(6)
+    go(3, 1)
+    go(4, 0)
     finish2(3)
-    step(7)
+    go(2, 2)
+    go(4, 1)
 
     def close2(k):
         at = back2.own(k)
-        back2.three(k, dresidual.at[at], dresidual.at[at]).wait_recv()
+        back2.three(k, dresidual.at[at], dresidual.at[at]).wait()
+        back2.one(k).wait_send()
 
     loop(0, PIECES, close2)
     forward2.begin()
@@ -657,11 +585,27 @@
         piece = out_grad[:, 128 * j : 128 * j + 128].reshape(2, 4, 32, 128)
         attn[j // 2, 2 * (j % 2) : 2 * (j % 2) + 2, :, 64:96] = piece
 
-    step(8)
+    go(5, 0)
     loop(0, PIECES, forward2.middle)
+    go(2, 3)
+    go(5, 1)
 
     def unrotate(grad):
         return (grad * cos_table[...] + swap_halves(grad) * sin_table[...]).astype(BF16)
+
+    def between(h):
+        if h == 0:
+            go(6, 0, 1)
+            go(3, 2)
+        elif h == 1:
+            go(3, 3)
+            go(7, 0)
+        elif h == 2:
+            go(7, 1)
+            go(4, 2, 3)
+        else:
+            go(8, 0, 1)
+            go(5, 2, 3)
 
     dkeys, dvalues = [], []
     for g in range(2):
@@ -689,8 +633,8 @@
                     dvalue[t] = dvalue[t] + dvalue_part[256 * t : 256 * t + 256]
                     dkey[t] = dkey[t] + dkey_part[256 * t : 256 * t + 256]
                 blocks.append(dot_tn(dscores, key[:until]))
-                if 2 * h + b < 6:
-                    step(9 + 2 * h + b)
+                if b == 1:
+                    between(h)
             dquery.append(jnp.concatenate(blocks, 0) * HD ** (-0.5))
         dqkv[:, 128 * g : 128 * g + 128] = unrotate(jnp.concatenate(dquery, 1))
         dkeys.append(jnp.concatenate(dkey, 0) * HD ** (-0.5))
@@ -698,42 +642,71 @@
     dqkv[:, 256:384] = unrotate(jnp.concatenate(dkeys, 1))
     dqkv[:, 384:512] = jnp.concatenate(dvalues, 1).astype(BF16)
 
-    hidden_grad = dot_tn(hidden1[...], dqkv[...])
+    for load in late:
+        load.wait()
+    hidden_grad = dot_tn(hidden2[...], dqkv[...])
     for j in range(4):
         piece = hidden_grad[:, 128 * j : 128 * j + 128].reshape(4, 4, 4, 16, 128)
         attn[:, :, :, 16 * j : 16 * j + 16] = piece
-    attn_ring.begin()
-    for ring in rings:
-        ring.turn()
-    dhidden1[...] = (
+    go(9, 0, 1)
+    go(6, 2, 3)
+    go(0, 4)
+    go(10, 0, 1)
+    dhidden2[...] = (
         dot_nt(dqkv[:, :256], w_query[...])
         + dot_nt(dqkv[:, 256:384], w_key[...])
         + dot_nt(dqkv[:, 384:512], w_value[...])
     )
     back1.begin()
-    attn_ring.rs1_step(1)
-    attn_ring.rs1_step(2)
-    for ring in rings:
-        ring.back()
+    go(7, 2, 3)
+    go(1, 4)
+
+    def finish_out(k):
+        done = forward2.total(k) + residual[forward2.local(k)]
+        at = forward2.local(k)
+        output[forward2.own(k)] = done.astype(BF16)
+        forward2.land1[at] = done
+        forward2.three(k, forward2.land1.at[at], land3.at[at]).start()
+
+    def close_out(k):
+        at = forward2.local(k)
+        forward2.three(k, forward2.land1.at[at], land3.at[at]).wait()
+        output[forward2.other(k)] = land3[at].astype(BF16)
+
+    loop(0, PIECES, finish_out)
+    go(11, 0)
     loop(0, PIECES, back1.middle)
-    gather(1)
-    attn_ring.rs1_step(3)
-    gather(2)
-    attn_ring.rs2_step(1)
+    go(8, 2, 3)
+    go(11, 1)
+    go(2, 4)
+    go(9, 2, 3)
+    loop(0, PIECES, close_out)
+    stores = [
+        pltpu.make_async_copy(output, output_hbm, late_sem.at[1]),
+        pltpu.make_async_copy(dresidual, input_grad_hbm, late_sem.at[2]),
+    ]
+    stores[0].start()
+    go(12, 0, 1)
+    go(10, 2)
+    go(3, 4)
+    go(10, 3)
 
     def finish1(k):
-        gather(3 + k)
         d = back1.total(k)
         at = back1.own(k)
         scaled, inverse = row_norm(tokens[at].astype(F32))
         folded[0:8] += fold(d * scaled)
-        input_grad[at] = dresidual[at] + norm_back(d, scaled, inverse, gain1[...])
-        back1.three(k, input_grad.at[at], input_grad.at[at]).start()
-
-    loop(0, 2, finish1)
-    attn_ring.rs2_step(2)
-    loop(2, PIECES, finish1)
-    attn_ring.rs2_step(3)
+        dresidual[at] = dresidual[at] + norm_back(d, scaled, inverse, gain1[...])
+        back1.three(k, dresidual.at[at], dresidual.at[at]).start()
+
+    finish1(0)
+    finish1(1)
+    go(13, 0, 1)
+    go(4, 4)
+    finish1(2)
+    go(11, 2)
+    go(5, 4)
+    finish1(3)
     gains[0] = jnp.concatenate(
         [
             jnp.sum(folded[0:8], 0, keepdims=True),
@@ -754,122 +727,104 @@
         swap(i).wait_recv()
         gains[i + 1] = gains[i] + gains_in[i]
 
-    def finish_out(k):
-        done = forward2.total(k) + residual[forward2.own(k)]
-        at = forward2.local(k)
-        output[forward2.own(k)] = done.astype(BF16)
-        forward2.land1[at] = done
-        forward2.three(k, forward2.land1.at[at], land3.at[at]).start()
-
-    def close_out(k):
-        at = forward2.local(k)
-        forward2.three(k, forward2.land1.at[at], land3.at[at]).wait_recv()
-        output[forward2.other(k)] = land3[at].astype(BF16)
-
     swap(0).start()
-    gather(7)
-    attn_ring.back()
+    go(11, 3)
+    go(6, 4)
     add_swap(0)
     swap(1).start()
-    gather(8)
-    attn_ring.ag2_step(1)
+
+    def close1(k):
+        at = back1.own(k)
+        back1.three(k, dresidual.at[at], dresidual.at[at]).wait()
+
+    loop(0, PIECES, close1)
+    stores[1].start()
+    go(12, 2)
     add_swap(1)
     swap(2).start()
-    gather(9)
-    attn_ring.ag2_step(2)
+    go(7, 4)
+    go(12, 3)
     add_swap(2)
     swap(3).start()
-    gather(10)
-    attn_ring.ag2_step(3)
+    go(8, 4)
+    go(13, 2)
     add_swap(3)
     swap(4).start()
-    loop(0, PIECES, finish_out)
-    gather(11)
-    attn_ring.ag1_step(1)
+    go(9, 4)
+    go(13, 3)
     add_swap(4)
     swap(5).start()
-    gather(12)
-    attn_ring.ag1_step(2)
+    go(10, 4)
     add_swap(5)
     gain_sums[...] = gains[6]
-    gather(13)
-    loop(0, PIECES, close_out)
-    gather(14)
-    attn_ring.ag1_step(3)
+    go(11, 4)
+    go(12, 4)
+    go(13, 4)
     for ring in rings:
-        ring.end()
-
-    def drain(s):
-        for ring in rings:
+        for s in range(3):
             ring.drain(s)
-
-    loop(0, 15, drain)
-    for s in range(3):
-        attn_ring.drain(s)
-    attn_ring.close()
+        ring.close()
     for i in range(6):
         swap(i).wait_send()
 
     def close(k):
-        for work in sums:
-            work.one(k).wait_send()
-        at = back2.own(k)
-        back2.three(k, dresidual.at[at], dresidual.at[at]).wait_send()
-        here = forward2.local(k)
-        forward2.three(k, forward2.land1.at[here], land3.at[here]).wait_send()
-        back1.three(k, input_grad.at[at], input_grad.at[at]).wait()
+        forward2.one(k).wait_send()
+        back1.one(k).wait_send()
 
     loop(0, PIECES, close)
-
-
-def back_part(grads, *rest):
-    rows, width = rest[0].shape
+    for store in stores:
+        store.wait()
+
+
+def back_part(*given):
+    rows, width = given[0].shape
     half = (rows // 2, width)
-    m, n = grads.shape[3], 96
+    grads, attn = (4, 4, 4, 4, 96, 128), (4, 4, 4, 96, 128)
     S = pltpu.VMEM
-    ring_sems = [DMA((2, 4, 15))] * 4 + [DMA((2, 4))] * 3
+    ring_sems = [DMA((4, 4, 3))] * 8 + [DMA((4, 4))] * 3
     attn_sems = [DMA((4, 3))] * 8 + [DMA((4,))] * 3
-    attn = (4, 4, 4, n, 128)
     return pl.pallas_call(
         back_kernel,
         out_shape=(
             jax.ShapeDtypeStruct((rows, width), BF16),
             jax.ShapeDtypeStruct((rows, width), F32),
             jax.ShapeDtypeStruct((8, width), F32),
-            jax.ShapeDtypeStruct(grads.shape, F32),
+            jax.ShapeDtypeStruct(grads, F32),
             jax.ShapeDtypeStruct(attn, F32),
         ),
-        in_specs=[ANY] + [VMEM] * len(rest),
-        out_specs=(VMEM,) * 5,
-        scratch_shapes=[
-            S(grads.shape, F32), S((2, 4, m, 128), F32),
-            S((2, 4, m, 128), F32),
-            S(attn, F32), S((4, 4, n, 128), F32), S((4, n, 128), F32),
-            S((4, n, 128), F32),
-            S((3,) + half, F32), S((3,) + half, F32),
-            S((rows, width), F32), S((rows, width), F32), S((rows, 512), BF16),
+        in_specs=[ANY] * len(given),
+        out_specs=(ANY, ANY, VMEM, ANY, ANY),
+        scratch_shapes=[S(a.shape, a.dtype) for a in given[:19]]
+        + [S((2, 2, width, 128), BF16), S((2, 2, width, 128), BF16), S((2, 2, 128, width), BF16)]
+        + [
+            S(grads, F32), S(grads, F32), S((4, 4, 4, 96, 128), F32), S((4, 4, 96, 128), F32),
+            S(attn, F32), S(attn, F32), S((4, 4, 96, 128), F32), S((4, 96, 128), F32),
+            S((rows, width), BF16), S((rows, width), F32),
+            S((rows, width), F32), S((rows, width), F32), S((width, rows), BF16),
+            S((2,) + half, F32), S((2,) + half, F32), S(half, F32),
             S((16, width), F32), S((7, 8, width), F32), S((6, 8, width), F32),
         ]
         + ring_sems
         + attn_sems
         + [DMA((3, PIECES))] * 6
-        + [DMA((2,)), DMA((6,)), DMA((6,))],
+        + [DMA((19,)), DMA((2, 3)), DMA((3,)), DMA((6,)), DMA((6,))],
         compiler_params=pltpu.CompilerParams(
-            collective_id=2, has_side_effects=True, vmem_limit_bytes=63 << 20
+            collective_id=2, has_side_effects=True, vmem_limit_bytes=64 << 20
         ),
-    )(grads, *rest)
+    )(*given)
 
 
 def unpack_kernel(
     grads, attn, gains, forward, backward, gate, up, down, query, key, value, out, gain1, gain2,
     output, input_grad
 ):
-    gate[0] = grads[0, :, 0:64].reshape(1024, 128)
-    up[0] = grads[0, :, 64:128].reshape(1024, 128)
-    for j in range(8):
-        lanes = slice(128 * j, 128 * j + 128)
-        for half in range(2):
-            down[0, 64 * half : 64 * half + 64, lanes] = grads[0, 2 * j + half, 128:192]
+    for h in range(2):
+        rows = slice(512 * h, 512 * h + 512)
+        gate[0, rows] = grads[0, h, :, 0:32].reshape(512, 128)
+        up[0, rows] = grads[0, h, :, 32:64].reshape(512, 128)
+        for a in range(4):
+            lanes = slice(128 * (4 * h + a), 128 * (4 * h + a) + 128)
+            down[0, :, lanes] = grads[0, h, 4 * a : 4 * a + 4, 64:96].reshape(128, 128)
     query[:, 0:128] = attn[:, 0:16].reshape(128, 128)
     query[:, 128:256] = attn[:, 16:32].reshape(128, 128)
     key[...] = attn[:, 32:48].reshape(128, 128)
@@ -899,7 +854,7 @@
             jax.ShapeDtypeStruct(backward.shape, F32),
         ),
         in_specs=[
-            pl.BlockSpec((1, 16, 192, 128), lambda p: (p, 0, 0, 0)),
+            pl.BlockSpec((1, 2, 16, 96, 128), lambda p: (p, 0, 0, 0, 0)),
             pl.BlockSpec((8, 96, 128), lambda p: (p, 0, 0)),
             pl.BlockSpec((8, 128), lambda p: (0, p)),
             pl.BlockSpec((64, 1024), lambda p: (p, 0)),
@@ -957,19 +912,16 @@
         tokens, gain1, cos_table, sin_table, w_query, w_key, w_value, segments, w_out, gain2,
         routes.T, gate_weights.T,
     )
-    expert_grads, dhidden2, out_part = experts_part(
-        hidden2, cotangent, expert_gate, expert_up, expert_down, side
-    )
     output, input_grad, gains, grads, attn = back_part(
-        expert_grads.reshape(2, 4, 16, 192, 128), dhidden2, out_part, residual, tokens,
-        cotangent, gain1, gain2, mixed, w_out, queries, keys, values, lse, side, segments,
-        cos_table, sin_table, hidden1, w_query, w_key, w_value,
+        hidden2, cotangent, side, residual, gain2, mixed, w_out, queries, keys, values, lse,
+        segments, cos_table, sin_table, w_query, w_key, w_value, tokens, gain1, expert_gate,
+        expert_up, expert_down, hidden1,
     )
     (
         gate_grad, up_grad, down_grad, query_grad, key_grad, value_grad, out_grad, gain1_grad,
         gain2_grad, output, input_grad,
     ) = unpack(
-        grads.reshape(experts, 16, 192, 128), attn.reshape(64, 96, 128), gains, output, input_grad
+        grads.reshape(experts, 2, 16, 96, 128), attn.reshape(64, 96, 128), gains, output, input_grad
     )
     return (
         output,

time: 271 us -> 259 us (0.956)
  Pallas kernels: 266 us -> 258 us
  local copies, waits for them, and re-layouts: 3.49 us -> 0 us
    pallas_call x2 -> x1, Pallas kernels: 51.1 us -> 33.4 us  [front_part(): pl.pallas_call(front_kernel, out_shape=made[:6] + (jax.ShapeDtypeStruct(h...]
    pallas_call x1, Pallas kernels: 200 us -> 210 us  [back_part(): pl.pallas_call(back_kernel, out_shape=(jax.ShapeDtypeStruct((rows, width)...]
    unnamed x8 -> x0, local copies, waits for them, and re-layouts: 3.49 us -> none
where the time goes in v5:
time: 259 us
  Pallas kernels  258 us (100%)
    pallas_call x1, Pallas kernels, back_part(): pl.pallas_call(back_kernel, out_shape=(jax.ShapeDtypeStruct((rows, width)...  210 us
    pallas_call x1, Pallas kernels, front_part(): pl.pallas_call(front_kernel, out_shape=made[:6] + (jax.ShapeDtypeStruct(h...  33.4 us
    pallas_call x1, Pallas kernels, unpack(): pl.pallas_call(unpack_kernel, grid=(8,), out_shape=(jax.ShapeDtypeStruct(...  14.8 us

profile of v5, /device:TPU:0, one launch (start us, length us, event | category | flops | bytes accessed | tf_op | source)
XLA Modules:
  0.0 259.3 jit_solution(9747117567937068331)
XLA Ops:
  0.6 33.4 %shard_map.239 = (bf16[512,1024]{1,0:T(8,128)(2,1)}, bf16[512,256]{1,0:T(8,128)(2,1)}, bf16[512,128]{1,0:T(8,128)(2,1)}, bf16[512,128]{1,0:T(8,128)(2,1)}, f32[8...) custom-call(bf16[512,1024]{1,0:T(8,128)(2,1)} %refs_17_.1, ...), custom_call_target="tpu_custom_call" | custom-call | tf_op jit(solution)/shard_map/pallas_call | solution.py:400
  34.0 210.3 %shard_map.240 = (bf16[512,1024]{1,0:T(8,128)(2,1)}, f32[512,1024]{1,0:T(8,128)}, f32[8,1024]{1,0:T(8,128)}, f32[4,4,4,4,96,128]{5,4,3,2,1,0:T(8,128)}, f32[4,4,4,96,128]{4,3,2,1,0:T(8,128)}) custom-call(bf16[512,1024]{1,0:T(8,128)(2,1)} %get-tuple-element.36.refs_0_, bf16[512,1024]{1,0:T(8,128)(2,1)} %refs_1_.1, f32[512,128]{1,0:T(8,128)} %get-tuple-element.37.refs_2_, ...), custom_call_target="tpu_custom_call" | custom-call | tf_op jit(solution)/shard_map/pallas_call | solution.py:786
  244.4 14.8 %shard_map.241 = (f32[8,1024,128]{2,1,0:T(8,128)}, f32[8,1024,128]{2,1,0:T(8,128)}, f32[8,128,1024]{2,1,0:T(8,128)}, f32[1024,256]{1,0:T(8,128)}, f32[1024,128]{...) custom-call(f32[8,2,16,96,128]{4,3,2,1,0:T(8,128)} %bitcast.8, ...), custom_call_target="tpu_custom_call" | custom-call | tf_op jit(solution)/shard_map/pallas_call | solution.py:840

commit v6 on v5

--- a/solution.py
+++ b/solution.py
@@ -17,6 +17,53 @@
 NORM_EPS = 1e-06
 ROPE_THETA = 10000.0
 PIECES = 4
+ORDER = (
+    ((0, 0),),
+    (),
+    (),
+    ((0, 1),),
+    (),
+    ((0, 2),),
+    (),
+    (),
+    ((0, 3), (1, 0),),
+    ((1, 1), (2, 0),),
+    (),
+    ((1, 2), (1, 3), (3, 0),),
+    ((2, 2),),
+    ((2, 1), (2, 3), (4, 0),),
+    (),
+    (),
+    (),
+    (),
+    (),
+    ((3, 2), (3, 1),),
+    ((4, 2), (3, 3),),
+    ((5, 0), (4, 1), (5, 2), (4, 3),),
+    ((0, 4), (6, 2), (5, 3), (5, 1),),
+    ((6, 0), (1, 4),),
+    ((7, 2), (6, 1),),
+    ((6, 3), (7, 0), (2, 4), (7, 1), (8, 0), (8, 2),),
+    ((7, 3), (3, 4), (9, 0), (8, 1), (8, 3), (9, 2),),
+    ((10, 0),),
+    ((4, 4), (10, 2), (9, 3), (9, 1),),
+    (),
+    ((5, 4), (11, 2), (10, 1),),
+    ((6, 4),),
+    (),
+    ((11, 0),),
+    (),
+    (),
+    ((10, 3), (7, 4), (11, 1), (8, 4), (12, 0),),
+    ((9, 4), (11, 3), (10, 4), (13, 0), (12, 2),),
+    (),
+    ((11, 4), (12, 3),),
+    (),
+    ((12, 4), (12, 1), (13, 3),),
+    (),
+    ((13, 2), (13, 4),),
+    ((13, 1),),
+)
 VMEM = pl.BlockSpec(memory_space=pltpu.VMEM)
 ANY = pl.BlockSpec(memory_space=pl.ANY)
 
@@ -483,8 +530,8 @@
         AxisRing(place, attn, attn_land, attn_land2, attn_zland, attn_sum, attn_sems)
     )
 
-    def go(k, *units):
-        for u in units:
+    def after(place_in_order):
+        for k, u in ORDER[place_in_order]:
             rings[u].op(k)
 
     sums = [
@@ -530,25 +577,25 @@
             for j in range(8):
                 piece = down_grad[128 * i : 128 * i + 128, 128 * j : 128 * j + 128]
                 mine[p, 2 * i + j // 4, j % 4, :, 64:96] = piece.reshape(4, 32, 128)
-        if p >= 2:
-            go(1, p - 2)
-        go(0, p)
+        after(2 * p)
         part = dot_nn(act_pair, down_pair)
         out_part[...] = part if p == 0 else out_part[...] + part
         if p < 2:
             for load in weight_loads(p + 2):
                 load.start()
+        after(2 * p + 1)
     late = [
         pltpu.make_async_copy(hidden1_hbm, hidden2, late_sem.at[0]),
     ]
     for load in late:
         load.start()
     back2.begin()
+    after(8)
     for load in loads[3:]:
         load.wait()
     seg_col = side[:, 8:9].astype(jnp.int32)
     loop(0, PIECES, back2.middle)
-    go(2, 0)
+    after(9)
 
     def finish2(k):
         d = back2.total(k)
@@ -559,16 +606,13 @@
         back2.three(k, dresidual.at[at], dresidual.at[at]).start()
 
     finish2(0)
-    go(2, 1)
+    after(10)
     finish2(1)
-    go(1, 2, 3)
-    go(3, 0)
+    after(11)
     finish2(2)
-    go(3, 1)
-    go(4, 0)
+    after(12)
     finish2(3)
-    go(2, 2)
-    go(4, 1)
+    after(13)
 
     def close2(k):
         at = back2.own(k)
@@ -576,7 +620,9 @@
         back2.one(k).wait_send()
 
     loop(0, PIECES, close2)
+    after(14)
     forward2.begin()
+    after(15)
 
     dbranch = dresidual[...].astype(BF16)
     dmixed = dot_nt(dbranch, w_out[...]).astype(BF16)
@@ -585,27 +631,12 @@
         piece = out_grad[:, 128 * j : 128 * j + 128].reshape(2, 4, 32, 128)
         attn[j // 2, 2 * (j % 2) : 2 * (j % 2) + 2, :, 64:96] = piece
 
-    go(5, 0)
+    after(16)
     loop(0, PIECES, forward2.middle)
-    go(2, 3)
-    go(5, 1)
+    after(17)
 
     def unrotate(grad):
         return (grad * cos_table[...] + swap_halves(grad) * sin_table[...]).astype(BF16)
-
-    def between(h):
-        if h == 0:
-            go(6, 0, 1)
-            go(3, 2)
-        elif h == 1:
-            go(3, 3)
-            go(7, 0)
-        elif h == 2:
-            go(7, 1)
-            go(4, 2, 3)
-        else:
-            go(8, 0, 1)
-            go(5, 2, 3)
 
     dkeys, dvalues = [], []
     for g in range(2):
@@ -634,7 +665,7 @@
                     dkey[t] = dkey[t] + dkey_part[256 * t : 256 * t + 256]
                 blocks.append(dot_tn(dscores, key[:until]))
                 if b == 1:
-                    between(h)
+                    after(18 + h)
             dquery.append(jnp.concatenate(blocks, 0) * HD ** (-0.5))
         dqkv[:, 128 * g : 128 * g + 128] = unrotate(jnp.concatenate(dquery, 1))
         dkeys.append(jnp.concatenate(dkey, 0) * HD ** (-0.5))
@@ -648,18 +679,15 @@
     for j in range(4):
         piece = hidden_grad[:, 128 * j : 128 * j + 128].reshape(4, 4, 4, 16, 128)
         attn[:, :, :, 16 * j : 16 * j + 16] = piece
-    go(9, 0, 1)
-    go(6, 2, 3)
-    go(0, 4)
-    go(10, 0, 1)
+    after(22)
     dhidden2[...] = (
         dot_nt(dqkv[:, :256], w_query[...])
         + dot_nt(dqkv[:, 256:384], w_key[...])
         + dot_nt(dqkv[:, 384:512], w_value[...])
     )
+    after(23)
     back1.begin()
-    go(7, 2, 3)
-    go(1, 4)
+    after(24)
 
     def finish_out(k):
         done = forward2.total(k) + residual[forward2.local(k)]
@@ -674,22 +702,16 @@
         output[forward2.other(k)] = land3[at].astype(BF16)
 
     loop(0, PIECES, finish_out)
-    go(11, 0)
+    after(25)
     loop(0, PIECES, back1.middle)
-    go(8, 2, 3)
-    go(11, 1)
-    go(2, 4)
-    go(9, 2, 3)
+    after(26)
     loop(0, PIECES, close_out)
+    after(27)
     stores = [
         pltpu.make_async_copy(output, output_hbm, late_sem.at[1]),
         pltpu.make_async_copy(dresidual, input_grad_hbm, late_sem.at[2]),
     ]
     stores[0].start()
-    go(12, 0, 1)
-    go(10, 2)
-    go(3, 4)
-    go(10, 3)
 
     def finish1(k):
         d = back1.total(k)
@@ -700,13 +722,13 @@
         back1.three(k, dresidual.at[at], dresidual.at[at]).start()
 
     finish1(0)
+    after(28)
     finish1(1)
-    go(13, 0, 1)
-    go(4, 4)
+    after(29)
     finish1(2)
-    go(11, 2)
-    go(5, 4)
+    after(30)
     finish1(3)
+    after(31)
     gains[0] = jnp.concatenate(
         [
             jnp.sum(folded[0:8], 0, keepdims=True),
@@ -728,38 +750,38 @@
         gains[i + 1] = gains[i] + gains_in[i]
 
     swap(0).start()
-    go(11, 3)
-    go(6, 4)
+    after(32)
     add_swap(0)
+    after(33)
     swap(1).start()
+    after(34)
 
     def close1(k):
         at = back1.own(k)
         back1.three(k, dresidual.at[at], dresidual.at[at]).wait()
 
     loop(0, PIECES, close1)
+    after(35)
     stores[1].start()
-    go(12, 2)
     add_swap(1)
+    after(36)
     swap(2).start()
-    go(7, 4)
-    go(12, 3)
+    after(37)
     add_swap(2)
+    after(38)
     swap(3).start()
-    go(8, 4)
-    go(13, 2)
+    after(39)
     add_swap(3)
+    after(40)
     swap(4).start()
-    go(9, 4)
-    go(13, 3)
+    after(41)
     add_swap(4)
+    after(42)
     swap(5).start()
-    go(10, 4)
+    after(43)
     add_swap(5)
     gain_sums[...] = gains[6]
-    go(11, 4)
-    go(12, 4)
-    go(13, 4)
+    after(44)
     for ring in rings:
         for s in range(3):
             ring.drain(s)

time: 259 us -> 235 us (0.907)
  Pallas kernels: 258 us -> 233 us
    pallas_call x1, Pallas kernels: 210 us -> 185 us  [back_part(): pl.pallas_call(back_kernel, out_shape=(jax.ShapeDtypeStruct((rows, width)...]
where the time goes in v6:
time: 235 us; the launch traced here: 234 us
  Pallas kernels  233 us (99%)
    pallas_call x1, Pallas kernels, back_part(): pl.pallas_call(back_kernel, out_shape=(jax.ShapeDtypeStruct((rows, width)...  185 us
    pallas_call x1, Pallas kernels, front_part(): pl.pallas_call(front_kernel, out_shape=made[:6] + (jax.ShapeDtypeStruct(h...  33.4 us
    pallas_call x1, Pallas kernels, unpack(): pl.pallas_call(unpack_kernel, grid=(8,), out_shape=(jax.ShapeDtypeStruct(...  14.8 us

profile of v6, /device:TPU:0, one launch (start us, length us, event | category | flops | bytes accessed | tf_op | source)
XLA Modules:
  0.0 234.3 jit_solution(13044402753480206785)
XLA Ops:
  0.6 33.4 %shard_map.239 = (bf16[512,1024]{1,0:T(8,128)(2,1)}, bf16[512,256]{1,0:T(8,128)(2,1)}, bf16[512,128]{1,0:T(8,128)(2,1)}, bf16[512,128]{1,0:T(8,128)(2,1)}, f32[8...) custom-call(bf16[512,1024]{1,0:T(8,128)(2,1)} %refs_17_.1, ...), custom_call_target="tpu_custom_call" | custom-call | tf_op jit(solution)/shard_map/pallas_call | solution.py:447
  34.0 185.3 %shard_map.240 = (bf16[512,1024]{1,0:T(8,128)(2,1)}, f32[512,1024]{1,0:T(8,128)}, f32[8,1024]{1,0:T(8,128)}, f32[4,4,4,4,96,128]{5,4,3,2,1,0:T(8,128)}, f32[4,4,4,96,128]{4,3,2,1,0:T(8,128)}) custom-call(bf16[512,1024]{1,0:T(8,128)(2,1)} %get-tuple-element.36.refs_0_, bf16[512,1024]{1,0:T(8,128)(2,1)} %refs_1_.1, f32[512,128]{1,0:T(8,128)} %get-tuple-element.37.refs_2_, ...), custom_call_target="tpu_custom_call" | custom-call | tf_op jit(solution)/shard_map/pallas_call | solution.py:808
  219.3 14.8 %shard_map.241 = (f32[8,1024,128]{2,1,0:T(8,128)}, f32[8,1024,128]{2,1,0:T(8,128)}, f32[8,128,1024]{2,1,0:T(8,128)}, f32[1024,256]{1,0:T(8,128)}, f32[1024,128]{...) custom-call(f32[8,2,16,96,128]{4,3,2,1,0:T(8,128)} %bitcast.8, ...), custom_call_target="tpu_custom_call" | custom-call | tf_op jit(solution)/shard_map/pallas_call | solution.py:862

commit v7 on v6

--- a/solution.py
+++ b/solution.py
@@ -109,7 +109,8 @@
 class AxisRing:
     def __init__(self, place, mine, land, land2, zland, out, sems):
         self.place, self.mine, self.land, self.land2 = place, mine, land, land2
-        self.zland, self.out, self.sems = zland, out, sems
+        self.zland, self.out = zland, out
+        self.sent, self.got1, self.got2, self.got3, self.got4, self.gotz, self.keep_s = sems
 
     def spots(self, f, back1, back2):
         step = 1 - 2 * (f % 2)
@@ -118,118 +119,58 @@
             pos1, pos2 = pos2, pos1
         return (pos1 - step * back1 + 8) % 4, (pos2 - step * back2 + 8) % 4
 
-    def send(self, f, s, stage, src, dst):
-        axis = f // 2 if stage in (0, 3) else 1 - f // 2
+    def send(self, f, n):
+        axis = f // 2
+        if n < 3:
+            i = self.spots(f, 1 + n, 0)[0]
+            src = (self.mine if n == 0 else self.land).at[f, i]
+            dst, got = self.land.at[f, i], self.got1.at[f, n]
+        elif n < 6:
+            i, j = self.spots(f, 0, n - 2)
+            src = self.land.at[f, i, j] if n == 3 else self.land2.at[f, j]
+            dst, got, axis = self.land2.at[f, j], self.got2.at[f, n - 3], 1 - axis
+        elif n == 6:
+            j = self.spots(f, 0, 0)[1]
+            src, dst, got = self.land2.at[f, j], self.zland.at[f], self.gotz.at[f]
+        elif n < 10:
+            i, j = self.spots(f, 0, n - 7)
+            src = (self.mine if n == 7 else self.out).at[f, i, j]
+            dst, got, axis = self.out.at[f, i, j], self.got4.at[f, n - 7], 1 - axis
+        else:
+            i = self.spots(f, n - 10, 0)[0]
+            src, dst, got = self.out.at[f, i], self.out.at[f, i], self.got3.at[f, n - 10]
+        to = self.place.z_far if n == 6 else self.place.across[2 * axis + f % 2]
         return pltpu.make_async_remote_copy(
-            src, dst, self.sems[2 * stage].at[f, s], self.sems[2 * stage + 1].at[f, s],
-            device_id=(self.place.across[2 * axis + f % 2], self.place.tensor),
-            device_id_type=MESH,
-        )
-
-    def rs1(self, f, s, src):
-        i = self.spots(f, 1 + s, 0)[0]
-        return self.send(f, s, 0, src.at[f, i], self.land.at[f, i])
-
-    def rs2(self, f, s, src):
-        j = self.spots(f, 0, 1 + s)[1]
-        return self.send(f, s, 1, src.at[j], self.land2.at[f, j])
-
-    def ag2(self, f, s, src):
-        i, j = self.spots(f, 0, s)
-        return self.send(f, s, 2, src.at[f, i, j], self.out.at[f, i, j])
-
-    def ag1(self, f, s, src):
-        return self.send(f, s, 3, src, self.out.at[f, self.spots(f, s, 0)[0]])
-
-    def zcopy(self, f):
-        return pltpu.make_async_remote_copy(
-            self.land2.at[f, self.spots(f, 0, 0)[1]], self.zland.at[f],
-            self.sems[8].at[f], self.sems[9].at[f],
-            device_id=(self.place.z_far, self.place.tensor), device_id_type=MESH,
+            src, dst, self.sent.at[f], got,
+            device_id=(to, self.place.tensor), device_id_type=MESH,
         )
 
     def keep(self, f):
         i, j = self.spots(f, 0, 0)
         return pltpu.make_async_copy(
-            self.mine.at[f, i, j], self.out.at[f, i, j], self.sems[10].at[f]
+            self.mine.at[f, i, j], self.out.at[f, i, j], self.keep_s.at[f]
         )
 
-    def begin(self):
+    def op(self, k):
         for f in range(4):
-            self.rs1(f, 0, self.mine).start()
-
-    def rs1_step(self, s):
-        for f in range(4):
-            self.rs1(f, s - 1, self.land).wait_recv()
-            if s == 1:
-                self.rs1(f, 0, self.mine).wait_send()
-            i = self.spots(f, 1 + s, 0)[0]
-            self.land[f, i] = self.land[f, i] + self.mine[f, i]
-            if s < 3:
-                self.rs1(f, s, self.land).start()
-            else:
-                self.rs2(f, 0, self.land.at[f, i]).start()
-
-    def rs2_step(self, s):
-        for f in range(4):
-            i, j = self.spots(f, 0, 1 + s)
-            self.rs2(f, s - 1, self.land2.at[f]).wait_recv()
-            self.land2[f, j] = self.land2[f, j] + self.land[f, i, j]
-            if s < 3:
-                self.rs2(f, s, self.land2.at[f]).start()
-            else:
-                self.zcopy(f).start()
-
-    def back(self):
-        for f in range(4):
-            self.zcopy(f).wait_recv()
-            i, j = self.spots(f, 0, 0)
-            self.mine[f, i, j] = self.land2[f, j] + self.zland[f]
-            self.ag2(f, 0, self.mine).start()
-            self.keep(f).start()
-
-    def ag2_step(self, s):
-        for f in range(4):
-            self.ag2(f, s - 1, self.out).wait_recv()
-            i = self.spots(f, 0, s)[0]
-            if s < 3:
-                self.ag2(f, s, self.out).start()
-            else:
+            if k > 0:
+                self.send(f, k - 1).wait_recv()
+            if 1 <= k <= 3:
+                i = self.spots(f, 1 + k, 0)[0]
+                self.land[f, i] = self.land[f, i] + self.mine[f, i]
+            elif 4 <= k <= 6:
+                i, j = self.spots(f, 0, k - 2)
+                self.land2[f, j] = self.land2[f, j] + self.land[f, i, j]
+            elif k == 7:
+                i, j = self.spots(f, 0, 0)
+                self.mine[f, i, j] = self.land2[f, j] + self.zland[f]
+                self.keep(f).start()
+            elif k == 10:
                 self.keep(f).wait()
-                self.ag1(f, 0, self.out.at[f, i]).start()
-
-    def ag1_step(self, s):
-        for f in range(4):
-            held = self.out.at[f, self.spots(f, s, 0)[0]]
-            self.ag1(f, s - 1, held).wait_recv()
-            if s < 3:
-                self.ag1(f, s, held).start()
-
-    def op(self, k):
-        if k == 0:
-            self.begin()
-        elif k <= 3:
-            self.rs1_step(k)
-        elif k <= 6:
-            self.rs2_step(k - 3)
-        elif k == 7:
-            self.back()
-        elif k <= 10:
-            self.ag2_step(k - 7)
-        else:
-            self.ag1_step(k - 10)
-
-    def drain(self, s):
-        for f in range(4):
-            if s > 0:
-                self.rs1(f, s, self.land).wait_send()
-            self.rs2(f, s, self.land2.at[f]).wait_send()
-            self.ag2(f, s, self.mine if s == 0 else self.out).wait_send()
-            self.ag1(f, s, self.out.at[f, 0]).wait_send()
-
-    def close(self):
-        for f in range(4):
-            self.zcopy(f).wait_send()
+            if k > 0:
+                self.send(f, k - 1).wait_send()
+            if k < 13:
+                self.send(f, k).start()
 
 
 class Sum4:
@@ -489,8 +430,8 @@
         dhidden2, out_part, hidden2_t, land1, land2, land3, folded, gains, gains_in,
     ) = refs[3:22]
     sems = refs[22:]
-    ring_sems, sems = sems[:11], sems[11:]
-    attn_sems, sems = sems[:11], sems[11:]
+    ring_sems, sems = sems[:7], sems[7:]
+    attn_sems, sems = sems[:7], sems[7:]
     sum_sems, sems = sems[:6], sems[6:]
     load_sem, weight_sem, late_sem, gain_s, gain_r = sems
     dqkv = hidden2_t.at[0:512]
@@ -782,10 +723,6 @@
     add_swap(5)
     gain_sums[...] = gains[6]
     after(44)
-    for ring in rings:
-        for s in range(3):
-            ring.drain(s)
-        ring.close()
     for i in range(6):
         swap(i).wait_send()
 
@@ -803,8 +740,8 @@
     half = (rows // 2, width)
     grads, attn = (4, 4, 4, 4, 96, 128), (4, 4, 4, 96, 128)
     S = pltpu.VMEM
-    ring_sems = [DMA((4, 4, 3))] * 8 + [DMA((4, 4))] * 3
-    attn_sems = [DMA((4, 3))] * 8 + [DMA((4,))] * 3
+    ring_sems = [DMA((4, 4))] + [DMA((4, 4, 3))] * 4 + [DMA((4, 4))] * 2
+    attn_sems = [DMA((4,))] + [DMA((4, 3))] * 4 + [DMA((4,))] * 2
     return pl.pallas_call(
         back_kernel,
         out_shape=(

time: 235 us -> 232 us (0.987)
    pallas_call x1, Pallas kernels: 185 us -> 183 us  [back_part(): pl.pallas_call(back_kernel, out_shape=(jax.ShapeDtypeStruct((rows, width)...]
where the time goes in v7:
time: 232 us
  Pallas kernels  231 us (100%)
    pallas_call x1, Pallas kernels, back_part(): pl.pallas_call(back_kernel, out_shape=(jax.ShapeDtypeStruct((rows, width)...  183 us
    pallas_call x1, Pallas kernels, front_part(): pl.pallas_call(front_kernel, out_shape=made[:6] + (jax.ShapeDtypeStruct(h...  33.4 us
    pallas_call x1, Pallas kernels, unpack(): pl.pallas_call(unpack_kernel, grid=(8,), out_shape=(jax.ShapeDtypeStruct(...  14.8 us

profile of v7, /device:TPU:0, one launch (start us, length us, event | category | flops | bytes accessed | tf_op | source)
XLA Modules:
  0.0 231.8 jit_solution(6569946434203682056)
XLA Ops:
  0.6 33.4 %shard_map.239 = (bf16[512,1024]{1,0:T(8,128)(2,1)}, bf16[512,256]{1,0:T(8,128)(2,1)}, bf16[512,128]{1,0:T(8,128)(2,1)}, bf16[512,128]{1,0:T(8,128)(2,1)}, f32[8...) custom-call(bf16[512,1024]{1,0:T(8,128)(2,1)} %refs_17_.1, ...), custom_call_target="tpu_custom_call" | custom-call | tf_op jit(solution)/shard_map/pallas_call | solution.py:388
  34.0 182.8 %shard_map.240 = (bf16[512,1024]{1,0:T(8,128)(2,1)}, f32[512,1024]{1,0:T(8,128)}, f32[8,1024]{1,0:T(8,128)}, f32[4,4,4,4,96,128]{5,4,3,2,1,0:T(8,128)}, f32[4,4,4,96,128]{4,3,2,1,0:T(8,128)}) custom-call(bf16[512,1024]{1,0:T(8,128)(2,1)} %get-tuple-element.36.refs_0_, bf16[512,1024]{1,0:T(8,128)(2,1)} %refs_1_.1, f32[512,128]{1,0:T(8,128)} %get-tuple-element.37.refs_2_, ...), custom_call_target="tpu_custom_call" | custom-call | tf_op jit(solution)/shard_map/pallas_call | solution.py:745
  216.8 14.8 %shard_map.241 = (f32[8,1024,128]{2,1,0:T(8,128)}, f32[8,1024,128]{2,1,0:T(8,128)}, f32[8,128,1024]{2,1,0:T(8,128)}, f32[1024,256]{1,0:T(8,128)}, f32[1024,128]{...) custom-call(f32[8,2,16,96,128]{4,3,2,1,0:T(8,128)} %bitcast.8, ...), custom_call_target="tpu_custom_call" | custom-call | tf_op jit(solution)/shard_map/pallas_call | solution.py:799
